TPU v7x, 32 devices: a whole 2x2x4 slice. The times are simulated.
32 devices in a mesh: side: 2 (over core), dev: 16 (over z, y, x).
Axes of the slice: x: 2, y: 2, z: 4, core: 2. Of those that a mesh axis runs over, the one named last changes fastest.
Arguments:
- queries: bfloat16 [256, 64, 576], P('dev'), may hold values from -18 to 18
- latent_cache: bfloat16 [256, 768, 576], P('dev', 'side'), may hold values from -18 to 18
- lengths: int32 [256], P('dev'), may hold values from 64 to 768, as said below
- value_lift: bfloat16 [64, 512, 128], P('side'), may hold values from -0.25 to 0.25
- output_map: bfloat16 [8192, 7168], P('side', 'dev'), may hold values from -0.5 to 0.5
- residual: bfloat16 [256, 7168], P(('side', 'dev')), may hold values from -6 to 6
- norm_gain: bfloat16 [7168], replicated, may hold values from 0.099609375 to 1.8984375
- expert_ids: int32 [256, 8], P(('side', 'dev')), may hold values from 0 to 7, all different within a row; in each aligned block of 8 rows (0 to 7, 8 to 15, ...) at most 8 rows name the same one
- gate_values: float32 [256, 8], P(('side', 'dev')), may hold values from 0.1 to 0.8
- expert_in: bfloat16 [16, 7168, 2, 512], P('dev', None, None, 'side'), may hold values from -0.0625 to 0.0625
- expert_down: bfloat16 [16, 512, 7168], P('dev', 'side'), may hold values from -0.1875 to 0.1875
Outputs:
- layer_out: bfloat16 [256, 7168], P(('side', 'dev'))
Inputs may be any that keep to these rules, and one draw needn't show every extreme that they name: `lengths`: request 0 has all 768 slots live. `expert_ids`: within the rows of one device (aligned blocks of 8 rows) no expert is chosen by more than 8 rows, and some expert is chosen by exactly 8 rows in some blocks.
All inputs are finite; a program needn't handle non-finite values.
Results may differ from a plain program's by a relative error of at most 0.02.
Values may be sent and summed in bfloat16 or wider, within the bound.
No kernel may reach another device: no remote copies, remote signals or barrier semaphores. Data moves between devices by JAX's collectives and lax.ppermute only.
A program may use at most 128 MiB of HBM per device.

v0:
```python
import jax
import jax.numpy as jnp
from jax import lax
from jax.sharding import PartitionSpec as P

QKD = 192


def on_device(
    queries,
    latent_cache,
    lengths,
    value_lift,
    output_map,
    residual,
    norm_gain,
    expert_ids,
    gate_values,
    expert_in,
    expert_down,
):
    request_count = queries.shape[0]
    latent_width = value_lift.shape[1]
    half_heads = value_lift.shape[0]
    value_width = value_lift.shape[2]
    half_slots = latent_cache.shape[1]
    model_width = residual.shape[1]
    side_index = lax.axis_index("side")
    score_scale = QKD ** (-0.5)
    scores = (
        jnp.einsum("rhc,rpc->rhp", queries, latent_cache, preferred_element_type=jnp.float32)
        * score_scale
    )
    positions = side_index * half_slots + jnp.arange(half_slots, dtype=jnp.int32)
    usable = (positions[None, :] < lengths[:, None])[:, None, :]
    masked = jnp.where(usable, scores, -1e30)
    row_top = lax.pmax(jnp.max(masked, axis=2), "side")
    raised = jnp.where(usable, jnp.exp(masked - row_top[:, :, None]), 0.0)
    local_total = jnp.sum(raised, axis=2)
    probabilities = raised.astype(jnp.bfloat16)
    local_latent = jnp.einsum(
        "rhp,rpc->rhc",
        probabilities,
        latent_cache[:, :, :latent_width],
        preferred_element_type=jnp.float32,
    )
    row_total, latent_sum = lax.psum((local_total, local_latent), "side")
    latent_out = (latent_sum / row_total[:, :, None]).astype(jnp.bfloat16)
    own_heads = lax.dynamic_slice_in_dim(latent_out, side_index * half_heads, half_heads, 1)
    head_values = jnp.einsum(
        "rhc,hcv->rhv", own_heads, value_lift, preferred_element_type=jnp.float32
    )
    head_values = head_values.astype(jnp.bfloat16).reshape(request_count, half_heads * value_width)
    partial_columns = jnp.dot(
        lax.all_gather(head_values, "dev", axis=0, tiled=True),
        output_map,
        preferred_element_type=jnp.float32,
    )
    summed_columns = lax.psum_scatter(
        partial_columns.astype(jnp.bfloat16), "side", scatter_dimension=0, tiled=True
    ).astype(jnp.float32)
    attention = lax.all_to_all(summed_columns, "dev", split_axis=0, concat_axis=1, tiled=True)
    hidden = (residual.astype(jnp.float32) + attention).astype(jnp.bfloat16)
    hidden_wide = hidden.astype(jnp.float32)
    normed = hidden_wide * lax.rsqrt(
        jnp.mean(hidden_wide * hidden_wide, axis=1, keepdims=True) + 1e-06
    )
    normed = (normed * norm_gain.astype(jnp.float32)[None, :]).astype(jnp.bfloat16)
    token_count = expert_ids.shape[0]
    route_count = expert_ids.shape[1]
    experts = lax.axis_size("dev") // 2
    capacity = max(4, token_count * route_count // experts)
    flat_ids = expert_ids.reshape(-1)
    expert_hits = (flat_ids[:, None] == jnp.arange(experts, dtype=jnp.int32)[None, :]).astype(
        jnp.int32
    )
    before = jnp.cumsum(expert_hits, axis=0) - expert_hits
    slot_index = jnp.sum(before * expert_hits, axis=1).reshape(token_count, route_count)
    slot_code = expert_ids * capacity + slot_index
    slot_table = jnp.arange(experts * capacity, dtype=jnp.int32)
    slot_match = slot_code[None, :, :] == slot_table[:, None, None]
    dispatch_matrix = jnp.any(slot_match, axis=2).astype(jnp.bfloat16)
    combine_matrix = jnp.sum(jnp.where(slot_match, gate_values[None, :, :], 0.0), axis=2).T
    outgoing = jnp.dot(dispatch_matrix, normed, preferred_element_type=jnp.float32).astype(
        jnp.bfloat16
    )
    outgoing = outgoing.reshape(experts, capacity, model_width)
    quarter_width = expert_in.shape[3]
    gate_up_local = expert_in.reshape(model_width, 2 * quarter_width)
    down_local = expert_down[0]
    spread = jnp.tile(jnp.repeat(outgoing, 2, axis=0), (2, 1, 1))
    arrivals = lax.all_to_all(spread, ("side", "dev"), split_axis=0, concat_axis=0, tiled=True)
    flat_rows = arrivals.reshape(-1, model_width)
    gate_up = jnp.dot(flat_rows, gate_up_local, preferred_element_type=jnp.float32)
    activated = (jax.nn.silu(gate_up[:, :quarter_width]) * gate_up[:, quarter_width:]).astype(
        jnp.bfloat16
    )
    activated = activated.reshape(arrivals.shape[0], arrivals.shape[1], quarter_width).reshape(
        -1, quarter_width
    )
    partial_out = jnp.dot(activated, down_local, preferred_element_type=jnp.float32)
    partial_value = partial_out.reshape(arrivals.shape[0], arrivals.shape[1], model_width)
    returned = lax.all_to_all(
        partial_value.astype(jnp.bfloat16), ("side", "dev"), split_axis=0, concat_axis=0, tiled=True
    ).astype(partial_value.dtype)
    expert_out = jnp.sum(
        returned.reshape(2, experts, 2, capacity, model_width), axis=(0, 2)
    ).astype(jnp.bfloat16)
    routed_sum = jnp.dot(
        combine_matrix,
        expert_out.reshape(experts * capacity, model_width).astype(jnp.float32),
        precision=lax.Precision.HIGHEST,
    )
    return (hidden.astype(jnp.float32) + routed_sum).astype(jnp.bfloat16)


def solution(mesh):
    in_specs = (
        P("dev", None, None),
        P("dev", "side", None),
        P("dev"),
        P("side", None, None),
        P("side", "dev"),
        P(("side", "dev"), None),
        P(),
        P(("side", "dev"), None),
        P(("side", "dev"), None),
        P("dev", None, None, "side"),
        P("dev", "side", None),
    )
    out_specs = P(("side", "dev"), None)
    return jax.shard_map(
        on_device, mesh=mesh, in_specs=in_specs, out_specs=out_specs, check_vma=False
    )
```

profile of v0, /device:TPU:0, one launch (start us, length us, event | category | flops | bytes accessed | tf_op | source)
XLA Modules:
  0.0 341.5 jit_solution(6723206857619323622)
XLA Ops:
  7.9 4.5 %fusion.30 = (f32[16,64]{1,0:T(8,128)S(1)}, f32[16,64,384]{2,1,0:T(8,128)S(1)}) fusion(bf16[16,64,576]{2,1,0:T(8,128)(2,1)S(1)} %copy-done, bf16[16,384,576]{1,2,0:T(8,128)(2,1)} %param.12, pred[16,384]{1,0:T(8,128)(4,1)S(1)} %broadcast_compare_fusion), kind=kOutput, calls=%fused_computation.50 | convolution fusion | flops 454163456 | bytes 9840640 | tf_op jit(solution)/shard_map/rhc,rpc->rhp/dot_general | solution.py:31
  12.4 2.6 pmax.7
  15.0 6.2 %fusion.2 = f32[16,64,512]{2,1,0:T(8,128)} fusion(bf16[16,384,576]{1,2,0:T(8,128)(2,1)} %param.12, f32[16,64,384]{2,1,0:T(8,128)S(1)} %get-tuple-element.8, f32[16,64]{1,0:T(8,128)S(1)} %pmax.7, pred[16,384]{1,0:T(8,128)(4,1)S(1)} %broadcast_compare_fusion), kind=kOutput, calls=%fused_computation.5 | convolution fusion | flops 403832832 | bytes 9971712 | tf_op jit(solution)/shard_map/rhp,rpc->rhc/dot_general | solution.py:41
  21.8 2.5 psum.15
  24.4 20.8 %all-reduce.2.cloned.1.call-done = f32[16,64,512]{2,1,0:T(8,128)} async-done(((f32[16,64,512]{2,1,0:T(8,128)}), f32[16,64,512]{2,1,0:T(8,128)}) %all-reduce.2.cloned.1.call-update) | async-done | bytes 2097168 | tf_op jit(solution)/shard_map/psum | solution.py:47
  45.2 1.4 fusion.10
  46.6 3.1 fusion.9
  50.4 61.9 %all-gather.2.cloned.1.call-done = bf16[256,4096]{1,0:T(8,128)(2,1)} async-done(((bf16[16,4096]{1,0:T(8,128)(2,1)}), bf16[256,4096]{1,0:T(8,128)(2,1)}) %all-gather.2.cloned.1.call-update) | async-done | bytes 2097168 | tf_op jit(solution)/shard_map/all_gather | solution.py:55
  112.4 3.8 %convolution_convert_fusion.2 = bf16[256,448]{0,1:T(8,128)(2,1)S(1)} fusion(bf16[256,4096]{1,0:T(8,128)(2,1)} %all-gather.2.cloned.1.call-done, bf16[4096,448]{0,1:T(8,128)(2,1)} %param.15), kind=kOutput, calls=%fused_computation.14 | convolution fusion | flops 939638784 | bytes 5996544 | tf_op jit(solution)/shard_map/dot_general | solution.py:54
  116.2 0.8 copy.26
  117.3 6.2 %reduce-scatter.4.cloned.1.call-done = bf16[128,448]{1,0:T(8,128)(2,1)} async-done(((bf16[256,448]{1,0:T(8,128)(2,1)}), bf16[128,448]{1,0:T(8,128)(2,1)}) %reduce-scatter.4.cloned.1.call-update) | async-done | bytes 114704 | tf_op jit(solution)/shard_map/reduce_scatter | solution.py:59
  123.5 1.6 bitcast_convert_fusion
  125.1 6.8 %all-to-all-start = ((f32[16,8,448]{2,1,0:T(8,128)}), f32[16,8,448]{2,1,0:T(8,128)S(1)}, u32[]{:S(2)}, u32[]{:S(2)}) async-start(f32[16,8,448]{2,1,0:T(8,128)} %bitcast_convert_fusion), calls=%async_computation | async-start | bytes 524288 | tf_op jit(solution)/shard_map/all_to_all | solution.py:62
  132.3 10.0 %all-to-all-done = f32[16,8,448]{2,1,0:T(8,128)S(1)} async-done(((f32[16,8,448]{2,1,0:T(8,128)}), f32[16,8,448]{2,1,0:T(8,128)S(1)}, u32[]{:S(2)}, u32[]{:S(2)}) %all-to-all-start) | async-done | bytes 229408 | tf_op jit(solution)/shard_map/all_to_all | solution.py:62
  143.4 2.3 tile.11
  145.7 3.6 %all-to-all-start.1 = ((bf16[32,8,7168]{2,1,0:T(8,128)(2,1)}), bf16[32,8,7168]{2,1,0:T(8,128)(2,1)}, u32[]{:S(2)}, u32[]{:S(2)}) async-start(bf16[32,8,7168]{2,1,0:T(8,128)(2,1)} %bitcast.40), calls=%async_computation.1 | async-start | bytes 7340032 | tf_op jit(solution)/shard_map/all_to_all | solution.py:92
  149.3 7.3 %copy.30 = bf16[896,8,2,256]{3,1,2,0:T(8,128)(2,1)} copy(bf16[896,8,2,256]{3,2,1,0:T(2,128)(2,1)} %bitcast.41) | data formatting | bytes 14680064
  156.6 77.0 %all-to-all-done.1 = bf16[32,8,7168]{2,1,0:T(8,128)(2,1)} async-done(((bf16[32,8,7168]{2,1,0:T(8,128)(2,1)}), bf16[32,8,7168]{2,1,0:T(8,128)(2,1)}, u32[]{:S(2)}, u32[]{:S(2)}) %all-to-all-start.1) | async-done | bytes 3670048 | tf_op jit(solution)/shard_map/all_to_all | solution.py:92
  233.7 6.4 %fusion.5 = f32[256,512]{1,0:T(8,128)S(1)} fusion(bf16[7168,512]{1,0:T(8,128)(2,1)} %bitcast.42, bf16[32,8,7168]{2,1,0:T(8,128)(2,1)} %all-to-all-done.1), kind=kOutput, calls=%fused_computation.8 | convolution fusion | flops 1879048192 | bytes 11534336 | tf_op jit(solution)/shard_map/dot_general | solution.py:94
  240.1 3.0 convolution_convert_fusion
  243.0 3.7 %all-to-all-start.2 = ((bf16[32,8,7168]{2,1,0:T(8,128)(2,1)}), bf16[32,8,7168]{2,1,0:T(8,128)(2,1)}, u32[]{:S(2)}, u32[]{:S(2)}) async-start(bf16[32,8,7168]{2,1,0:T(8,128)(2,1)} %convolution_convert_fusion), calls=%async_computation.2 | async-start | bytes 7340032 | tf_op jit(solution)/shard_map/all_to_all | solution.py:103
  246.8 84.3 %all-to-all-done.2 = bf16[32,8,7168]{2,1,0:T(8,128)(2,1)} async-done(((bf16[32,8,7168]{2,1,0:T(8,128)(2,1)}), bf16[32,8,7168]{2,1,0:T(8,128)(2,1)}, u32[]{:S(2)}, u32[]{:S(2)}) %all-to-all-start.2) | async-done | bytes 3670048 | tf_op jit(solution)/shard_map/all_to_all | solution.py:103
  331.1 2.7 reduce
  333.8 1.1 fusion.1
  (38 shorter events, 4.6 us)
Async XLA Ops:
  6.5 1.3 copy-start
  6.5 38.6 %all-reduce.2.cloned.1.call-start = ((), (), s32[]{:S(2)}) async-start(), calls=%async_computation.4 | async-start | bytes 4194304 | tf_op jit(solution)/shard_map/psum | solution.py:47
  21.2 91.1 %all-gather.2.cloned.1.call-start = ((), (), s32[]{:S(2)}) async-start(), calls=%async_computation.5 | async-start | bytes 2228224 | tf_op jit(solution)/shard_map/all_gather | solution.py:55
  50.3 66.7 %copy-start.3 = (s32[8,8]{1,0:T(8,128)S(1)}, s32[8,8]{1,0:T(8,128)}, u32[]{:S(2)}) copy-start(s32[8,8]{1,0:T(8,128)} %param.18) | copy-start | bytes 772
  50.3 66.8 %copy-start.4 = (bf16[7168]{0:T(1024)(128)(2,1)S(1)}, bf16[7168]{0:T(1024)(128)(2,1)}, u32[]{:S(2)}) copy-start(bf16[7168]{0:T(1024)(128)(2,1)} %param.17) | copy-start | bytes 43012
  50.3 92.2 %copy-start.2 = (bf16[8,7168]{1,0:T(8,128)(2,1)S(1)}, bf16[8,7168]{1,0:T(8,128)(2,1)}, u32[]{:S(2)}) copy-start(bf16[8,7168]{1,0:T(8,128)(2,1)} %param.16) | copy-start | bytes 344068
  50.4 73.1 %reduce-scatter.4.cloned.1.call-start = ((), (), s32[]{:S(2)}) async-start(), calls=%async_computation.6 | async-start | bytes 393216 | tf_op jit(solution)/shard_map/reduce_scatter | solution.py:59
  125.1 17.1 %all-to-all-start = ((f32[16,8,448]{2,1,0:T(8,128)}), f32[16,8,448]{2,1,0:T(8,128)S(1)}, u32[]{:S(2)}, u32[]{:S(2)}) async-start(f32[16,8,448]{2,1,0:T(8,128)} %bitcast_convert_fusion), calls=%async_computation | async-start | bytes 524288 | tf_op jit(solution)/shard_map/all_to_all | solution.py:62
  145.7 87.9 %all-to-all-start.1 = ((bf16[32,8,7168]{2,1,0:T(8,128)(2,1)}), bf16[32,8,7168]{2,1,0:T(8,128)(2,1)}, u32[]{:S(2)}, u32[]{:S(2)}) async-start(bf16[32,8,7168]{2,1,0:T(8,128)(2,1)} %bitcast.40), calls=%async_computation.1 | async-start | bytes 7340032 | tf_op jit(solution)/shard_map/all_to_all | solution.py:92
  233.7 6.4 %copy-start.1 = (bf16[1,256,7168]{2,1,0:T(8,128)(2,1)S(1)}, bf16[1,256,7168]{2,1,0:T(8,128)(2,1)}, u32[]{:S(2)}) copy-start(bf16[1,256,7168]{2,1,0:T(8,128)(2,1)} %param.21) | copy-start | bytes 11010052
  243.0 3.7 %copy-start.5 = (f32[8,8]{1,0:T(8,128)S(1)}, f32[8,8]{1,0:T(8,128)}, u32[]{:S(2)}) copy-start(f32[8,8]{1,0:T(8,128)} %param.19) | copy-start | bytes 772
  243.0 88.1 %all-to-all-start.2 = ((bf16[32,8,7168]{2,1,0:T(8,128)(2,1)}), bf16[32,8,7168]{2,1,0:T(8,128)(2,1)}, u32[]{:S(2)}, u32[]{:S(2)}) async-start(bf16[32,8,7168]{2,1,0:T(8,128)(2,1)} %convolution_convert_fusion), calls=%async_computation.2 | async-start | bytes 7340032 | tf_op jit(solution)/shard_map/all_to_all | solution.py:103
Sparse Core Ops, SparseCore 0:
  21.3 23.7 all-reduce.1
  50.4 61.8 all-gather.1
  117.2 6.3 reduce-scatter.3
where the time goes:
time: 342 us; the launch traced here: 341 us
  waiting for transfers between devices  260 us (76%)
  matrix products  28.5 us (8%)
  starting transfers between devices  14.1 us (4%)
  between operations  13.3 us (4%)
  local copies, waits for them, and re-layouts  12.4 us (4%)
  other arithmetic  7.82 us (2%)
  blocking collectives  5.14 us (2%)
    all_to_all x1, waiting for transfers between devices, on_device(): lax.all_to_all(partial_value.astype(jnp.bfloat16), ('side', 'dev'), split...  84.3 us
    all_to_all x1, waiting for transfers between devices, on_device(): lax.all_to_all(spread, ('side', 'dev'), split_axis=0, concat_axis=0, tile...  77 us
    all_gather x1, waiting for transfers between devices, on_device(): lax.all_gather(head_values, 'dev', axis=0, tiled=True)  61.9 us
    psum x1, waiting for transfers between devices, on_device(): row_total, latent_sum = lax.psum((local_total, local_latent), 'side')  20.8 us
    all_to_all x1, waiting for transfers between devices, on_device(): lax.all_to_all(summed_columns, 'dev', split_axis=0, concat_axis=1, tiled=...  9.98 us
    unnamed x14, local copies, waits for them, and re-layouts  8.7 us
  transfers between devices with their start and end apart: 6, of which 6 were waited for; matrix products, arithmetic and copies ran while one was open for 3% of the time, Pallas kernels for 0%

commit v1 on v0

v1 whole, which is shorter than its diff:
```python
import functools

import jax
import jax.numpy as jnp
from jax import lax
from jax.experimental import pallas as pl
from jax.experimental.pallas import tpu as pltpu
from jax.sharding import PartitionSpec as P

QKD = 192
F32 = jnp.float32
BF16 = jnp.bfloat16


def hop(value, axis, size, mask):
    return lax.ppermute(value, axis, [(i, i ^ mask) for i in range(size)])


def plane_of(count):
    return 4 if count % 4 == 0 else count


def project_kernel(place_ref, *refs, groups, rows, steps):
    parts, (map_ref, own_ref, send_ref, total, ordered) = refs[:groups], refs[groups:]
    step = pl.program_id(0)
    left = jnp.concatenate([part[...] for part in parts], axis=0)
    term = jnp.dot(left, map_ref[...], preferred_element_type=F32)

    @pl.when(step == 0)
    def _():
        total[...] = term

    @pl.when(step > 0)
    def _():
        total[...] += term

    @pl.when(step == steps - 1)
    def _():
        count = total.shape[0] // rows
        half = total.shape[0] // 2
        for block in range(count):
            target = pl.multiple_of(place_ref[block] * rows, rows)
            ordered[pl.ds(target, rows), :] = total[block * rows : (block + 1) * rows, :]
        side = place_ref[count]
        own_ref[...] = ordered[pl.ds(pl.multiple_of(side * half, half), half), :]
        send_ref[...] = ordered[pl.ds(pl.multiple_of((1 - side) * half, half), half), :].astype(BF16)


def project(parts, output_map, place, rows):
    groups = len(parts)
    depth, width = output_map.shape
    part_rows = parts[0].shape[0]
    total_rows = part_rows * groups
    steps = 8
    tile = depth // steps
    return pl.pallas_call(
        functools.partial(project_kernel, groups=groups, rows=rows, steps=steps),
        grid_spec=pltpu.PrefetchScalarGridSpec(
            num_scalar_prefetch=1,
            grid=(steps,),
            in_specs=[pl.BlockSpec((part_rows, tile), lambda k, place: (0, k))] * groups
            + [pl.BlockSpec((tile, width), lambda k, place: (k, 0))],
            out_specs=[pl.BlockSpec((total_rows // 2, width), lambda k, place: (0, 0))] * 2,
            scratch_shapes=[pltpu.VMEM((total_rows, width), F32)] * 2,
        ),
        out_shape=[
            jax.ShapeDtypeStruct((total_rows // 2, width), F32),
            jax.ShapeDtypeStruct((total_rows // 2, width), BF16),
        ],
        compiler_params=pltpu.CompilerParams(vmem_limit_bytes=24 * 2**20),
        cost_estimate=pl.CostEstimate(
            flops=2 * total_rows * depth * width,
            bytes_accessed=2 * (total_rows * depth + depth * width),
            transcendentals=0,
        ),
    )(place, *parts, output_map)


def expert_kernel(place_ref, *refs, groups, blocks, width):
    parts = refs[:groups]
    gain_ref, in_ref, gate_ref, down_ref, out_ref, total, squares, activated = refs[groups:]
    step = pl.program_id(0)
    line = blocks // groups
    hidden_units = down_ref.shape[0]

    @pl.when(step == 0)
    def _():
        total[...] = jnp.zeros_like(total)
        squares[...] = jnp.zeros_like(squares)

    for group, part in enumerate(parts):

        @pl.when((step >= group * line) & (step < (group + 1) * line))
        def _(part=part):
            wide = part[0].astype(F32)
            squares[...] += jnp.sum(wide * wide, axis=1, keepdims=True)
            scaled = (wide * gain_ref[0].astype(F32)).astype(BF16)
            total[...] += jnp.dot(scaled, in_ref[0], preferred_element_type=F32)

    @pl.when(step == blocks)
    def _():
        level = lax.rsqrt(squares[...] / width + 1e-06)
        gate_part = total[:, :hidden_units] * level
        up_part = total[:, hidden_units:] * level
        raised = gate_part / (1.0 + jnp.exp(-gate_part))
        activated[...] = (raised * up_part * gate_ref[...]).astype(BF16)

    @pl.when(step >= blocks)
    def _():
        out_ref[...] = jnp.dot(
            activated[...], down_ref[...], preferred_element_type=F32
        ).astype(BF16)


def expert_part(parts, gain, expert_rows, gates, down, place):
    groups = len(parts)
    line, tokens, columns = parts[0].shape
    blocks = groups * line
    units, width = down.shape
    tile = 1024 if width % 1024 == 0 else width
    out_steps = width // tile

    def part_spec(group):
        return pl.BlockSpec(
            (1, tokens, columns),
            lambda b, place: (jnp.clip(b - group * line, 0, line - 1), 0, 0),
        )

    def placed(b, place):
        return (place[jnp.minimum(b, blocks - 1)], 0, 0)

    return pl.pallas_call(
        functools.partial(expert_kernel, groups=groups, blocks=blocks, width=float(width)),
        grid_spec=pltpu.PrefetchScalarGridSpec(
            num_scalar_prefetch=1,
            grid=(blocks + out_steps,),
            in_specs=[part_spec(group) for group in range(groups)]
            + [
                pl.BlockSpec((1, 1, columns), placed),
                pl.BlockSpec((1, columns, 2 * units), placed),
                pl.BlockSpec((tokens, 1), lambda b, place: (0, 0)),
                pl.BlockSpec((units, tile), lambda b, place: (0, jnp.maximum(b - blocks, 0))),
            ],
            out_specs=pl.BlockSpec((tokens, tile), lambda b, place: (0, jnp.maximum(b - blocks, 0))),
            scratch_shapes=[
                pltpu.VMEM((tokens, 2 * units), F32),
                pltpu.VMEM((tokens, 1), F32),
                pltpu.VMEM((tokens, units), BF16),
            ],
        ),
        out_shape=jax.ShapeDtypeStruct((tokens, width), BF16),
        compiler_params=pltpu.CompilerParams(vmem_limit_bytes=24 * 2**20),
        cost_estimate=pl.CostEstimate(
            flops=6 * tokens * width * units,
            bytes_accessed=6 * width * units + 4 * tokens * width,
            transcendentals=tokens * units,
        ),
    )(place, *parts, gain, expert_rows, gates, down)


def on_device(
    queries,
    latent_cache,
    lengths,
    value_lift,
    output_map,
    residual,
    norm_gain,
    expert_ids,
    gate_values,
    expert_in,
    expert_down,
):
    request_count = queries.shape[0]
    latent_width = value_lift.shape[1]
    half_heads = value_lift.shape[0]
    value_width = value_lift.shape[2]
    half_slots = latent_cache.shape[1]
    token_count, model_width = residual.shape
    chips = lax.axis_size("dev")
    plane = plane_of(chips)
    line = chips // plane
    columns = output_map.shape[1]
    experts = chips // 2
    units = expert_down.shape[1]
    side = lax.axis_index("side")
    chip = lax.axis_index("dev")
    line_at, plane_at = chip // plane, chip % plane
    half_tokens = token_count * chips

    def line_hop(value, k):
        return hop(value, "dev", chips, k * plane)

    def plane_hop(value, k):
        return hop(value, "dev", chips, k)

    def swap(value):
        return hop(value, "side", 2, 1)

    chosen = expert_ids[:, :, None] == jnp.arange(experts, dtype=jnp.int32)[None, None, :]
    weights = jnp.sum(jnp.where(chosen, gate_values[:, :, None], 0.0), axis=1)
    all_weights = lax.all_gather(weights, ("side", "dev"), axis=0, tiled=True)
    own_weights = lax.dynamic_slice_in_dim(all_weights, chip // 2, 1, 1)
    gates_own = lax.dynamic_slice_in_dim(own_weights, side * half_tokens, half_tokens, 0)
    gates_other = lax.dynamic_slice_in_dim(own_weights, (1 - side) * half_tokens, half_tokens, 0)

    residual_blocks = residual.reshape(token_count, chips, columns).swapaxes(0, 1)
    residual_columns = lax.all_to_all(
        residual_blocks, "dev", split_axis=0, concat_axis=0, tiled=True
    ).reshape(half_tokens, columns)

    score_scale = QKD ** (-0.5)
    scores = (
        jnp.einsum("rhc,rpc->rhp", queries, latent_cache, preferred_element_type=F32) * score_scale
    )
    positions = side * half_slots + jnp.arange(half_slots, dtype=jnp.int32)
    usable = (positions[None, :] < lengths[:, None])[:, None, :]
    masked = jnp.where(usable, scores, -1e30)
    local_top = jnp.max(masked, axis=2)
    raised = jnp.where(usable, jnp.exp(masked - local_top[:, :, None]), 0.0)
    local_total = jnp.sum(raised, axis=2)
    local_latent = jnp.einsum(
        "rhp,rpc->rhc",
        raised.astype(BF16),
        latent_cache[:, :, :latent_width],
        preferred_element_type=F32,
    )
    local_latent = (local_latent / jnp.maximum(local_total, 1e-30)[:, :, None]).astype(BF16)

    def heads_of(value, which):
        return lax.dynamic_slice_in_dim(value, which * half_heads, half_heads, 1)

    stats = jnp.stack([local_top, local_total], axis=2)
    other_latent = swap(heads_of(local_latent, 1 - side))
    other_stats = swap(heads_of(stats, 1 - side))
    own_latent = heads_of(local_latent, side)
    own_stats = heads_of(stats, side)
    top = jnp.maximum(own_stats[:, :, 0], other_stats[:, :, 0])
    own_share = own_stats[:, :, 1] * jnp.exp(own_stats[:, :, 0] - top)
    other_share = other_stats[:, :, 1] * jnp.exp(other_stats[:, :, 0] - top)
    share_sum = own_share + other_share
    latent_out = (
        own_latent.astype(F32) * (own_share / share_sum)[:, :, None]
        + other_latent.astype(F32) * (other_share / share_sum)[:, :, None]
    ).astype(BF16)
    head_values = jnp.einsum("rhc,hcv->rhv", latent_out, value_lift, preferred_element_type=F32)
    head_values = head_values.astype(BF16).reshape(request_count, half_heads * value_width)

    def gather(block):
        stacked = jnp.stack([block] + [line_hop(block, k) for k in range(1, line)])
        return [stacked] + [plane_hop(stacked, k) for k in range(1, plane)]

    places = [
        (line_at ^ k_line) * plane + (plane_at ^ k_plane)
        for k_plane in range(plane)
        for k_line in range(line)
    ]
    place = jnp.stack(places + [side]).astype(jnp.int32)
    gathered = [
        part.reshape(line * request_count, half_heads * value_width) for part in gather(head_values)
    ]
    own_columns, sent_columns = project(gathered, output_map, place, request_count)
    attention = own_columns + swap(sent_columns).astype(F32)
    hidden = (residual_columns.astype(F32) + attention).astype(BF16)

    hidden_own = gather(hidden)
    hidden_other = [swap(part) for part in hidden_own]
    gain = norm_gain.reshape(chips, 1, columns)
    expert_rows = expert_in.reshape(chips, columns, 2 * units)
    down = expert_down[0]
    partial_own = expert_part(hidden_own, gain, expert_rows, gates_own, down, place)
    partial_other = expert_part(hidden_other, gain, expert_rows, gates_other, down, place)
    partial = (partial_own.astype(F32) + swap(partial_other).astype(F32)).astype(BF16)

    partial = partial.reshape(line, plane, token_count, model_width)

    def to_plane(k):
        return lax.dynamic_index_in_dim(partial, plane_at ^ k, 1, keepdims=False)

    plane_sum = to_plane(0).astype(F32)
    for k in range(1, plane):
        plane_sum = plane_sum + plane_hop(to_plane(k), k).astype(F32)
    plane_sum = plane_sum.astype(BF16)

    def to_line(k):
        return lax.dynamic_index_in_dim(plane_sum, line_at ^ k, 0, keepdims=False)

    routed_sum = to_line(0).astype(F32)
    for k in range(1, line):
        routed_sum = routed_sum + line_hop(to_line(k), k).astype(F32)

    stacked = jnp.concatenate(
        [lax.dynamic_slice_in_dim(part, chip * token_count, token_count, 1) for part in hidden_own]
    )
    order = jnp.stack(
        [
            ((plane_at ^ (at % plane)) * line + (line_at ^ (at // plane)))
            for at in range(chips)
        ]
    )
    own_hidden = jnp.take(stacked, order, axis=0).swapaxes(0, 1).reshape(token_count, model_width)
    return (own_hidden.astype(F32) + routed_sum).astype(BF16)


def solution(mesh):
    in_specs = (
        P("dev", None, None),
        P("dev", "side", None),
        P("dev"),
        P("side", None, None),
        P("side", "dev"),
        P(("side", "dev"), None),
        P(),
        P(("side", "dev"), None),
        P(("side", "dev"), None),
        P("dev", None, None, "side"),
        P("dev", "side", None),
    )
    out_specs = P(("side", "dev"), None)
    return jax.shard_map(
        on_device, mesh=mesh, in_specs=in_specs, out_specs=out_specs, check_vma=False
    )
```

time: 342 us -> 265 us (0.77)
  waiting for transfers between devices: 260 us -> 82.5 us
  blocking collectives: 5.14 us -> 67.1 us
  Pallas kernels: 0 us -> 27.5 us
  local copies, waits for them, and re-layouts: 12.4 us -> 37.7 us
  matrix products: 28.5 us -> 10 us
  starting transfers between devices: 14.1 us -> 31.5 us
  between operations: 13.3 us -> 0.4 us
    all_to_all x3 -> x1, waiting for transfers between devices: 171 us -> 0.01 us  [on_device(): lax.all_to_all(residual_blocks, 'dev', split_axis=0, concat_axis=0, tiled...]
    ppermute x0 -> x26, waiting for transfers between devices: none -> 82.5 us  [hop(): return lax.ppermute(value, axis, [(i, i ^ mask) for i in range(size)])]
    all_gather x0 -> x1, blocking collectives: none -> 67.1 us  [on_device(): all_weights = lax.all_gather(weights, ('side', 'dev'), axis=0, tiled=True)]
    all_gather x1 -> x0, waiting for transfers between devices: 61.9 us -> none  [on_device(): lax.all_gather(head_values, 'dev', axis=0, tiled=True)]
    pallas_call x0 -> x3, Pallas kernels: none -> 27.5 us  [the longest x2 23.2 us: expert_part(): pl.pallas_call(functools.partial(expert_kernel, groups=groups, blocks=blo...]
    ppermute x0 -> x26, starting transfers between devices: none -> 25.7 us  [hop(): return lax.ppermute(value, axis, [(i, i ^ mask) for i in range(size)])]
    psum x1 -> x0, waiting for transfers between devices: 20.8 us -> none  [on_device(): row_total, latent_sum = lax.psum((local_total, local_latent), 'side')]
    dot_general x7 -> x2, matrix products: 24 us -> 5.37 us  [the longest x1 3.07 us: on_device(): jnp.einsum('rhc,hcv->rhv', latent_out, value_lift, preferred_element_type...]
  transfers between devices with their start and end apart: 6 -> 27, of which waited for: 6 -> 16; matrix products, arithmetic and copies ran while one was open for 3% -> 9% of each run, Pallas kernels for 0% -> 5%
where the time goes in v1:
time: 265 us; the launch traced here: 264 us
  waiting for transfers between devices  82.5 us (31%)
  blocking collectives  67.1 us (25%)
  local copies, waits for them, and re-layouts  37.7 us (14%)
  starting transfers between devices  31.5 us (12%)
  Pallas kernels  27.5 us (10%)
  matrix products  10 us (4%)
  other arithmetic  7.47 us (3%)
    ppermute x26, waiting for transfers between devices, hop(): return lax.ppermute(value, axis, [(i, i ^ mask) for i in range(size)])  82.5 us
    all_gather x1, blocking collectives, on_device(): all_weights = lax.all_gather(weights, ('side', 'dev'), axis=0, tiled=True)  67.1 us
    ppermute x26, starting transfers between devices, hop(): return lax.ppermute(value, axis, [(i, i ^ mask) for i in range(size)])  25.7 us
    pallas_call x2, Pallas kernels, expert_part(): pl.pallas_call(functools.partial(expert_kernel, groups=groups, blocks=blo...  23.2 us
    unnamed x23, local copies, waits for them, and re-layouts  20 us
    reshape x1, local copies, waits for them, and re-layouts, on_device(): expert_rows = expert_in.reshape(chips, columns, 2 * units)  12.4 us
    all_to_all x1, starting transfers between devices, on_device(): lax.all_to_all(residual_blocks, 'dev', split_axis=0, concat_axis=0, tiled...  5.77 us
  transfers between devices with their start and end apart: 27, of which 16 were waited for; matrix products, arithmetic and copies ran while one was open for 9% of the time, Pallas kernels for 5%

profile of v1, /device:TPU:0, one launch (start us, length us, event | category | flops | bytes accessed | tf_op | source)
XLA Modules:
  0.0 264.2 jit_solution(15865013048835639911)
XLA Ops:
  1.3 4.7 %fusion.30 = (f32[16,64]{1,0:T(8,128)S(1)}, f32[16,64,384]{2,1,0:T(8,128)S(1)}) fusion(bf16[16,64,576]{2,1,0:T(8,128)(2,1)S(1)} %copy-done, bf16[16,384,576]{1,2,0:T(8,128)(2,1)} %param.12, pred[16,384]{1,0:T(8,128)(4,1)S(1)} %broadcast_compare_fusion), kind=kOutput, calls=%fused_computation.71 | convolution fusion | flops 454163456 | bytes 9840640 | tf_op jit(solution)/shard_map/rhc,rpc->rhp/dot_general | solution.py:214
  11.3 3.1 %convolution_convert_fusion = bf16[32,16,128]{2,1,0:T(8,128)(2,1)S(1)} fusion(bf16[32,512,128]{2,1,0:T(8,128)(2,1)} %param.14, bf16[16,32,512]{2,1,0:T(8,128)(2,1)S(1)} %add_convert_fusion.1), kind=kOutput, calls=%fused_computation.9 | convolution fusion | flops 67174400 | bytes 4849664 | tf_op jit(solution)/shard_map/rhc,hcv->rhv/dot_general | solution.py:246
  14.4 5.0 %collective-permute-start.4 = (bf16[16,4096]{1,0:T(8,128)(2,1)S(1)}, bf16[16,4096]{1,0:T(8,128)(2,1)S(1)}, u32[]{:S(2)}, u32[]{:S(2)}) collective-permute-start(bf16[16,4096]{1,0:T(8,128)(2,1)S(1)} %copy_bitcast_fusion), channel_id=1, source_target_pairs={{0,12},{1,13},{2,14},{3,15},{4,8},{5,9},{6,10},{7,11},{8,4},{9,5},... | collective-permute-start | bytes 393224 | tf_op jit(solution)/shard_map/ppermute | solution.py:16
  20.2 3.6 %collective-permute-done.4 = bf16[16,4096]{1,0:T(8,128)(2,1)S(1)} collective-permute-done((bf16[16,4096]{1,0:T(8,128)(2,1)S(1)}, bf16[16,4096]{1,0:T(8,128)(2,1)S(1)}, u32[]{:S(2)}, u32[]{:S(2)}) %collective-permute-start.4) | collective-permute-done | bytes 131104 | tf_op jit(solution)/shard_map/ppermute | solution.py:16
  23.9 7.0 %collective-permute-done.3 = bf16[16,4096]{1,0:T(8,128)(2,1)S(1)} collective-permute-done((bf16[16,4096]{1,0:T(8,128)(2,1)S(1)}, bf16[16,4096]{1,0:T(8,128)(2,1)S(1)}, u32[]{:S(2)}, u32[]{:S(2)}) %collective-permute-start.3) | collective-permute-done | bytes 131104 | tf_op jit(solution)/shard_map/ppermute | solution.py:16
  36.3 5.8 %all-to-all-start = ((bf16[16,8,448]{2,1,0:T(8,128)(2,1)}), bf16[16,8,448]{2,1,0:T(8,128)(2,1)S(1)}, u32[]{:S(2)}, u32[]{:S(2)}) async-start(bf16[16,8,448]{2,1,0:T(8,128)(2,1)} %bitcast.116), calls=%async_computation | async-start | bytes 262144 | tf_op jit(solution)/shard_map/all_to_all | solution.py:208
  42.1 6.4 %copy.32.refs_4_ = bf16[4096,448]{1,0:T(8,128)(2,1)} copy(bf16[4096,448]{0,1:T(8,128)(2,1)} %param.15) | data formatting | bytes 7340032 | tf_op args[4]
  48.7 8.9 %collective-permute-done.6 = bf16[4,16,4096]{2,1,0:T(8,128)(2,1)S(1)} collective-permute-done((bf16[4,16,4096]{2,1,0:T(8,128)(2,1)S(1)}, bf16[4,16,4096]{2,1,0:T(8,128)(2,1)S(1)}, u32[]{:S(2)}, u32[]{:S(2)}) %collective-permute-start.6) | collective-permute-done | bytes 524320 | tf_op jit(solution)/shard_map/ppermute | solution.py:16
  59.8 4.4 %shard_map.109 = (f32[128,448]{1,0:T(8,128)S(1)}, bf16[128,448]{1,0:T(8,128)(2,1)}) custom-call(s32[17]{0:T(128)S(1)} %stack.205.place_ref, bf16[64,4096]{1,0:T(8,128)(2,1)S(1)} %bitcast.109, bf16[64,4096]{1,0:T(8,128)(2,1)S(1)} %bitcast.112, bf16[64,4096]{1,0:T(8,128)(2,1)S(1)} %bitcast.111, bf16[64,4096]{1,0:T(8,128)(2,1)S(1)} %bitcast.110, ...), custom_call_target="tpu_custom_call" | custom-call | flops 939524096 | bytes 5767168 | tf_op jit(solution)/shard_map/pallas_call | solution.py:56
  71.9 3.9 %collective-permute-done.11 = bf16[128,448]{1,0:T(8,128)(2,1)S(1)} collective-permute-done((bf16[128,448]{1,0:T(8,128)(2,1)S(1)}, bf16[128,448]{1,0:T(8,128)(2,1)S(1)}, u32[]{:S(2)}, u32[]{:S(2)}) %collective-permute-start.11) | collective-permute-done | bytes 114720 | tf_op jit(solution)/shard_map/ppermute | solution.py:16
  75.7 5.0 %collective-permute-done.10 = bf16[128,448]{1,0:T(8,128)(2,1)S(1)} collective-permute-done((bf16[128,448]{1,0:T(8,128)(2,1)S(1)}, bf16[128,448]{1,0:T(8,128)(2,1)S(1)}, u32[]{:S(2)}, u32[]{:S(2)}) %collective-permute-start.10) | collective-permute-done | bytes 114720 | tf_op jit(solution)/shard_map/ppermute | solution.py:16
  84.4 12.2 %collective-permute-done.14.refs_3_ = bf16[4,128,448]{2,1,0:T(8,128)(2,1)S(1)} collective-permute-done((bf16[4,128,448]{2,1,0:T(8,128)(2,1)S(1)}, bf16[4,128,448]{2,1,0:T(8,128)(2,1)S(1)}, u32[]{:S(2)}, u32[]{:S(2)}) %collective-permute-start.14) | collective-permute-done | bytes 458784 | tf_op jit(solution)/shard_map/ppermute | solution.py:16
  96.7 10.2 %collective-permute-done.13.refs_2_ = bf16[4,128,448]{2,1,0:T(8,128)(2,1)S(1)} collective-permute-done((bf16[4,128,448]{2,1,0:T(8,128)(2,1)S(1)}, bf16[4,128,448]{2,1,0:T(8,128)(2,1)S(1)}, u32[]{:S(2)}, u32[]{:S(2)}) %collective-permute-start.13) | collective-permute-done | bytes 458784 | tf_op jit(solution)/shard_map/ppermute | solution.py:16
  108.2 12.4 %reshape.762.refs_5_ = bf16[16,448,512]{2,1,0:T(8,128)(2,1)} reshape(bf16[1,7168,2,256]{3,2,1,0:T(2,128)(2,1)} %param.20) | data formatting | bytes 14680064 | tf_op jit(solution)/shard_map/reshape | solution.py:269
  120.7 67.1 %all_gather.3 = f32[256,8]{1,0:T(8,128)S(1)} all-gather(f32[8,8]{1,0:T(8,128)S(1)} %select_reduce_fusion), channel_id=1, replica_groups=mesh['side'=2,'dev'=16] {'side','dev'}, dimensions={0}, use_global_device_ids=true | all-gather | bytes 8448 | tf_op jit(solution)/shard_map/all_gather | solution.py:202
  188.0 3.1 %copy-done.1 = bf16[16,448,512]{2,1,0:T(8,128)(2,1)S(1)} copy-done((bf16[16,448,512]{2,1,0:T(8,128)(2,1)S(1)}, bf16[16,448,512]{2,1,0:T(8,128)(2,1)}, u32[]{:S(2)}) %copy-start.1) | copy-done | bytes 7340056
  193.1 15.3 %shard_map.111 = bf16[128,7168]{1,0:T(8,128)(2,1)} custom-call(s32[17]{0:T(128)S(1)} %stack.205.place_ref, bf16[4,128,448]{2,1,0:T(8,128)(2,1)} %collective-permute-done.15.refs_0_, bf16[4,128,448]{2,1,0:T(8,128)(2,1)} %collective-permute-done.16.refs_1_, bf16[4,128,448]{2,1,0:T(8,128)(2,1)} %collective-permute-done.17.refs_2_, ...), custom_call_target="tpu_custom_call" | custom-call | flops 1409286144 | bytes 14680064 | tf_op jit(solution)/shard_map/pallas_call | solution.py:132
  209.0 3.1 %copy-done.2 = bf16[16,448,512]{2,1,0:T(8,128)(2,1)S(1)} copy-done((bf16[16,448,512]{2,1,0:T(8,128)(2,1)S(1)}, bf16[16,448,512]{2,1,0:T(8,128)(2,1)}, u32[]{:S(2)}) %copy-start.2) | copy-done | bytes 7340056
  214.1 7.9 %shard_map.110 = bf16[128,7168]{1,0:T(8,128)(2,1)S(1)} custom-call(s32[17]{0:T(128)S(1)} %stack.205.place_ref, bf16[4,128,448]{2,1,0:T(8,128)(2,1)S(1)} %pad_maximum_fusion.1.refs_0_, bf16[4,128,448]{2,1,0:T(8,128)(2,1)S(1)} %collective-permute-done.12.refs_1_, bf16[4,128,448]{2,1,0:T(8,128)(2,1)S(1)} %collective-permute-done.13.refs_2_, ...), custom_call_target="tpu_custom_call" | custom-call | flops 1409286144 | bytes 14680064 | tf_op jit(solution)/shard_map/pallas_call | solution.py:132
  225.1 3.5 %collective-permute-start.21 = (bf16[4,8,7168]{2,1,0:T(8,128)(2,1)}, bf16[4,8,7168]{2,1,0:T(8,128)(2,1)}, u32[]{:S(2)}, u32[]{:S(2)}) collective-permute-start(bf16[4,8,7168]{2,1,0:T(8,128)(2,1)} %get-tuple-element.11), channel_id=1, source_target_pairs={{0,2},{1,3},{2,0},{3,1},{4,6},{5,7},{6,4},{7,5},{8,10},{9,11},{10,... | collective-permute-start | bytes 1376264 | tf_op jit(solution)/shard_map/ppermute | solution.py:16
  229.2 9.5 %collective-permute-done.20 = bf16[4,8,7168]{2,1,0:T(8,128)(2,1)} collective-permute-done((bf16[4,8,7168]{2,1,0:T(8,128)(2,1)}, bf16[4,8,7168]{2,1,0:T(8,128)(2,1)}, u32[]{:S(2)}, u32[]{:S(2)}) %collective-permute-start.20) | collective-permute-done | bytes 458784 | tf_op jit(solution)/shard_map/ppermute | solution.py:16
  238.8 7.4 %collective-permute-done.22 = bf16[4,8,7168]{2,1,0:T(8,128)(2,1)} collective-permute-done((bf16[4,8,7168]{2,1,0:T(8,128)(2,1)}, bf16[4,8,7168]{2,1,0:T(8,128)(2,1)}, u32[]{:S(2)}, u32[]{:S(2)}) %collective-permute-start.22) | collective-permute-done | bytes 458784 | tf_op jit(solution)/shard_map/ppermute | solution.py:16
  250.9 3.4 %collective-permute-start.24 = (bf16[8,7168]{1,0:T(8,128)(2,1)S(1)}, bf16[8,7168]{1,0:T(8,128)(2,1)S(1)}, u32[]{:S(2)}, u32[]{:S(2)}) collective-permute-start(bf16[8,7168]{1,0:T(8,128)(2,1)S(1)} %get-tuple-element.14), channel_id=1, source_target_pairs={{0,8},{1,9},{2,10},{3,11},{4,12},{5,13},{6,14},{7,15},{8,0},{9,1},... | collective-permute-start | bytes 344072 | tf_op jit(solution)/shard_map/ppermute | solution.py:16
  258.2 5.3 %collective-permute-done.24 = bf16[8,7168]{1,0:T(8,128)(2,1)S(1)} collective-permute-done((bf16[8,7168]{1,0:T(8,128)(2,1)S(1)}, bf16[8,7168]{1,0:T(8,128)(2,1)S(1)}, u32[]{:S(2)}, u32[]{:S(2)}) %collective-permute-start.24) | collective-permute-done | bytes 114720 | tf_op jit(solution)/shard_map/ppermute | solution.py:16
  (100 shorter events, 45.7 us)
Async XLA Ops:
  14.4 9.4 %collective-permute-start.4 = (bf16[16,4096]{1,0:T(8,128)(2,1)S(1)}, bf16[16,4096]{1,0:T(8,128)(2,1)S(1)}, u32[]{:S(2)}, u32[]{:S(2)}) collective-permute-start(bf16[16,4096]{1,0:T(8,128)(2,1)S(1)} %copy_bitcast_fusion), channel_id=1, source_target_pairs={{0,12},{1,13},{2,14},{3,15},{4,8},{5,9},{6,10},{7,11},{8,4},{9,5},... | collective-permute-start | bytes 393224 | tf_op jit(solution)/shard_map/ppermute | solution.py:16
  19.5 11.4 %collective-permute-start.3 = (bf16[16,4096]{1,0:T(8,128)(2,1)S(1)}, bf16[16,4096]{1,0:T(8,128)(2,1)S(1)}, u32[]{:S(2)}, u32[]{:S(2)}) collective-permute-start(bf16[16,4096]{1,0:T(8,128)(2,1)S(1)} %copy_bitcast_fusion), channel_id=1, source_target_pairs={{0,8},{1,9},{2,10},{3,11},{4,12},{5,13},{6,14},{7,15},{8,0},{9,1},... | collective-permute-start | bytes 393224 | tf_op jit(solution)/shard_map/ppermute | solution.py:16
  19.5 11.4 %collective-permute-start.2 = (bf16[16,4096]{1,0:T(8,128)(2,1)S(1)}, bf16[16,4096]{1,0:T(8,128)(2,1)S(1)}, u32[]{:S(2)}, u32[]{:S(2)}) collective-permute-start(bf16[16,4096]{1,0:T(8,128)(2,1)S(1)} %copy_bitcast_fusion), channel_id=1, source_target_pairs={{0,4},{1,5},{2,6},{3,7},{4,0},{5,1},{6,2},{7,3},{8,12},{9,13},{10,... | collective-permute-start | bytes 393224 | tf_op jit(solution)/shard_map/ppermute | solution.py:16
  30.9 17.7 %collective-permute-start.7 = (bf16[4,16,4096]{2,1,0:T(8,128)(2,1)S(1)}, bf16[4,16,4096]{2,1,0:T(8,128)(2,1)S(1)}, u32[]{:S(2)}, u32[]{:S(2)}) collective-permute-start(bf16[4,16,4096]{2,1,0:T(8,128)(2,1)S(1)} %pad_maximum_fusion), channel_id=1, source_target_pairs={{0,3},{1,2},{2,1},{3,0},{4,7},{5,6},{6,5},{7,4},{8,11},{9,10},{10,... | collective-permute-start | bytes 1572872 | tf_op jit(solution)/shard_map/ppermute | solution.py:16
  33.5 24.1 %collective-permute-start.6 = (bf16[4,16,4096]{2,1,0:T(8,128)(2,1)S(1)}, bf16[4,16,4096]{2,1,0:T(8,128)(2,1)S(1)}, u32[]{:S(2)}, u32[]{:S(2)}) collective-permute-start(bf16[4,16,4096]{2,1,0:T(8,128)(2,1)S(1)} %pad_maximum_fusion), channel_id=1, source_target_pairs={{0,2},{1,3},{2,0},{3,1},{4,6},{5,7},{6,4},{7,5},{8,10},{9,11},{10,... | collective-permute-start | bytes 1572872 | tf_op jit(solution)/shard_map/ppermute | solution.py:16
  34.0 23.6 %collective-permute-start.5 = (bf16[4,16,4096]{2,1,0:T(8,128)(2,1)S(1)}, bf16[4,16,4096]{2,1,0:T(8,128)(2,1)S(1)}, u32[]{:S(2)}, u32[]{:S(2)}) collective-permute-start(bf16[4,16,4096]{2,1,0:T(8,128)(2,1)S(1)} %pad_maximum_fusion), channel_id=1, source_target_pairs={{0,1},{1,0},{2,3},{3,2},{4,5},{5,4},{6,7},{7,6},{8,9},{9,8},{10,11... | collective-permute-start | bytes 1572872 | tf_op jit(solution)/shard_map/ppermute | solution.py:16
  36.3 28.6 %all-to-all-start = ((bf16[16,8,448]{2,1,0:T(8,128)(2,1)}), bf16[16,8,448]{2,1,0:T(8,128)(2,1)S(1)}, u32[]{:S(2)}, u32[]{:S(2)}) async-start(bf16[16,8,448]{2,1,0:T(8,128)(2,1)} %bitcast.116), calls=%async_computation | async-start | bytes 262144 | tf_op jit(solution)/shard_map/all_to_all | solution.py:208
  67.4 8.3 %collective-permute-start.11 = (bf16[128,448]{1,0:T(8,128)(2,1)S(1)}, bf16[128,448]{1,0:T(8,128)(2,1)S(1)}, u32[]{:S(2)}, u32[]{:S(2)}) collective-permute-start(bf16[128,448]{1,0:T(8,128)(2,1)S(1)} %fusion.14), channel_id=1, source_target_pairs={{0,12},{1,13},{2,14},{3,15},{4,8},{5,9},{6,10},{7,11},{8,4},{9,5},... | collective-permute-start | bytes 344072 | tf_op jit(solution)/shard_map/ppermute | solution.py:16
  70.0 10.8 %collective-permute-start.10 = (bf16[128,448]{1,0:T(8,128)(2,1)S(1)}, bf16[128,448]{1,0:T(8,128)(2,1)S(1)}, u32[]{:S(2)}, u32[]{:S(2)}) collective-permute-start(bf16[128,448]{1,0:T(8,128)(2,1)S(1)} %fusion.14), channel_id=1, source_target_pairs={{0,8},{1,9},{2,10},{3,11},{4,12},{5,13},{6,14},{7,15},{8,0},{9,1},... | collective-permute-start | bytes 344072 | tf_op jit(solution)/shard_map/ppermute | solution.py:16
  70.0 10.8 %collective-permute-start.9 = (bf16[128,448]{1,0:T(8,128)(2,1)S(1)}, bf16[128,448]{1,0:T(8,128)(2,1)S(1)}, u32[]{:S(2)}, u32[]{:S(2)}) collective-permute-start(bf16[128,448]{1,0:T(8,128)(2,1)S(1)} %fusion.14), channel_id=1, source_target_pairs={{0,4},{1,5},{2,6},{3,7},{4,0},{5,1},{6,2},{7,3},{8,12},{9,13},{10,... | collective-permute-start | bytes 344072 | tf_op jit(solution)/shard_map/ppermute | solution.py:16
  80.8 15.8 %collective-permute-start.14 = (bf16[4,128,448]{2,1,0:T(8,128)(2,1)S(1)}, bf16[4,128,448]{2,1,0:T(8,128)(2,1)S(1)}, u32[]{:S(2)}, u32[]{:S(2)}) collective-permute-start(bf16[4,128,448]{2,1,0:T(8,128)(2,1)S(1)} %pad_maximum_fusion.1.refs_0_), channel_id=1, source_target_pairs={{0,3},{1,2},{2,1},{3,0},{4,7},{5,6},{6,5},{7,4},{8,11},{9,10},{10,... | collective-permute-start | bytes 1376264 | tf_op jit(solution)/shard_map/ppermute | solution.py:16
  82.6 24.3 %collective-permute-start.13 = (bf16[4,128,448]{2,1,0:T(8,128)(2,1)S(1)}, bf16[4,128,448]{2,1,0:T(8,128)(2,1)S(1)}, u32[]{:S(2)}, u32[]{:S(2)}) collective-permute-start(bf16[4,128,448]{2,1,0:T(8,128)(2,1)S(1)} %pad_maximum_fusion.1.refs_0_), channel_id=1, source_target_pairs={{0,2},{1,3},{2,0},{3,1},{4,6},{5,7},{6,4},{7,5},{8,10},{9,11},{10,... | collective-permute-start | bytes 1376264 | tf_op jit(solution)/shard_map/ppermute | solution.py:16
  83.9 23.0 %collective-permute-start.12 = (bf16[4,128,448]{2,1,0:T(8,128)(2,1)S(1)}, bf16[4,128,448]{2,1,0:T(8,128)(2,1)S(1)}, u32[]{:S(2)}, u32[]{:S(2)}) collective-permute-start(bf16[4,128,448]{2,1,0:T(8,128)(2,1)S(1)} %pad_maximum_fusion.1.refs_0_), channel_id=1, source_target_pairs={{0,1},{1,0},{2,3},{3,2},{4,5},{5,4},{6,7},{7,6},{8,9},{9,8},{10,11... | collective-permute-start | bytes 1376264 | tf_op jit(solution)/shard_map/ppermute | solution.py:16
  84.4 103.5 %collective-permute-start.15 = (bf16[4,128,448]{2,1,0:T(8,128)(2,1)S(1)}, bf16[4,128,448]{2,1,0:T(8,128)(2,1)}, u32[]{:S(2)}, u32[]{:S(2)}) collective-permute-start(bf16[4,128,448]{2,1,0:T(8,128)(2,1)S(1)} %pad_maximum_fusion.1.refs_0_), channel_id=1, source_target_pairs={{0,16},{16,0},{1,17},{17,1},{2,18},{18,2},{3,19},{19,3},{4,20},{20... | collective-permute-start | bytes 1376264 | tf_op jit(solution)/shard_map/ppermute | solution.py:16
  96.7 91.3 %collective-permute-start.18 = (bf16[4,128,448]{2,1,0:T(8,128)(2,1)S(1)}, bf16[4,128,448]{2,1,0:T(8,128)(2,1)}, u32[]{:S(2)}, u32[]{:S(2)}) collective-permute-start(bf16[4,128,448]{2,1,0:T(8,128)(2,1)S(1)} %collective-permute-done.14.refs_3_), channel_id=1, source_target_pairs={{0,16},{16,0},{1,17},{17,1},{2,18},{18,2},{3,19},{19,3},{4,20},{20... | collective-permute-start | bytes 1376264 | tf_op jit(solution)/shard_map/ppermute | solution.py:16
  106.8 81.1 %collective-permute-start.17 = (bf16[4,128,448]{2,1,0:T(8,128)(2,1)S(1)}, bf16[4,128,448]{2,1,0:T(8,128)(2,1)}, u32[]{:S(2)}, u32[]{:S(2)}) collective-permute-start(bf16[4,128,448]{2,1,0:T(8,128)(2,1)S(1)} %collective-permute-done.13.refs_2_), channel_id=1, source_target_pairs={{0,16},{16,0},{1,17},{17,1},{2,18},{18,2},{3,19},{19,3},{4,20},{20... | collective-permute-start | bytes 1376264 | tf_op jit(solution)/shard_map/ppermute | solution.py:16
  106.9 81.1 %collective-permute-start.16 = (bf16[4,128,448]{2,1,0:T(8,128)(2,1)S(1)}, bf16[4,128,448]{2,1,0:T(8,128)(2,1)}, u32[]{:S(2)}, u32[]{:S(2)}) collective-permute-start(bf16[4,128,448]{2,1,0:T(8,128)(2,1)S(1)} %collective-permute-done.12.refs_1_), channel_id=1, source_target_pairs={{0,16},{16,0},{1,17},{17,1},{2,18},{18,2},{3,19},{19,3},{4,20},{20... | collective-permute-start | bytes 1376264 | tf_op jit(solution)/shard_map/ppermute | solution.py:16
  208.4 13.6 %collective-permute-start.19 = (bf16[128,7168]{1,0:T(8,128)(2,1)}, bf16[128,7168]{1,0:T(8,128)(2,1)}, u32[]{:S(2)}, u32[]{:S(2)}) collective-permute-start(bf16[128,7168]{1,0:T(8,128)(2,1)} %shard_map.111), channel_id=1, source_target_pairs={{0,16},{16,0},{1,17},{17,1},{2,18},{18,2},{3,19},{19,3},{4,20},{20... | collective-permute-start | bytes 5505032 | tf_op jit(solution)/shard_map/ppermute | solution.py:16
  225.1 13.7 %collective-permute-start.20 = (bf16[4,8,7168]{2,1,0:T(8,128)(2,1)}, bf16[4,8,7168]{2,1,0:T(8,128)(2,1)}, u32[]{:S(2)}, u32[]{:S(2)}) collective-permute-start(bf16[4,8,7168]{2,1,0:T(8,128)(2,1)} %get-tuple-element.9), channel_id=1, source_target_pairs={{0,1},{1,0},{2,3},{3,2},{4,5},{5,4},{6,7},{7,6},{8,9},{9,8},{10,11... | collective-permute-start | bytes 1376264 | tf_op jit(solution)/shard_map/ppermute | solution.py:16
  225.1 21.0 %collective-permute-start.22 = (bf16[4,8,7168]{2,1,0:T(8,128)(2,1)}, bf16[4,8,7168]{2,1,0:T(8,128)(2,1)}, u32[]{:S(2)}, u32[]{:S(2)}) collective-permute-start(bf16[4,8,7168]{2,1,0:T(8,128)(2,1)} %get-tuple-element.10), channel_id=1, source_target_pairs={{0,3},{1,2},{2,1},{3,0},{4,7},{5,6},{6,5},{7,4},{8,11},{9,10},{10,... | collective-permute-start | bytes 1376264 | tf_op jit(solution)/shard_map/ppermute | solution.py:16
  225.1 23.9 %collective-permute-start.21 = (bf16[4,8,7168]{2,1,0:T(8,128)(2,1)}, bf16[4,8,7168]{2,1,0:T(8,128)(2,1)}, u32[]{:S(2)}, u32[]{:S(2)}) collective-permute-start(bf16[4,8,7168]{2,1,0:T(8,128)(2,1)} %get-tuple-element.11), channel_id=1, source_target_pairs={{0,2},{1,3},{2,0},{3,1},{4,6},{5,7},{6,4},{7,5},{8,10},{9,11},{10,... | collective-permute-start | bytes 1376264 | tf_op jit(solution)/shard_map/ppermute | solution.py:16
  250.8 6.5 %collective-permute-start.23 = (bf16[8,7168]{1,0:T(8,128)(2,1)S(1)}, bf16[8,7168]{1,0:T(8,128)(2,1)S(1)}, u32[]{:S(2)}, u32[]{:S(2)}) collective-permute-start(bf16[8,7168]{1,0:T(8,128)(2,1)S(1)} %get-tuple-element.12), channel_id=1, source_target_pairs={{0,4},{1,5},{2,6},{3,7},{4,0},{5,1},{6,2},{7,3},{8,12},{9,13},{10,... | collective-permute-start | bytes 344072 | tf_op jit(solution)/shard_map/ppermute | solution.py:16
  250.8 7.3 %collective-permute-start.25 = (bf16[8,7168]{1,0:T(8,128)(2,1)S(1)}, bf16[8,7168]{1,0:T(8,128)(2,1)S(1)}, u32[]{:S(2)}, u32[]{:S(2)}) collective-permute-start(bf16[8,7168]{1,0:T(8,128)(2,1)S(1)} %get-tuple-element.13), channel_id=1, source_target_pairs={{0,12},{1,13},{2,14},{3,15},{4,8},{5,9},{6,10},{7,11},{8,4},{9,5},... | collective-permute-start | bytes 344072 | tf_op jit(solution)/shard_map/ppermute | solution.py:16
  250.9 12.6 %collective-permute-start.24 = (bf16[8,7168]{1,0:T(8,128)(2,1)S(1)}, bf16[8,7168]{1,0:T(8,128)(2,1)S(1)}, u32[]{:S(2)}, u32[]{:S(2)}) collective-permute-start(bf16[8,7168]{1,0:T(8,128)(2,1)S(1)} %get-tuple-element.14), channel_id=1, source_target_pairs={{0,8},{1,9},{2,10},{3,11},{4,12},{5,13},{6,14},{7,15},{8,0},{9,1},... | collective-permute-start | bytes 344072 | tf_op jit(solution)/shard_map/ppermute | solution.py:16
  (14 other events, 54.4 us)

commit v2 on v1

v2 whole, which is shorter than its diff:
```python
import functools

import jax
import jax.numpy as jnp
from jax import lax
from jax.experimental import pallas as pl
from jax.experimental.pallas import tpu as pltpu
from jax.sharding import PartitionSpec as P

QKD = 192
F32 = jnp.float32
BF16 = jnp.bfloat16


def hop(value, axis, size, mask):
    return lax.ppermute(value, axis, [(i, i ^ mask) for i in range(size)])


def budget(*arrays):
    count = sum(2 * a.size * a.dtype.itemsize for a in arrays)
    return 8 * 2**20 + count


def gather(first, second, line, line_hop, plane_hop):
    both = jnp.concatenate([first.reshape(-1), second.reshape(-1)]) if first.shape != second.shape else None
    if both is None:
        sent = jnp.stack([first, second])
        arrived = [line_hop(sent, k) for k in range(1, line)]
        far = [jnp.stack([a[h] for a in arrived]) for h in (0, 1)]
    else:
        far = [jnp.stack([line_hop(part, k) for k in range(1, line)]) for part in (first, second)]
    near = [first[None], second[None]]
    far_at = list(range(1, line))
    halves = []
    near_one = [plane_hop(near[h], 1 + h) for h in (0, 1)]
    near_two = [plane_hop(jnp.concatenate([near[h], near_one[h]]), 2 - h) for h in (0, 1)]
    far_one = [plane_hop(far[h], 1 + h) for h in (0, 1)]
    far_two = [plane_hop(jnp.concatenate([far[h], far_one[h]]), 2 - h) for h in (0, 1)]
    for h in (0, 1):
        one, two = 1 + h, 2 - h
        halves.append(
            [
                (near[h], [(0, 0)]),
                (near_one[h], [(one, 0)]),
                (near_two[h], [(two, 0), (3, 0)]),
                (far[h], [(0, k) for k in far_at]),
                (far_one[h], [(one, k) for k in far_at]),
                (far_two[h], [(p, k) for p in (two, 3) for k in far_at]),
            ]
        )
    return halves


def project_kernel(place_ref, *refs, groups, rows, steps):
    first, second = refs[:groups], refs[groups : 2 * groups]
    map_ref, own_ref, send_ref, totals, ordered = refs[2 * groups :]
    step = pl.program_id(0)
    blocks = totals.shape[1] // rows

    def add(parts, half):
        left = jnp.concatenate([part[...] for part in parts], axis=0)
        term = lax.dot_general(
            left, map_ref[...], (((1,), (1,)), ((), ())), preferred_element_type=F32
        )

        @pl.when(step == half * steps)
        def _():
            totals[half] = term

        @pl.when(step != half * steps)
        def _():
            totals[half] += term

    @pl.when(step < steps)
    def _():
        add(first, 0)

    @pl.when(step >= steps)
    def _():
        add(second, 1)

    @pl.when(step == 2 * steps - 1)
    def _():
        half_rows = totals.shape[1] // 2
        for block in range(blocks):
            target = pl.multiple_of(place_ref[block] * rows, rows)
            ordered[pl.ds(target, rows), :] = totals[0, block * rows : (block + 1) * rows, :]
        for block in range(blocks):
            target = pl.multiple_of(place_ref[blocks + block] * rows, rows)
            ordered[pl.ds(target, rows), :] += totals[1, block * rows : (block + 1) * rows, :]
        side = place_ref[2 * blocks]
        own_ref[...] = ordered[pl.ds(pl.multiple_of(side * half_rows, half_rows), half_rows), :]
        send_ref[...] = ordered[
            pl.ds(pl.multiple_of((1 - side) * half_rows, half_rows), half_rows), :
        ].astype(BF16)


def project(first, second, columns_map, place, rows):
    groups = len(first)
    width, depth = columns_map.shape
    total_rows = sum(part.shape[0] for part in first)
    steps = 4
    tile = depth // (2 * steps)
    return pl.pallas_call(
        functools.partial(project_kernel, groups=groups, rows=rows, steps=steps),
        grid_spec=pltpu.PrefetchScalarGridSpec(
            num_scalar_prefetch=1,
            grid=(2 * steps,),
            in_specs=[
                pl.BlockSpec((p.shape[0], tile), lambda k, place: (0, jnp.minimum(k, steps - 1)))
                for p in first
            ]
            + [
                pl.BlockSpec((p.shape[0], tile), lambda k, place: (0, jnp.maximum(k - steps, 0)))
                for p in second
            ]
            + [pl.BlockSpec((width, tile), lambda k, place: (0, k))],
            out_specs=[pl.BlockSpec((total_rows // 2, width), lambda k, place: (0, 0))] * 2,
            scratch_shapes=[
                pltpu.VMEM((2, total_rows, width), F32),
                pltpu.VMEM((total_rows, width), F32),
            ],
        ),
        out_shape=[
            jax.ShapeDtypeStruct((total_rows // 2, width), F32),
            jax.ShapeDtypeStruct((total_rows // 2, width), BF16),
        ],
        compiler_params=pltpu.CompilerParams(vmem_limit_bytes=24 * 2**20),
        cost_estimate=pl.CostEstimate(
            flops=2 * total_rows * depth * width,
            bytes_accessed=2 * (total_rows * depth + depth * width),
            transcendentals=0,
        ),
    )(place, *first, *second, columns_map)


def expert_kernel(place_ref, *refs, sources, plan, last, line, model_width, owner_rows):
    count = len(sources)
    own, other = refs[:count], refs[count : 2 * count]
    refs = refs[2 * count :]
    if last:
        gain_ref, in_ref, sums_in, squares_in, rows_in, gate_ref = refs[:6]
        out_ref, rows_out, weights, wide, total, squares, arrived = refs[6:]
    else:
        gain_ref, in_ref, total, squares, rows_out, weights, wide, arrived = refs
    blocks = sum(steps for steps, _, _ in plan)
    offsets = []
    for steps, _, _ in plan:
        offsets.append(sum(p[0] for p in plan[: len(offsets)]))

    def load(at):
        return pltpu.make_async_copy(in_ref.at[place_ref[at]], weights.at[at], arrived.at[at])

    def start(at, carry):
        load(at).start()
        return carry

    lax.fori_loop(0, blocks, start, 0)
    if last:
        total[...] = sums_in[...]
        squares[...] = squares_in[...]
        rows_out[...] = rows_in[...]
    else:
        total[...] = jnp.zeros_like(total)
        squares[...] = jnp.zeros_like(squares)
        rows_out[...] = jnp.zeros_like(rows_out)
    half = wide.shape[0] // 4
    owner = place_ref[blocks]

    def work(at, first, second):
        source, index = first
        wide[0:half] = own[source][index].astype(F32)
        wide[2 * half : 3 * half] = other[source][index].astype(F32)
        source, index = second
        wide[half : 2 * half] = own[source][index].astype(F32)
        wide[3 * half : 4 * half] = other[source][index].astype(F32)
        chip = place_ref[at]
        rows_out[chip] = wide[pl.ds(pl.multiple_of(owner * owner_rows, owner_rows), owner_rows), :]
        values = wide[...]
        squares[...] += jnp.sum(values * values, axis=1, keepdims=True)
        scaled = (values * gain_ref[chip].astype(F32)).astype(BF16)
        load(at).wait()
        total[...] += jnp.dot(scaled, weights[at], preferred_element_type=F32)

    for offset, (steps, (first, first_at), (second, second_at)) in zip(offsets, plan):
        if steps == 1:
            work(offset, (first, first_at), (second, second_at))
        else:

            def step(k, carry):
                work(offset + k, (first, first_at + k), (second, second_at + k))
                return carry

            lax.fori_loop(0, steps, step, 0)

    if last:
        units = total.shape[1] // 2
        level = lax.rsqrt(squares[...] / model_width + 1e-06)
        gate_part = total[:, :units] * level
        up_part = total[:, units:] * level
        raised = gate_part / (1.0 + jnp.exp(-gate_part))
        total[:, :units] = raised * up_part * gate_ref[...]
        chips = rows_out.shape[0]
        side_rows = total.shape[0] // 2
        for first_row in (0, side_rows):
            for pair in range(chips // 2):
                pieces = [
                    total[
                        pl.ds(
                            pl.multiple_of(
                                first_row + place_ref[blocks + 1 + 2 * pair + j] * owner_rows,
                                owner_rows,
                            ),
                            owner_rows,
                        ),
                        :units,
                    ]
                    for j in (0, 1)
                ]
                row = first_row + 2 * pair * owner_rows
                out_ref[row : row + 2 * owner_rows, :] = jnp.concatenate(pieces).astype(BF16)


def expert_rows(sources, other_sources, plan, gain, weights, place, owner_rows, carried=None, gates=None):
    last = carried is not None
    chips, columns, double = weights.shape
    half = sources[0].shape[1]
    tokens = 4 * half
    blocks = sum(steps for steps, _, _ in plan)
    model_width = chips * columns
    whole = pl.BlockSpec(memory_space=pltpu.VMEM)
    operands = [*sources, *other_sources, gain]
    extra = [*carried, gates] if last else []
    sums = [
        jax.ShapeDtypeStruct((tokens, double), F32),
        jax.ShapeDtypeStruct((tokens, 1), F32),
        jax.ShapeDtypeStruct((chips, owner_rows, columns), F32),
    ]
    scratch = [
        pltpu.VMEM((blocks, columns, double), BF16),
        pltpu.VMEM((tokens, columns), F32),
    ]
    if last:
        out_shape = [jax.ShapeDtypeStruct((tokens, double // 2), BF16), sums[2]]
        scratch += [pltpu.VMEM((tokens, double), F32), pltpu.VMEM((tokens, 1), F32)]
    else:
        out_shape = sums
    scratch += [pltpu.SemaphoreType.DMA((blocks,))]
    return pl.pallas_call(
        functools.partial(
            expert_kernel,
            sources=sources,
            plan=plan,
            last=last,
            line=0,
            model_width=float(model_width),
            owner_rows=owner_rows,
        ),
        in_specs=[pl.BlockSpec(memory_space=pltpu.SMEM)]
        + [whole] * len(operands)
        + [pl.BlockSpec(memory_space=pl.ANY)]
        + [whole] * len(extra),
        out_specs=[whole] * len(out_shape),
        out_shape=out_shape,
        scratch_shapes=scratch,
        compiler_params=pltpu.CompilerParams(
            vmem_limit_bytes=budget(*operands, *extra, weights, *out_shape, *sums)
        ),
        cost_estimate=pl.CostEstimate(
            flops=2 * tokens * blocks * columns * double,
            bytes_accessed=2 * blocks * columns * (double + tokens),
            transcendentals=tokens * double,
        ),
    )(place, *operands, weights, *extra)


def down_kernel(rows_ref, down_ref, *outs, order):
    rows = rows_ref.shape[0] // 8
    product = jnp.dot(rows_ref[...], down_ref[...], preferred_element_type=F32).astype(BF16)
    for at, groups in enumerate(order):
        for j, group in enumerate(groups):
            outs[at][j * rows : (j + 1) * rows, :] = product[group * rows : (group + 1) * rows, :]


def lower(rows, down, half, order):
    units, width = down.shape
    steps = 4
    tile = width // (2 * steps)
    count = rows.shape[0] // 4
    return pl.pallas_call(
        functools.partial(down_kernel, order=order),
        grid=(steps,),
        in_specs=[
            pl.BlockSpec(rows.shape, lambda k: (0, 0)),
            pl.BlockSpec((units, tile), lambda k: (0, half * steps + k)),
        ],
        out_specs=[pl.BlockSpec((count, tile), lambda k: (0, k))] * 4,
        out_shape=[jax.ShapeDtypeStruct((count, width // 2), BF16)] * 4,
        compiler_params=pltpu.CompilerParams(vmem_limit_bytes=24 * 2**20),
        cost_estimate=pl.CostEstimate(
            flops=rows.shape[0] * units * width,
            bytes_accessed=(units + rows.shape[0]) * width,
            transcendentals=0,
        ),
    )(rows, down)


def on_device(
    queries,
    latent_cache,
    lengths,
    value_lift,
    output_map,
    residual,
    norm_gain,
    expert_ids,
    gate_values,
    expert_in,
    expert_down,
):
    request_count = queries.shape[0]
    latent_width = value_lift.shape[1]
    half_heads = value_lift.shape[0]
    value_width = value_lift.shape[2]
    half_slots = latent_cache.shape[1]
    token_count, model_width = residual.shape
    chips = lax.axis_size("dev")
    plane = 4
    line = chips // plane
    columns = output_map.shape[1]
    experts = chips // 2
    units = expert_down.shape[1]
    side = lax.axis_index("side")
    chip = lax.axis_index("dev")
    line_at, plane_at = chip // plane, chip % plane
    half_tokens = token_count * chips

    def line_hop(value, k):
        return hop(value, "dev", chips, k * plane)

    def plane_hop(value, k):
        return hop(value, "dev", chips, k)

    def swap(value):
        return hop(value, "side", 2, 1)

    def placed(offsets):
        return [(line_at ^ k_line) * plane + (plane_at ^ k_plane) for k_plane, k_line in offsets]

    chosen = expert_ids[:, :, None] == jnp.arange(experts, dtype=jnp.int32)[None, None, :]
    weights = jnp.sum(jnp.where(chosen, gate_values[:, :, None], 0.0), axis=1)
    weights_high = lax.reduce_precision(weights, 8, 7)
    weight_terms = jnp.concatenate([weights_high, weights - weights_high], axis=1).astype(BF16)
    weight_width = -(-token_count * 2 * experts // (request_count * 128)) * 128
    weight_block = jnp.pad(
        weight_terms.reshape(-1), (0, request_count * weight_width - weight_terms.size)
    ).reshape(request_count, weight_width)

    residual_blocks = residual.reshape(token_count, chips, columns).swapaxes(0, 1)
    residual_columns = lax.all_to_all(
        residual_blocks, "dev", split_axis=0, concat_axis=0, tiled=True
    ).reshape(half_tokens, columns)

    score_scale = QKD ** (-0.5)
    scores = (
        jnp.einsum("rhc,rpc->rhp", queries, latent_cache, preferred_element_type=F32) * score_scale
    )
    positions = side * half_slots + jnp.arange(half_slots, dtype=jnp.int32)
    usable = (positions[None, :] < lengths[:, None])[:, None, :]
    masked = jnp.where(usable, scores, -1e30)
    local_top = jnp.max(masked, axis=2)
    raised = jnp.where(usable, jnp.exp(masked - local_top[:, :, None]), 0.0)
    local_total = jnp.sum(raised, axis=2)
    local_latent = jnp.einsum(
        "rhp,rpc->rhc",
        raised.astype(BF16),
        latent_cache[:, :, :latent_width],
        preferred_element_type=F32,
    )
    local_latent = (local_latent / jnp.maximum(local_total, 1e-30)[:, :, None]).astype(BF16)

    def heads_of(value, which):
        return lax.dynamic_slice_in_dim(value, which * half_heads, half_heads, 1)

    stats = jnp.stack([local_top, local_total], axis=2)
    other_latent = swap(heads_of(local_latent, 1 - side))
    other_stats = swap(heads_of(stats, 1 - side))
    own_latent = heads_of(local_latent, side)
    own_stats = heads_of(stats, side)
    top = jnp.maximum(own_stats[:, :, 0], other_stats[:, :, 0])
    own_share = own_stats[:, :, 1] * jnp.exp(own_stats[:, :, 0] - top)
    other_share = other_stats[:, :, 1] * jnp.exp(other_stats[:, :, 0] - top)
    share_sum = own_share + other_share
    latent_out = (
        own_latent.astype(F32) * (own_share / share_sum)[:, :, None]
        + other_latent.astype(F32) * (other_share / share_sum)[:, :, None]
    ).astype(BF16)
    head_values = jnp.einsum("rhc,hcv->rhv", latent_out, value_lift, preferred_element_type=F32)
    head_values = head_values.astype(BF16).reshape(request_count, half_heads * value_width)

    half_depth = half_heads * value_width // 2
    first, second = gather(
        jnp.concatenate([head_values[:, :half_depth], weight_block], axis=1),
        jnp.concatenate([head_values[:, half_depth:], jnp.zeros_like(weight_block)], axis=1),
        line,
        line_hop,
        plane_hop,
    )
    place = jnp.stack(
        [at for half in (first, second) for _, offsets in half for at in placed(offsets)] + [side]
    ).astype(jnp.int32)
    first_parts, second_parts = [
        [part.reshape(-1, part.shape[-1]) for part, _ in half] for half in (first, second)
    ]
    own_columns, sent_columns = project(
        first_parts, second_parts, output_map.T, place, request_count
    )
    attention = own_columns + swap(sent_columns).astype(F32)
    hidden = (residual_columns.astype(F32) + attention).astype(BF16)

    gathered = jnp.concatenate([part[:, :, half_depth:] for part, _ in first])
    gathered = gathered.reshape(chips, -1)[:, : token_count * 2 * experts]
    gathered = gathered.reshape(chips, token_count, 2, experts).astype(F32)
    gathered = lax.dynamic_index_in_dim(gathered, chip // 2, 3, keepdims=False).sum(axis=2)
    order = [offsets for _, part_offsets in first for offsets in part_offsets]
    spots = jnp.stack(placed(order))
    own_gates = jnp.zeros((chips, token_count), F32).at[spots].set(gathered).reshape(-1, 1)
    gates = jnp.concatenate([own_gates, swap(own_gates)])

    half_rows = half_tokens // 2
    first, second = gather(hidden[:half_rows], hidden[half_rows:], line, line_hop, plane_hop)
    (near_a, near_one_a, near_two_a, far_a, far_one_a, far_two_a) = [part for part, _ in first]
    (near_b, near_one_b, near_two_b, far_b, far_one_b, far_two_b) = [part for part, _ in second]
    early = [near_a, near_b, near_one_a, near_one_b, near_two_a, near_two_b, far_a, far_b]
    late = [far_one_a, far_one_b, far_two_a, far_two_b]
    steps = line - 1
    early_plan = [
        (1, (0, 0), (1, 0)),
        (1, (2, 0), (5, 0)),
        (1, (4, 0), (3, 0)),
        (1, (4, 1), (5, 1)),
        (steps, (6, 0), (7, 0)),
    ]
    late_plan = [
        (steps, (0, 0), (3, 0)),
        (steps, (2, 0), (1, 0)),
        (steps, (2, steps), (3, steps)),
    ]
    early_at = [(0, 0), (1, 0), (2, 0), (3, 0)] + [(0, k) for k in range(1, line)]
    late_at = [(p, k) for p in (1, 2, 3) for k in range(1, line)]
    out_at = [(p, k) for p in range(plane) for k in range(line)]
    early_place = jnp.stack(placed(early_at) + [chip]).astype(jnp.int32)
    late_place = jnp.stack(placed(late_at) + [chip] + placed(out_at)).astype(jnp.int32)
    gain = norm_gain.reshape(chips, 1, columns)
    in_rows = expert_in.reshape(chips, columns, 2 * units)
    down = expert_down[0]
    carried = expert_rows(
        early, [swap(part) for part in early], early_plan, gain, in_rows, early_place, token_count
    )
    activated, own_hidden = expert_rows(
        late,
        [swap(part) for part in late],
        late_plan,
        gain,
        in_rows,
        late_place,
        token_count,
        carried,
        gates,
    )

    sums = []
    for half in (0, 1):
        one, two = 1 + half, 2 - half
        kept, moved = [0, two], [one, 3]
        own_moved, own_kept, other_moved, other_kept = lower(
            activated, down, half, [moved, kept, [4 + g for g in moved], [4 + g for g in kept]]
        )
        moved_sum = (own_moved.astype(F32) + swap(other_moved).astype(F32)).astype(BF16)
        kept_sum = own_kept.astype(F32) + swap(other_kept).astype(F32)
        kept_sum = kept_sum + plane_hop(moved_sum, one).astype(F32)
        rows = kept_sum.shape[0] // 2
        arrived = plane_hop(kept_sum[rows:].astype(BF16), two).astype(F32)
        sums.append(kept_sum[:rows] + arrived)
    plane_sum = jnp.concatenate(sums, axis=1).reshape(line, token_count, model_width)
    routed_sum = plane_sum[0]
    for k in range(1, line):
        routed_sum = routed_sum + line_hop(plane_sum[k].astype(BF16), k).astype(F32)
    own_hidden = own_hidden.swapaxes(0, 1).reshape(token_count, model_width)
    return (own_hidden + routed_sum).astype(BF16)


def solution(mesh):
    in_specs = (
        P("dev", None, None),
        P("dev", "side", None),
        P("dev"),
        P("side", None, None),
        P("side", "dev"),
        P(("side", "dev"), None),
        P(),
        P(("side", "dev"), None),
        P(("side", "dev"), None),
        P("dev", None, None, "side"),
        P("dev", "side", None),
    )
    out_specs = P(("side", "dev"), None)
    return jax.shard_map(
        on_device, mesh=mesh, in_specs=in_specs, out_specs=out_specs, check_vma=False
    )
```

time: 265 us -> 199 us (0.75)
  blocking collectives: 67.1 us -> 0 us
  starting transfers between devices: 31.5 us -> 51.8 us
  waiting for transfers between devices: 82.5 us -> 68.9 us
  local copies, waits for them, and re-layouts: 37.7 us -> 32.4 us
  Pallas kernels: 27.5 us -> 24.2 us
    all_gather x1 -> x0, blocking collectives: 67.1 us -> none  [on_device(): all_weights = lax.all_gather(weights, ('side', 'dev'), axis=0, tiled=True)]
    ppermute x26 -> x49, starting transfers between devices: 25.7 us -> 46.9 us  [hop(): return lax.ppermute(value, axis, [(i, i ^ mask) for i in range(size)])]
    ppermute x26 -> x49, waiting for transfers between devices: 82.5 us -> 68.9 us  [hop(): return lax.ppermute(value, axis, [(i, i ^ mask) for i in range(size)])]
    pallas_call x2 -> x4, Pallas kernels: 23.2 us -> 17.8 us  [the longest x2 14.6 us: expert_rows(): pl.pallas_call(functools.partial(expert_kernel, sources=sources, plan=pla...]
    unnamed x23 -> x49, local copies, waits for them, and re-layouts: 20 us -> 15 us
    convert_element_type x4 -> x3, other arithmetic: 4.41 us -> 0.92 us  [the longest x1 0.71 us: on_device(): return (own_hidden + routed_sum).astype(BF16)]
    reshape x1 -> x5, local copies, waits for them, and re-layouts: 12.4 us -> 13.8 us  [the longest x1 12.5 us: on_device(): in_rows = expert_in.reshape(chips, columns, 2 * units)]
  transfers between devices with their start and end apart: 27 -> 50, of which waited for: 16 -> 25; matrix products, arithmetic and copies ran while one was open for 9% -> 13% of each run, Pallas kernels for 5% -> 7%
where the time goes in v2:
time: 199 us; the launch traced here: 198 us
  waiting for transfers between devices  68.9 us (35%)
  starting transfers between devices  51.8 us (26%)
  local copies, waits for them, and re-layouts  32.4 us (16%)
  Pallas kernels  24.2 us (12%)
  matrix products  12.5 us (6%)
  other arithmetic  7.07 us (4%)
    ppermute x49, waiting for transfers between devices, hop(): return lax.ppermute(value, axis, [(i, i ^ mask) for i in range(size)])  68.9 us
    ppermute x49, starting transfers between devices, hop(): return lax.ppermute(value, axis, [(i, i ^ mask) for i in range(size)])  46.9 us
    unnamed x49, local copies, waits for them, and re-layouts  15 us
    pallas_call x2, Pallas kernels, expert_rows(): pl.pallas_call(functools.partial(expert_kernel, sources=sources, plan=pla...  14.6 us
    reshape x1, local copies, waits for them, and re-layouts, on_device(): in_rows = expert_in.reshape(chips, columns, 2 * units)  12.5 us
    pallas_call x1, Pallas kernels, project(): pl.pallas_call(functools.partial(project_kernel, groups=groups, rows=rows...  6.39 us
    dot_general x1, matrix products, on_device(): jnp.einsum('rhp,rpc->rhc', raised.astype(BF16), latent_cache[:, :, :laten...  4.94 us
    all_to_all x1, starting transfers between devices, on_device(): lax.all_to_all(residual_blocks, 'dev', split_axis=0, concat_axis=0, tiled...  4.93 us
  transfers between devices with their start and end apart: 50, of which 25 were waited for; matrix products, arithmetic and copies ran while one was open for 13% of the time, Pallas kernels for 7%

profile of v2, /device:TPU:0, one launch (start us, length us, event | category | flops | bytes accessed | tf_op | source)
XLA Modules:
  0.0 197.5 jit_solution(10167875348463358516)
XLA Ops:
  1.3 4.5 %fusion.44 = (f32[16,64]{1,0:T(8,128)S(1)}, f32[16,64,384]{2,1,0:T(8,128)S(1)}) fusion(bf16[16,64,576]{2,1,0:T(8,128)(2,1)S(1)} %copy-done, bf16[16,384,576]{1,2,0:T(8,128)(2,1)} %param.12, pred[16,384]{1,0:T(8,128)(4,1)S(1)} %broadcast_compare_fusion), kind=kOutput, calls=%fused_computation.106 | convolution fusion | flops 454163456 | bytes 9840640 | tf_op jit(solution)/shard_map/rhc,rpc->rhp/dot_general | solution.py:366
  7.0 4.9 %divide_convert_fusion = bf16[16,64,512]{2,1,0:T(8,128)(2,1)S(1)} fusion(f32[16,64]{1,0:T(8,128)S(1)} %broadcast_maximum_fusion, bf16[16,384,576]{1,2,0:T(8,128)(2,1)} %param.12, f32[16,64,384]{2,1,0:T(8,128)S(1)} %get-tuple-element.71, f32[16,64]{1,0:T(8,128)S(1)} %get-tuple-element.70, pred[16,384]{1,0:T(8,128)(4,1)S(1)} %broadcast_compare_fusion), kind=kOutput, calls=%fused_computation.3 | convolution fusion | flops 404881408 | bytes 8927232 | tf_op jit(solution)/shard_map/rhp,rpc->rhc/dot_general | solution.py:374
  16.3 3.1 %fusion.4 = bf16[32,2,8,128]{3,2,1,0:T(8,128)(2,1)S(1)} fusion(bf16[32,512,128]{2,1,0:T(8,128)(2,1)} %param.14, bf16[16,32,512]{2,1,0:T(8,128)(2,1)S(1)} %add_convert_fusion), kind=kOutput, calls=%fused_computation.9 | convolution fusion | flops 67174400 | bytes 4849664 | tf_op jit(solution)/shard_map/rhc,hcv->rhv/dot_general | solution.py:398
  19.4 2.7 %collective-permute-start.2 = (bf16[1,16,2176]{2,1,0:T(8,128)(2,1)S(1)}, bf16[1,16,2176]{2,1,0:T(8,128)(2,1)S(1)}, u32[]{:S(2)}, u32[]{:S(2)}) collective-permute-start(bf16[1,16,2176]{2,1,0:T(8,128)(2,1)S(1)} %get-tuple-element.57), channel_id=1, source_target_pairs={{0,1},{1,0},{2,3},{3,2},{4,5},{5,4},{6,7},{7,6},{8,9},{9,8},{10,11... | collective-permute-start | bytes 208904 | tf_op jit(solution)/shard_map/ppermute | solution.py:16
  29.1 4.9 %all-to-all-start = ((bf16[16,8,448]{2,1,0:T(8,128)(2,1)}), bf16[16,8,448]{2,1,0:T(8,128)(2,1)S(1)}, u32[]{:S(2)}, u32[]{:S(2)}) async-start(bf16[16,8,448]{2,1,0:T(8,128)(2,1)} %bitcast.82), calls=%async_computation | async-start | bytes 262144 | tf_op jit(solution)/shard_map/all_to_all | solution.py:360
  34.3 2.8 %collective-permute-start.5 = (bf16[2,16,2176]{2,1,0:T(8,128)(2,1)S(1)}, bf16[2,16,2176]{2,1,0:T(8,128)(2,1)S(1)}, u32[]{:S(2)}, u32[]{:S(2)}) collective-permute-start(bf16[2,16,2176]{2,1,0:T(8,128)(2,1)S(1)} %get-tuple-element.55), channel_id=1, source_target_pairs={{0,8},{1,9},{2,10},{3,11},{4,12},{5,13},{6,14},{7,15},{8,0},{9,1},... | collective-permute-start | bytes 417800 | tf_op jit(solution)/shard_map/ppermute | solution.py:16
  38.6 10.7 %collective-permute-done.5 = bf16[2,16,2176]{2,1,0:T(8,128)(2,1)S(1)} collective-permute-done((bf16[2,16,2176]{2,1,0:T(8,128)(2,1)S(1)}, bf16[2,16,2176]{2,1,0:T(8,128)(2,1)S(1)}, u32[]{:S(2)}, u32[]{:S(2)}) %collective-permute-start.5) | collective-permute-done | bytes 139296 | tf_op jit(solution)/shard_map/ppermute | solution.py:16
  52.5 2.8 %collective-permute-done.7 = bf16[3,16,2176]{2,1,0:T(8,128)(2,1)S(1)} collective-permute-done((bf16[3,16,2176]{2,1,0:T(8,128)(2,1)S(1)}, bf16[3,16,2176]{2,1,0:T(8,128)(2,1)S(1)}, u32[]{:S(2)}, u32[]{:S(2)}) %collective-permute-start.7) | collective-permute-done | bytes 208928 | tf_op jit(solution)/shard_map/ppermute | solution.py:16
  56.9 2.2 %collective-permute-done.11 = bf16[3,16,2176]{2,1,0:T(8,128)(2,1)S(1)} collective-permute-done((bf16[3,16,2176]{2,1,0:T(8,128)(2,1)S(1)}, bf16[3,16,2176]{2,1,0:T(8,128)(2,1)S(1)}, u32[]{:S(2)}, u32[]{:S(2)}) %collective-permute-start.11) | collective-permute-done | bytes 208928 | tf_op jit(solution)/shard_map/ppermute | solution.py:16
  62.7 5.8 %collective-permute-done.3 = bf16[2,16,2176]{2,1,0:T(8,128)(2,1)S(1)} collective-permute-done((bf16[2,16,2176]{2,1,0:T(8,128)(2,1)S(1)}, bf16[2,16,2176]{2,1,0:T(8,128)(2,1)S(1)}, u32[]{:S(2)}, u32[]{:S(2)}) %collective-permute-start.3) | collective-permute-done | bytes 139296 | tf_op jit(solution)/shard_map/ppermute | solution.py:16
  68.8 2.0 %copy-done.4 = bf16[4096,448]{0,1:T(8,128)(2,1)S(1)} copy-done((bf16[4096,448]{0,1:T(8,128)(2,1)S(1)}, bf16[4096,448]{0,1:T(8,128)(2,1)}, u32[]{:S(2)}) %copy-start.4) | copy-done | bytes 3670040
  70.8 6.4 %shard_map.109 = (f32[128,448]{1,0:T(8,128)S(1)}, bf16[128,448]{1,0:T(8,128)(2,1)S(1)}) custom-call(s32[33]{0:T(128)S(1)} %stack.215.place_ref, bf16[16,2176]{1,0:T(8,128)(2,1)S(1)} %get-tuple-element.58.refs_0_, bf16[16,2176]{1,0:T(8,128)(2,1)S(1)} %bitcast.92, bf16[32,2176]{1,0:T(8,128)(2,1)S(1)} %bitcast.95, bf16[48,2176]{1,0:T(8,128)(2,1)S(1)} %bitcast.87, ...), custom_call_target="tpu_custom_call" | custom-call | flops 939524096 | bytes 5767168 | tf_op jit(solution)/shard_map/pallas_call | solution.py:104
  80.8 2.2 %collective-permute-done.25.refs_2_ = bf16[1,64,448]{2,1,0:T(8,128)(2,1)S(1)} collective-permute-done((bf16[1,64,448]{2,1,0:T(8,128)(2,1)S(1)}, bf16[1,64,448]{2,1,0:T(8,128)(2,1)S(1)}, u32[]{:S(2)}, u32[]{:S(2)}) %collective-permute-start.25) | collective-permute-done | bytes 57376 | tf_op jit(solution)/shard_map/ppermute | solution.py:16
  84.4 3.2 %collective-permute-start.14 = (bf16[2,64,448]{2,1,0:T(8,128)(2,1)S(1)}, bf16[2,64,448]{2,1,0:T(8,128)(2,1)S(1)}, u32[]{:S(2)}, u32[]{:S(2)}) collective-permute-start(bf16[2,64,448]{2,1,0:T(8,128)(2,1)S(1)} %get-tuple-element.60), channel_id=1, source_target_pairs={{0,4},{1,5},{2,6},{3,7},{4,0},{5,1},{6,2},{7,3},{8,12},{9,13},{10,... | collective-permute-start | bytes 344072 | tf_op jit(solution)/shard_map/ppermute | solution.py:16
  87.6 2.3 %collective-permute-start.15 = (bf16[2,64,448]{2,1,0:T(8,128)(2,1)S(1)}, bf16[2,64,448]{2,1,0:T(8,128)(2,1)S(1)}, u32[]{:S(2)}, u32[]{:S(2)}) collective-permute-start(bf16[2,64,448]{2,1,0:T(8,128)(2,1)S(1)} %get-tuple-element.60), channel_id=1, source_target_pairs={{0,8},{1,9},{2,10},{3,11},{4,12},{5,13},{6,14},{7,15},{8,0},{9,1},... | collective-permute-start | bytes 344072 | tf_op jit(solution)/shard_map/ppermute | solution.py:16
  92.0 8.5 %collective-permute-done.15 = bf16[2,64,448]{2,1,0:T(8,128)(2,1)S(1)} collective-permute-done((bf16[2,64,448]{2,1,0:T(8,128)(2,1)S(1)}, bf16[2,64,448]{2,1,0:T(8,128)(2,1)S(1)}, u32[]{:S(2)}, u32[]{:S(2)}) %collective-permute-start.15) | collective-permute-done | bytes 114720 | tf_op jit(solution)/shard_map/ppermute | solution.py:16
  103.7 2.8 %collective-permute-done.18.refs_1_ = bf16[3,64,448]{2,1,0:T(8,128)(2,1)S(1)} collective-permute-done((bf16[3,64,448]{2,1,0:T(8,128)(2,1)S(1)}, bf16[3,64,448]{2,1,0:T(8,128)(2,1)S(1)}, u32[]{:S(2)}, u32[]{:S(2)}) %collective-permute-start.18) | collective-permute-done | bytes 172064 | tf_op jit(solution)/shard_map/ppermute | solution.py:16
  123.0 12.5 %reshape.736.refs_17_.refs_9_ = bf16[16,448,512]{2,1,0:T(8,128)(2,1)} reshape(bf16[1,7168,2,256]{3,2,1,0:T(2,128)(2,1)} %param.20) | data formatting | bytes 14680064 | tf_op jit(solution)/shard_map/reshape | solution.py:455
  136.4 3.1 %copy-done.1 = bf16[16,448,512]{2,1,0:T(8,128)(2,1)S(1)} copy-done((bf16[16,448,512]{2,1,0:T(8,128)(2,1)S(1)}, bf16[16,448,512]{2,1,0:T(8,128)(2,1)}, u32[]{:S(2)}) %copy-start.1) | copy-done | bytes 7340056
  144.6 6.0 %shard_map.110 = (f32[256,512]{1,0:T(8,128)S(1)}, f32[256,1]{1,0:T(8,128)S(1)}, f32[16,8,448]{2,1,0:T(8,128)S(1)}) custom-call(s32[8]{0:T(128)S(1)} %stack.226.place_ref, bf16[1,64,448]{2,1,0:T(8,128)(2,1)S(1)} %get-tuple-element.51.refs_0_, bf16[1,64,448]{2,1,0:T(8,128)(2,1)S(1)} %get-tuple-element.50.refs_1_, ...), custom_call_target="tpu_custom_call" | custom-call | flops 822083584 | bytes 4816896 | tf_op jit(solution)/shard_map/pallas_call | solution.py:249
  150.7 8.6 %shard_map.111 = (bf16[256,256]{1,0:T(8,128)(2,1)S(1)}, f32[16,8,448]{2,1,0:T(8,128)S(1)}) custom-call(s32[26]{0:T(128)S(1)} %stack.213.place_ref, bf16[3,64,448]{2,1,0:T(8,128)(2,1)S(1)} %collective-permute-done.17.refs_0_, bf16[3,64,448]{2,1,0:T(8,128)(2,1)S(1)} %collective-permute-done.18.refs_1_, bf16[6,64,448]{2,1,0:T(8,128)(2,1)} %collective-permute-done.19.refs_2_, ...), custom_call_target="tpu_custom_call" | custom-call | flops 1056964608 | bytes 6193152 | tf_op jit(solution)/shard_map/pallas_call | solution.py:249
  166.2 10.1 %collective-permute-done.44 = bf16[64,3584]{1,0:T(8,128)(2,1)S(1)} collective-permute-done((bf16[64,3584]{1,0:T(8,128)(2,1)S(1)}, bf16[64,3584]{1,0:T(8,128)(2,1)S(1)}, u32[]{:S(2)}, u32[]{:S(2)}) %collective-permute-start.44) | collective-permute-done | bytes 458784 | tf_op jit(solution)/shard_map/ppermute | solution.py:16
  179.1 4.3 %collective-permute-done.45 = bf16[32,3584]{1,0:T(8,128)(2,1)S(1)} collective-permute-done((bf16[32,3584]{1,0:T(8,128)(2,1)S(1)}, bf16[32,3584]{1,0:T(8,128)(2,1)S(1)}, u32[]{:S(2)}, u32[]{:S(2)}) %collective-permute-start.45) | collective-permute-done | bytes 229408 | tf_op jit(solution)/shard_map/ppermute | solution.py:16
  190.4 6.4 %collective-permute-done.47 = bf16[8,7168]{1,0:T(8,128)(2,1)S(1)} collective-permute-done((bf16[8,7168]{1,0:T(8,128)(2,1)S(1)}, bf16[8,7168]{1,0:T(8,128)(2,1)S(1)}, u32[]{:S(2)}, u32[]{:S(2)}) %collective-permute-start.47) | collective-permute-done | bytes 114720 | tf_op jit(solution)/shard_map/ppermute | solution.py:16
  (199 shorter events, 73.9 us)
Async XLA Ops:
  26.6 12.1 %collective-permute-start.4 = (bf16[2,16,2176]{2,1,0:T(8,128)(2,1)S(1)}, bf16[2,16,2176]{2,1,0:T(8,128)(2,1)S(1)}, u32[]{:S(2)}, u32[]{:S(2)}) collective-permute-start(bf16[2,16,2176]{2,1,0:T(8,128)(2,1)S(1)} %get-tuple-element.55), channel_id=1, source_target_pairs={{0,4},{1,5},{2,6},{3,7},{4,0},{5,1},{6,2},{7,3},{8,12},{9,13},{10,... | collective-permute-start | bytes 417800 | tf_op jit(solution)/shard_map/ppermute | solution.py:16
  29.1 48.2 %all-to-all-start = ((bf16[16,8,448]{2,1,0:T(8,128)(2,1)}), bf16[16,8,448]{2,1,0:T(8,128)(2,1)S(1)}, u32[]{:S(2)}, u32[]{:S(2)}) async-start(bf16[16,8,448]{2,1,0:T(8,128)(2,1)} %bitcast.82), calls=%async_computation | async-start | bytes 262144 | tf_op jit(solution)/shard_map/all_to_all | solution.py:360
  34.3 15.0 %collective-permute-start.5 = (bf16[2,16,2176]{2,1,0:T(8,128)(2,1)S(1)}, bf16[2,16,2176]{2,1,0:T(8,128)(2,1)S(1)}, u32[]{:S(2)}, u32[]{:S(2)}) collective-permute-start(bf16[2,16,2176]{2,1,0:T(8,128)(2,1)S(1)} %get-tuple-element.55), channel_id=1, source_target_pairs={{0,8},{1,9},{2,10},{3,11},{4,12},{5,13},{6,14},{7,15},{8,0},{9,1},... | collective-permute-start | bytes 417800 | tf_op jit(solution)/shard_map/ppermute | solution.py:16
  37.2 12.2 %collective-permute-start.6 = (bf16[2,16,2176]{2,1,0:T(8,128)(2,1)S(1)}, bf16[2,16,2176]{2,1,0:T(8,128)(2,1)S(1)}, u32[]{:S(2)}, u32[]{:S(2)}) collective-permute-start(bf16[2,16,2176]{2,1,0:T(8,128)(2,1)S(1)} %get-tuple-element.55), channel_id=1, source_target_pairs={{0,12},{1,13},{2,14},{3,15},{4,8},{5,9},{6,10},{7,11},{8,4},{9,5},... | collective-permute-start | bytes 417800 | tf_op jit(solution)/shard_map/ppermute | solution.py:16
  55.4 13.4 %collective-permute-start.8 = (bf16[6,16,2176]{2,1,0:T(8,128)(2,1)S(1)}, bf16[6,16,2176]{2,1,0:T(8,128)(2,1)S(1)}, u32[]{:S(2)}, u32[]{:S(2)}) collective-permute-start(bf16[6,16,2176]{2,1,0:T(8,128)(2,1)S(1)} %pad_maximum_fusion.1), channel_id=1, source_target_pairs={{0,2},{1,3},{2,0},{3,1},{4,6},{5,7},{6,4},{7,5},{8,10},{9,11},{10,... | collective-permute-start | bytes 1253384 | tf_op jit(solution)/shard_map/ppermute | solution.py:16
  59.2 9.6 %collective-permute-start.12 = (bf16[6,16,2176]{2,1,0:T(8,128)(2,1)S(1)}, bf16[6,16,2176]{2,1,0:T(8,128)(2,1)S(1)}, u32[]{:S(2)}, u32[]{:S(2)}) collective-permute-start(bf16[6,16,2176]{2,1,0:T(8,128)(2,1)S(1)} %pad_maximum_fusion.2), channel_id=1, source_target_pairs={{0,1},{1,0},{2,3},{3,2},{4,5},{5,4},{6,7},{7,6},{8,9},{9,8},{10,11... | collective-permute-start | bytes 1253384 | tf_op jit(solution)/shard_map/ppermute | solution.py:16
  59.3 9.3 %collective-permute-start.3 = (bf16[2,16,2176]{2,1,0:T(8,128)(2,1)S(1)}, bf16[2,16,2176]{2,1,0:T(8,128)(2,1)S(1)}, u32[]{:S(2)}, u32[]{:S(2)}) collective-permute-start(bf16[2,16,2176]{2,1,0:T(8,128)(2,1)S(1)} %get-tuple-element.56), channel_id=1, source_target_pairs={{0,2},{1,3},{2,0},{3,1},{4,6},{5,7},{6,4},{7,5},{8,10},{9,11},{10,... | collective-permute-start | bytes 417800 | tf_op jit(solution)/shard_map/ppermute | solution.py:16
  87.6 12.8 %collective-permute-start.15 = (bf16[2,64,448]{2,1,0:T(8,128)(2,1)S(1)}, bf16[2,64,448]{2,1,0:T(8,128)(2,1)S(1)}, u32[]{:S(2)}, u32[]{:S(2)}) collective-permute-start(bf16[2,64,448]{2,1,0:T(8,128)(2,1)S(1)} %get-tuple-element.60), channel_id=1, source_target_pairs={{0,8},{1,9},{2,10},{3,11},{4,12},{5,13},{6,14},{7,15},{8,0},{9,1},... | collective-permute-start | bytes 344072 | tf_op jit(solution)/shard_map/ppermute | solution.py:16
  90.0 10.5 %collective-permute-start.16 = (bf16[2,64,448]{2,1,0:T(8,128)(2,1)S(1)}, bf16[2,64,448]{2,1,0:T(8,128)(2,1)S(1)}, u32[]{:S(2)}, u32[]{:S(2)}) collective-permute-start(bf16[2,64,448]{2,1,0:T(8,128)(2,1)S(1)} %get-tuple-element.60), channel_id=1, source_target_pairs={{0,12},{1,13},{2,14},{3,15},{4,8},{5,9},{6,10},{7,11},{8,4},{9,5},... | collective-permute-start | bytes 344072 | tf_op jit(solution)/shard_map/ppermute | solution.py:16
  102.7 11.5 %collective-permute-start.29 = (bf16[1,64,448]{2,1,0:T(8,128)(2,1)S(1)}, bf16[1,64,448]{2,1,0:T(8,128)(2,1)S(1)}, u32[]{:S(2)}, u32[]{:S(2)}) collective-permute-start(bf16[1,64,448]{2,1,0:T(8,128)(2,1)S(1)} %get-tuple-element.51.refs_0_), channel_id=1, source_target_pairs={{0,16},{16,0},{1,17},{17,1},{2,18},{18,2},{3,19},{19,3},{4,20},{20... | collective-permute-start | bytes 172040 | tf_op jit(solution)/shard_map/ppermute | solution.py:16
  102.7 14.8 %collective-permute-start.27 = (bf16[2,64,448]{2,1,0:T(8,128)(2,1)}, bf16[2,64,448]{2,1,0:T(8,128)(2,1)S(1)}, u32[]{:S(2)}, u32[]{:S(2)}) collective-permute-start(bf16[2,64,448]{2,1,0:T(8,128)(2,1)} %get-tuple-element.61), channel_id=1, source_target_pairs={{0,2},{1,3},{2,0},{3,1},{4,6},{5,7},{6,4},{7,5},{8,10},{9,11},{10,... | collective-permute-start | bytes 344072 | tf_op jit(solution)/shard_map/ppermute | solution.py:16
  107.3 12.2 %collective-permute-start.20 = (bf16[6,64,448]{2,1,0:T(8,128)(2,1)}, bf16[6,64,448]{2,1,0:T(8,128)(2,1)S(1)}, u32[]{:S(2)}, u32[]{:S(2)}) collective-permute-start(bf16[6,64,448]{2,1,0:T(8,128)(2,1)} %pad_maximum_fusion.4), channel_id=1, source_target_pairs={{0,1},{1,0},{2,3},{3,2},{4,5},{5,4},{6,7},{7,6},{8,9},{9,8},{10,11... | collective-permute-start | bytes 1032200 | tf_op jit(solution)/shard_map/ppermute | solution.py:16
  108.9 10.9 %collective-permute-start.19 = (bf16[6,64,448]{2,1,0:T(8,128)(2,1)}, bf16[6,64,448]{2,1,0:T(8,128)(2,1)}, u32[]{:S(2)}, u32[]{:S(2)}) collective-permute-start(bf16[6,64,448]{2,1,0:T(8,128)(2,1)} %pad_maximum_fusion.3), channel_id=1, source_target_pairs={{0,2},{1,3},{2,0},{3,1},{4,6},{5,7},{6,4},{7,5},{8,10},{9,11},{10,... | collective-permute-start | bytes 1032200 | tf_op jit(solution)/shard_map/ppermute | solution.py:16
  119.3 16.5 %collective-permute-start.36 = (bf16[3,64,448]{2,1,0:T(8,128)(2,1)S(1)}, bf16[3,64,448]{2,1,0:T(8,128)(2,1)}, u32[]{:S(2)}, u32[]{:S(2)}) collective-permute-start(bf16[3,64,448]{2,1,0:T(8,128)(2,1)S(1)} %pad_maximum_fusion.8.refs_7_), channel_id=1, source_target_pairs={{0,16},{16,0},{1,17},{17,1},{2,18},{18,2},{3,19},{19,3},{4,20},{20... | collective-permute-start | bytes 516104 | tf_op jit(solution)/shard_map/ppermute | solution.py:16
  119.5 31.2 %collective-permute-start.24 = (bf16[6,64,448]{2,1,0:T(8,128)(2,1)S(1)}, bf16[6,64,448]{2,1,0:T(8,128)(2,1)S(1)}, u32[]{:S(2)}, u32[]{:S(2)}) collective-permute-start(bf16[6,64,448]{2,1,0:T(8,128)(2,1)S(1)} %collective-permute-done.20.refs_3_), channel_id=1, source_target_pairs={{0,16},{16,0},{1,17},{17,1},{2,18},{18,2},{3,19},{19,3},{4,20},{20... | collective-permute-start | bytes 1032200 | tf_op jit(solution)/shard_map/ppermute | solution.py:16
  119.8 30.8 %collective-permute-start.23 = (bf16[6,64,448]{2,1,0:T(8,128)(2,1)}, bf16[6,64,448]{2,1,0:T(8,128)(2,1)}, u32[]{:S(2)}, u32[]{:S(2)}) collective-permute-start(bf16[6,64,448]{2,1,0:T(8,128)(2,1)} %collective-permute-done.19.refs_2_), channel_id=1, source_target_pairs={{0,16},{16,0},{1,17},{17,1},{2,18},{18,2},{3,19},{19,3},{4,20},{20... | collective-permute-start | bytes 1032200 | tf_op jit(solution)/shard_map/ppermute | solution.py:16
  121.6 14.0 %collective-permute-start.34 = (bf16[2,64,448]{2,1,0:T(8,128)(2,1)S(1)}, bf16[2,64,448]{2,1,0:T(8,128)(2,1)}, u32[]{:S(2)}, u32[]{:S(2)}) collective-permute-start(bf16[2,64,448]{2,1,0:T(8,128)(2,1)S(1)} %collective-permute-done.28.refs_5_), channel_id=1, source_target_pairs={{0,16},{16,0},{1,17},{17,1},{2,18},{18,2},{3,19},{19,3},{4,20},{20... | collective-permute-start | bytes 344072 | tf_op jit(solution)/shard_map/ppermute | solution.py:16
  122.3 14.0 %collective-permute-start.35 = (bf16[3,64,448]{2,1,0:T(8,128)(2,1)S(1)}, bf16[3,64,448]{2,1,0:T(8,128)(2,1)}, u32[]{:S(2)}, u32[]{:S(2)}) collective-permute-start(bf16[3,64,448]{2,1,0:T(8,128)(2,1)S(1)} %pad_maximum_fusion.7.refs_6_), channel_id=1, source_target_pairs={{0,16},{16,0},{1,17},{17,1},{2,18},{18,2},{3,19},{19,3},{4,20},{20... | collective-permute-start | bytes 516104 | tf_op jit(solution)/shard_map/ppermute | solution.py:16
  135.6 15.0 %collective-permute-start.22 = (bf16[3,64,448]{2,1,0:T(8,128)(2,1)S(1)}, bf16[3,64,448]{2,1,0:T(8,128)(2,1)}, u32[]{:S(2)}, u32[]{:S(2)}) collective-permute-start(bf16[3,64,448]{2,1,0:T(8,128)(2,1)S(1)} %collective-permute-done.18.refs_1_), channel_id=1, source_target_pairs={{0,16},{16,0},{1,17},{17,1},{2,18},{18,2},{3,19},{19,3},{4,20},{20... | collective-permute-start | bytes 516104 | tf_op jit(solution)/shard_map/ppermute | solution.py:16
  135.7 14.9 %collective-permute-start.21 = (bf16[3,64,448]{2,1,0:T(8,128)(2,1)S(1)}, bf16[3,64,448]{2,1,0:T(8,128)(2,1)}, u32[]{:S(2)}, u32[]{:S(2)}) collective-permute-start(bf16[3,64,448]{2,1,0:T(8,128)(2,1)S(1)} %collective-permute-done.17.refs_0_), channel_id=1, source_target_pairs={{0,16},{16,0},{1,17},{17,1},{2,18},{18,2},{3,19},{19,3},{4,20},{20... | collective-permute-start | bytes 516104 | tf_op jit(solution)/shard_map/ppermute | solution.py:16
  163.2 14.4 %collective-permute-start.38 = (bf16[64,3584]{1,0:T(8,128)(2,1)S(1)}, bf16[64,3584]{1,0:T(8,128)(2,1)S(1)}, u32[]{:S(2)}, u32[]{:S(2)}) collective-permute-start(bf16[64,3584]{1,0:T(8,128)(2,1)S(1)} %get-tuple-element.28), channel_id=1, source_target_pairs={{0,16},{16,0},{1,17},{17,1},{2,18},{18,2},{3,19},{19,3},{4,20},{20... | collective-permute-start | bytes 1376264 | tf_op jit(solution)/shard_map/ppermute | solution.py:16
  163.8 12.6 %collective-permute-start.44 = (bf16[64,3584]{1,0:T(8,128)(2,1)S(1)}, bf16[64,3584]{1,0:T(8,128)(2,1)S(1)}, u32[]{:S(2)}, u32[]{:S(2)}) collective-permute-start(bf16[64,3584]{1,0:T(8,128)(2,1)S(1)} %add_convert_fusion.1), channel_id=1, source_target_pairs={{0,2},{1,3},{2,0},{3,1},{4,6},{5,7},{6,4},{7,5},{8,10},{9,11},{10,... | collective-permute-start | bytes 1376264 | tf_op jit(solution)/shard_map/ppermute | solution.py:16
  165.1 12.6 %collective-permute-start.40 = (bf16[64,3584]{1,0:T(8,128)(2,1)S(1)}, bf16[64,3584]{1,0:T(8,128)(2,1)S(1)}, u32[]{:S(2)}, u32[]{:S(2)}) collective-permute-start(bf16[64,3584]{1,0:T(8,128)(2,1)S(1)} %add_convert_fusion.2), channel_id=1, source_target_pairs={{0,1},{1,0},{2,3},{3,2},{4,5},{5,4},{6,7},{7,6},{8,9},{9,8},{10,11... | collective-permute-start | bytes 1376264 | tf_op jit(solution)/shard_map/ppermute | solution.py:16
  186.9 9.9 %collective-permute-start.47 = (bf16[8,7168]{1,0:T(8,128)(2,1)S(1)}, bf16[8,7168]{1,0:T(8,128)(2,1)S(1)}, u32[]{:S(2)}, u32[]{:S(2)}) collective-permute-start(bf16[8,7168]{1,0:T(8,128)(2,1)S(1)} %get-tuple-element.37), channel_id=1, source_target_pairs={{0,8},{1,9},{2,10},{3,11},{4,12},{5,13},{6,14},{7,15},{8,0},{9,1},... | collective-permute-start | bytes 344072 | tf_op jit(solution)/shard_map/ppermute | solution.py:16
  (48 other events, 202.4 us)

commit v3 on v0

v3 whole, which is shorter than its diff:
```python
import functools

import jax
import jax.numpy as jnp
from jax import lax
from jax.experimental import pallas as pl
from jax.experimental.pallas import tpu as pltpu
from jax.sharding import PartitionSpec as P

QKD = 192
F32 = jnp.float32
BF16 = jnp.bfloat16
VMEM_LIMIT = 48 * 2**20


def hop(value, axis, size, mask):
    return lax.ppermute(value, axis, [(i, i ^ mask) for i in range(size)])


def gather(block, split, groups, line_hop, plane_hop, beside):
    arrived = {0: block}
    for group in groups:
        for k in group:
            if k:
                arrived[k] = line_hop(block, k)
    halves = ([], [])
    for at, group in enumerate(groups):
        column = jnp.stack([arrived[k] for k in group])
        if at == len(groups) - 1:
            column, beside = lax.optimization_barrier((column, beside))
        for parts, half, (one, two) in zip(halves, split(column), ((1, 2), (2, 1))):
            near = plane_hop(half, one)
            rest = plane_hop(jnp.concatenate([half, near]), two)
            parts.append((half, [(0, k) for k in group]))
            parts.append((near, [(one, k) for k in group]))
            parts.append((rest, [(p, k) for p in (two, 3) for k in group]))
    return halves, beside


def attend_kernel(length_ref, query_ref, cache_ref, own_ref, other_ref, stats_ref, latents, *, scale):
    group, heads, _ = query_ref.shape
    latent_width = own_ref.shape[2]
    slots = cache_ref.shape[2]
    half = heads // 2
    first = pl.program_id(0) * group
    side = length_ref[length_ref.shape[0] - 1]
    positions = side * slots + lax.broadcasted_iota(jnp.int32, (heads, slots), 1)
    lanes = lax.broadcasted_iota(jnp.int32, (heads, stats_ref.shape[2]), 1)
    for at in range(group):
        usable = positions < length_ref[first + at]
        scores = jnp.dot(query_ref[at], cache_ref[at], preferred_element_type=F32) * scale
        masked = jnp.where(usable, scores, -1e30)
        top = jnp.max(masked, axis=1, keepdims=True)
        raised = jnp.where(usable, jnp.exp(masked - top), 0.0)
        total = jnp.sum(raised, axis=1, keepdims=True)
        latent = lax.dot_general(
            raised.astype(BF16),
            cache_ref[at, :latent_width, :],
            (((1,), (1,)), ((), ())),
            preferred_element_type=F32,
        )
        latents[at] = latent / jnp.maximum(total, 1e-30)
        stats_ref[at] = jnp.where(lanes == 0, top, total)
    for at in range(group):
        own_ref[at] = latents[at, pl.ds(pl.multiple_of(side * half, half), half), :].astype(BF16)
        other_ref[at] = latents[
            at, pl.ds(pl.multiple_of((1 - side) * half, half), half), :
        ].astype(BF16)


def attend(queries, cache_columns, lengths, side, latent_width):
    requests, heads, width = queries.shape
    slots = cache_columns.shape[2]
    group = 4
    table = jnp.concatenate([lengths, side.reshape(1)]).astype(jnp.int32)
    return pl.pallas_call(
        functools.partial(attend_kernel, scale=QKD ** (-0.5)),
        grid_spec=pltpu.PrefetchScalarGridSpec(
            num_scalar_prefetch=1,
            grid=(requests // group,),
            in_specs=[
                pl.BlockSpec((group, heads, width), lambda r, table: (r, 0, 0)),
                pl.BlockSpec((group, width, slots), lambda r, table: (r, 0, 0)),
            ],
            out_specs=[
                pl.BlockSpec((group, heads // 2, latent_width), lambda r, table: (r, 0, 0)),
                pl.BlockSpec((group, heads // 2, latent_width), lambda r, table: (r, 0, 0)),
                pl.BlockSpec((group, heads, 128), lambda r, table: (r, 0, 0)),
            ],
            scratch_shapes=[pltpu.VMEM((group, heads, latent_width), F32)],
        ),
        out_shape=[
            jax.ShapeDtypeStruct((requests, heads // 2, latent_width), BF16),
            jax.ShapeDtypeStruct((requests, heads // 2, latent_width), BF16),
            jax.ShapeDtypeStruct((requests, heads, 128), F32),
        ],
        compiler_params=pltpu.CompilerParams(vmem_limit_bytes=48 * 2**20),
        cost_estimate=pl.CostEstimate(
            flops=4 * requests * heads * width * slots,
            bytes_accessed=2 * requests * width * (heads + slots),
            transcendentals=requests * heads * slots,
        ),
    )(table, queries, cache_columns)


def project_kernel(place_ref, *refs, counts, rows, depths, steps):
    groups = len(counts)
    parts = (refs[:groups], refs[groups : 2 * groups])
    map_ref, own_ref, send_ref, first, second, mapping, total, arrived, map_arrived = refs[2 * groups :]
    blocks = sum(counts)
    copies, map_copies = [], []
    for half, left in enumerate((first, second)):
        at = half * blocks
        for part, count in zip(parts[half], counts):
            for k in range(count):
                row = pl.multiple_of(place_ref[at] * rows, rows)
                copies.append(
                    pltpu.make_async_copy(part.at[k], left.at[pl.ds(row, rows)], arrived.at[at])
                )
                at += 1
    tile = mapping.shape[1] // steps
    for step in range(steps):
        columns = pl.ds(step * tile, tile)
        map_copies.append(
            pltpu.make_async_copy(
                map_ref.at[:, columns], mapping.at[:, columns], map_arrived.at[step]
            )
        )
    for copy in copies + map_copies:
        copy.start()
    for copy in copies:
        copy.wait()
    for step in range(steps):
        map_copies[step].wait()
        left = first if step * tile < depths else second
        column = step * tile if step * tile < depths else step * tile - depths
        term = lax.dot_general(
            left[:, column : column + tile],
            mapping[:, step * tile : (step + 1) * tile],
            (((1,), (1,)), ((), ())),
            preferred_element_type=F32,
        )
        if step:
            total[...] += term
        else:
            total[...] = term
    half_rows = total.shape[0] // 2
    side = place_ref[2 * blocks]
    own_ref[...] = total[pl.ds(pl.multiple_of(side * half_rows, half_rows), half_rows), :].T
    send_ref[...] = total[
        pl.ds(pl.multiple_of((1 - side) * half_rows, half_rows), half_rows), :
    ].T.astype(BF16)


def project(first, second, columns_map, place):
    width, depth = columns_map.shape
    rows = first[0].shape[1]
    counts = [part.shape[0] for part in first]
    total_rows = rows * sum(counts)
    steps = 4
    anywhere = pl.BlockSpec(memory_space=pl.ANY)
    whole = pl.BlockSpec(memory_space=pltpu.VMEM)
    return pl.pallas_call(
        functools.partial(
            project_kernel, counts=counts, rows=rows, depths=depth // 2, steps=steps
        ),
        in_specs=[pl.BlockSpec(memory_space=pltpu.SMEM)] + [anywhere] * (2 * len(counts) + 1),
        out_specs=[whole] * 2,
        out_shape=[
            jax.ShapeDtypeStruct((width, total_rows // 2), F32),
            jax.ShapeDtypeStruct((width, total_rows // 2), BF16),
        ],
        scratch_shapes=[
            pltpu.VMEM((total_rows, first[0].shape[2]), BF16),
            pltpu.VMEM((total_rows, second[0].shape[2]), BF16),
            pltpu.VMEM((width, depth), BF16),
            pltpu.VMEM((total_rows, width), F32),
            pltpu.SemaphoreType.DMA((2 * sum(counts),)),
            pltpu.SemaphoreType.DMA((steps,)),
        ],
        compiler_params=pltpu.CompilerParams(vmem_limit_bytes=VMEM_LIMIT),
        cost_estimate=pl.CostEstimate(
            flops=2 * total_rows * depth * width,
            bytes_accessed=2 * (total_rows * depth + depth * width),
            transcendentals=0,
        ),
    )(place, *first, *second, columns_map)


def expert_kernel(place_ref, *refs, blocks, heights, halves, carried, sizes):
    count = len(blocks)
    own, other, refs = refs[:count], refs[count : 2 * count], refs[2 * count :]
    gain_refs, in_ref, refs = refs[:2], refs[2], refs[3:]
    sums_in, refs = refs[: 2 * carried], refs[2 * carried :]
    if sizes:
        gate_ref, down_ref, *refs = refs
        outs, refs = refs[: 2 * len(sizes[2])], refs[2 * len(sizes[2]) :]
        total, squares, weights, rows, arrived, part_arrived = refs[:6]
        activated, results, down, down_arrived, sent = refs[6:]
        down_copy = pltpu.make_async_copy(down_ref, down, down_arrived)
    else:
        total, squares, weights, rows, arrived, part_arrived = refs
    lanes = rows.shape[1] // 2
    offsets = [sum(n * h for n, h in zip(blocks[:at], heights[:at])) for at in range(count + 1)]
    spots = []
    for entry in range(count):
        for k in range(blocks[entry]):
            row = offsets[entry] + k * heights[entry]
            spots.append((entry, k, row, heights[entry]))
    part_copies, weight_copies = [], []
    for at, (entry, k, row, height) in enumerate(spots):
        for side, ref in enumerate((own[entry], other[entry])):
            part_copies.append(
                pltpu.make_async_copy(
                    ref.at[k],
                    rows.at[pl.ds(row, height), pl.ds(side * lanes, lanes)],
                    part_arrived.at[2 * at + side],
                )
            )
        source = pl.multiple_of(place_ref[at], 8)
        weight_copies.append(
            pltpu.make_async_copy(
                in_ref.at[pl.ds(source, height)], weights.at[pl.ds(row, height)], arrived.at[at]
            )
        )
    for copy in part_copies + weight_copies:
        copy.start()
    if sizes:
        down_copy.start()
    if sums_in:
        squares[...] = sums_in[1][...]
    else:
        squares[...] = jnp.zeros_like(squares)
    diagonals = {
        height: lax.broadcasted_iota(jnp.int32, (height, height), 0)
        == lax.broadcasted_iota(jnp.int32, (height, height), 1)
        for height in set(heights)
    }
    for at, (entry, k, row, height) in enumerate(spots):
        part_copies[2 * at].wait()
        part_copies[2 * at + 1].wait()
        wide = rows[row : row + height].astype(F32)
        squares[...] += jnp.sum((wide * wide).reshape(height // 8, 8, 2 * lanes), axis=0)
        gain = gain_refs[halves[entry]][pl.ds(place_ref[len(spots) + at], 1), :]
        gain = jnp.where(diagonals[height], gain, 0.0).astype(BF16)
        rows[row : row + height] = jnp.dot(
            gain, rows[row : row + height], preferred_element_type=F32
        ).astype(BF16)
    for entry in range(count):
        for at, spot in enumerate(spots):
            if spot[0] == entry:
                weight_copies[at].wait()
        term = lax.dot_general(
            rows[offsets[entry] : offsets[entry + 1]],
            weights[offsets[entry] : offsets[entry + 1]],
            (((0,), (0,)), ((), ())),
            preferred_element_type=F32,
        )
        if entry:
            total[...] += term
        elif sums_in:
            total[...] = sums_in[0][...] + term
        else:
            total[...] = term
    if not sizes:
        return

    units = total.shape[1] // 2
    mean = jnp.sum(squares[...].T, axis=1, keepdims=True) / in_ref.shape[0]
    level = lax.rsqrt(mean + 1e-06)
    gate_part = total[:, :units] * level
    up_part = total[:, units:] * level
    raised = gate_part / (1.0 + jnp.exp(-gate_part))
    total[:, :units] = raised * up_part * gate_ref[...]
    owner_rows, moved, groups = sizes
    line = sum(len(group) for group in groups)
    side_rows = total.shape[0] // 2
    order_at = 2 * len(spots)
    for first_row in (0, side_rows):
        for pair in range(side_rows // (2 * owner_rows)):
            pieces = []
            for j in (0, 1):
                row = first_row + place_ref[order_at + 2 * pair + j] * owner_rows
                row = pl.multiple_of(row, owner_rows)
                pieces.append(total[pl.ds(row, owner_rows), :units])
            row = first_row + 2 * pair * owner_rows
            activated[row : row + 2 * owner_rows, :] = jnp.concatenate(pieces).astype(BF16)
    down_copy.wait()
    width = down.shape[1] // 2
    tile = 512
    plane_rows = side_rows // 4
    copies = []
    for half in (0, 1):
        order = [*moved[half], *(group for group in range(4) if group not in moved[half])]
        for column in range(0, width, tile):
            product = jnp.dot(
                activated[...],
                down[:, half * width + column : half * width + column + tile],
                preferred_element_type=F32,
            ).astype(BF16)
            for side in (0, 1):
                source = 0
                for group in groups:
                    for place, at in enumerate(order):
                        size = len(group) * owner_rows
                        row = side * side_rows + at * plane_rows + source
                        target = half * 2 * side_rows + side * side_rows + 4 * source + place * size
                        results[target : target + size, column : column + tile] = product[
                            row : row + size, :
                        ]
                    source += size
        for side in (1, 0):
            source = 0
            for which, group in enumerate(groups):
                size = 4 * len(group) * owner_rows
                target = half * 2 * side_rows + side * side_rows + 4 * source
                copies.append(
                    pltpu.make_async_copy(
                        results.at[pl.ds(target, size)],
                        outs[2 * which + side].at[half],
                        sent.at[len(copies)],
                    )
                )
                copies[-1].start()
                source += len(group) * owner_rows
    for copy in copies:
        copy.wait()


def expert_rows(parts, other_parts, halves, gains, weights, place, carried, finish):
    model_width, double = weights.shape
    lanes = parts[0].shape[2]
    tokens = 2 * lanes
    blocks = [part.shape[0] for part in parts]
    heights = [part.shape[1] for part in parts]
    depth = sum(n * h for n, h in zip(blocks, heights))
    whole = pl.BlockSpec(memory_space=pltpu.VMEM)
    anywhere = pl.BlockSpec(memory_space=pl.ANY)
    sums = [jax.ShapeDtypeStruct((tokens, double), F32), jax.ShapeDtypeStruct((8, tokens), F32)]
    scratch = [
        pltpu.VMEM((depth, double), BF16),
        pltpu.VMEM((depth, tokens), BF16),
        pltpu.SemaphoreType.DMA((sum(blocks),)),
        pltpu.SemaphoreType.DMA((2 * sum(blocks),)),
    ]
    operands = [place, *parts, *other_parts, *gains, weights, *carried]
    in_specs = [pl.BlockSpec(memory_space=pltpu.SMEM)] + [anywhere] * (2 * len(parts))
    in_specs += [whole] * 2 + [anywhere] + [whole] * len(carried)
    sizes = None
    out_shape, out_specs = sums, [whole] * 2
    if finish is not None:
        gates, down, *sizes = finish
        operands += [gates, down]
        in_specs += [whole, anywhere]
        owner_rows, _, groups = sizes
        out_shape = [
            jax.ShapeDtypeStruct((2, 4 * len(group) * owner_rows, model_width // 2), BF16)
            for group in groups
            for _ in range(2)
        ]
        out_specs = [anywhere] * len(out_shape)
        scratch = [pltpu.VMEM(a.shape, F32) for a in sums] + scratch
        scratch += [
            pltpu.VMEM((tokens, double // 2), BF16),
            pltpu.VMEM((2 * tokens, model_width // 2), BF16),
            pltpu.VMEM(down.shape, BF16),
            pltpu.SemaphoreType.DMA,
            pltpu.SemaphoreType.DMA((2 * len(out_shape),)),
        ]
    return pl.pallas_call(
        functools.partial(
            expert_kernel,
            blocks=blocks,
            heights=heights,
            halves=halves,
            carried=len(carried) // 2,
            sizes=sizes,
        ),
        in_specs=in_specs,
        out_specs=out_specs,
        out_shape=out_shape,
        scratch_shapes=scratch,
        compiler_params=pltpu.CompilerParams(vmem_limit_bytes=VMEM_LIMIT),
        cost_estimate=pl.CostEstimate(
            flops=2 * tokens * depth * double,
            bytes_accessed=2 * depth * (double + tokens),
            transcendentals=0,
        ),
    )(*operands)


def on_device(
    queries,
    latent_cache,
    lengths,
    value_lift,
    output_map,
    residual,
    norm_gain,
    expert_ids,
    gate_values,
    expert_in,
    expert_down,
):
    request_count = queries.shape[0]
    latent_width = value_lift.shape[1]
    half_heads = value_lift.shape[0]
    value_width = value_lift.shape[2]
    token_count, model_width = residual.shape
    chips = lax.axis_size("dev")
    plane = 4
    line = chips // plane
    columns = output_map.shape[1]
    experts = chips // 2
    units = expert_down.shape[1]
    side = lax.axis_index("side")
    chip = lax.axis_index("dev")
    line_at, plane_at = chip // plane, chip % plane
    half_tokens = token_count * chips

    def line_hop(value, k):
        return hop(value, "dev", chips, k * plane)

    def plane_hop(value, k):
        return hop(value, "dev", chips, k)

    def swap(value):
        return hop(value, "side", 2, 1)

    def placed(offsets):
        return [(line_at ^ k_line) * plane + (plane_at ^ k_plane) for k_plane, k_line in offsets]

    chosen = expert_ids[:, :, None] == jnp.arange(experts, dtype=jnp.int32)[None, None, :]
    weights = jnp.sum(jnp.where(chosen, gate_values[:, :, None], 0.0), axis=1)
    weights_high = lax.reduce_precision(weights, 8, 7)
    weight_terms = jnp.concatenate([weights_high, weights - weights_high], axis=1).astype(BF16)
    weight_width = -(-token_count * 2 * experts // (request_count * 128)) * 128
    weight_block = jnp.pad(
        weight_terms.reshape(-1), (0, request_count * weight_width - weight_terms.size)
    ).reshape(request_count, weight_width)

    own_latent, sent_latent, stats = attend(
        queries, latent_cache.swapaxes(1, 2), lengths, side, latent_width
    )
    stats = stats[:, :, :2]

    def heads_of(value, which):
        return lax.dynamic_slice_in_dim(value, which * half_heads, half_heads, 1)

    other_latent = swap(sent_latent)
    other_stats = swap(heads_of(stats, 1 - side))
    own_stats = heads_of(stats, side)
    top = jnp.maximum(own_stats[:, :, 0], other_stats[:, :, 0])
    own_share = own_stats[:, :, 1] * jnp.exp(own_stats[:, :, 0] - top)
    other_share = other_stats[:, :, 1] * jnp.exp(other_stats[:, :, 0] - top)
    share_sum = own_share + other_share
    latent_out = (
        own_latent.astype(F32) * (own_share / share_sum)[:, :, None]
        + other_latent.astype(F32) * (other_share / share_sum)[:, :, None]
    ).astype(BF16)
    head_values = jnp.einsum("rhc,hcv->rhv", latent_out, value_lift, preferred_element_type=F32)
    head_values = head_values.astype(BF16).reshape(request_count, half_heads * value_width)

    groups = [list(range(line))]

    half_depth = half_heads * value_width // 2
    first_width = half_depth + weight_width
    sent = jnp.concatenate(
        [head_values[:, :half_depth], weight_block, head_values[:, half_depth:]], axis=1
    )
    sent, residual, expert_in, norm_gain = lax.optimization_barrier(
        (sent, residual, expert_in, norm_gain)
    )

    residual_blocks = residual.reshape(token_count, chips, columns).swapaxes(0, 1)
    residual_columns = lax.all_to_all(
        residual_blocks, "dev", split_axis=0, concat_axis=0, tiled=True
    )
    residual_columns = residual_columns.reshape(half_tokens, columns).T
    (first, second), in_rows = gather(
        sent,
        lambda column: (column[:, :, :first_width], column[:, :, first_width:]),
        groups,
        line_hop,
        plane_hop,
        expert_in.reshape(model_width, 2 * units),
    )
    place = jnp.stack(
        [
            at
            for half in (first, second)
            for _, offsets in half
            for at in placed(offsets)
        ]
        + [side]
    ).astype(jnp.int32)
    first_parts, second_parts = [[part for part, _ in half] for half in (first, second)]
    own_columns, sent_columns = project(first_parts, second_parts, output_map.T, place)
    attention = own_columns + swap(sent_columns).astype(F32)
    hidden = (residual_columns.astype(F32) + attention).astype(BF16)

    gathered = jnp.concatenate([part[:, :, half_depth:] for part, _ in first])
    gathered = gathered.reshape(chips, -1)[:, : token_count * 2 * experts]
    gathered = gathered.reshape(chips, token_count, 2, experts).astype(F32)
    gathered = lax.dynamic_index_in_dim(gathered, chip // 2, 3, keepdims=False).sum(axis=2)
    spots = place[:chips]
    own_gates = jnp.zeros((chips, token_count), F32).at[spots].set(gathered).reshape(-1, 1)
    gates = jnp.concatenate([own_gates, swap(own_gates)])

    first_rows = -(-columns // 32) * 16
    gains = norm_gain.astype(F32).reshape(chips, columns)
    gains = [gains[:, :first_rows], gains[:, first_rows:]]
    back_groups = [list(range(line))]
    hidden_groups = [list(range(line))]
    (first, second), gates = gather(
        hidden,
        lambda column: (column[:, :first_rows], column[:, first_rows:]),
        hidden_groups,
        line_hop,
        plane_hop,
        gates,
    )
    down = expert_down[0]
    out_at = [(p, k) for p in range(plane) for k in range(line)]
    moved = ((1, 3), (2, 3))
    stages = [[0], [1], [2]]
    carried = ()
    for at, stage in enumerate(stages):
        last = at == len(stages) - 1
        parts, halves, spots = [], [], []
        for which in stage:
            for half, (part, offsets) in enumerate((first[which], second[which])):
                parts.append(part)
                halves.append(half)
                spots += [(spot, half) for spot in placed(offsets)]
        table = [spot * columns + half * first_rows for spot, half in spots]
        table += [spot for spot, _ in spots]
        if last:
            parts, carried = lax.optimization_barrier((parts, carried))
            table += placed((p, k) for p in range(plane) for g in back_groups for k in g)
        carried = expert_rows(
            parts,
            [swap(part) for part in parts],
            halves,
            gains,
            in_rows,
            jnp.stack(table).astype(jnp.int32),
            carried,
            (gates, down, token_count, moved, back_groups) if last else None,
        )

    routed_sum = 0.0
    sent_sum = None
    for at, group in enumerate(back_groups):
        own, other = carried[2 * at : 2 * at + 2]
        if sent_sum is not None:
            other, _ = lax.optimization_barrier((other, sent_sum))
        other = swap(other)
        half_sums = []
        for half, (one, two) in enumerate(((1, 2), (2, 1))):
            rows = own.shape[1] // 2
            moved_sum = own[half, :rows].astype(F32) + other[half, :rows].astype(F32)
            sent_sum = moved_sum.astype(BF16)
            kept_sum = own[half, rows:].astype(F32) + other[half, rows:].astype(F32)
            kept_sum = kept_sum + plane_hop(sent_sum, one).astype(F32)
            rows = rows // 2
            arrived = plane_hop(kept_sum[rows:].astype(BF16), two).astype(F32)
            half_sums.append(kept_sum[:rows] + arrived)
        plane_sum = jnp.concatenate(half_sums, axis=1).reshape(len(group), token_count, model_width)
        for place_at, k in enumerate(group):
            if k:
                routed_sum += line_hop(plane_sum[place_at].astype(BF16), k).astype(F32)
            else:
                routed_sum += plane_sum[place_at]

    tokens = chip * token_count + jnp.arange(token_count, dtype=jnp.int32)
    picked = (tokens[:, None] == jnp.arange(half_tokens, dtype=jnp.int32)[None, :]).astype(BF16)
    own_parts, _ = lax.optimization_barrier(([part for half in (first, second) for part, _ in half], sent_sum))
    own_rows = []
    for half, parts in ((first, own_parts[: len(first)]), (second, own_parts[len(first) :])):
        blocks = jnp.concatenate(
            [jnp.einsum("qt,krt->kqr", picked, part, preferred_element_type=F32) for part in parts]
        )
        offsets = [at for _, part_offsets in half for at in part_offsets]
        spots = jnp.stack(placed(offsets))
        own_rows.append(jnp.zeros_like(blocks).at[spots].set(blocks))
    own_hidden = jnp.concatenate(own_rows, axis=2).swapaxes(0, 1).reshape(token_count, model_width)
    return (own_hidden + routed_sum).astype(BF16)


def solution(mesh):
    in_specs = (
        P("dev", None, None),
        P("dev", "side", None),
        P("dev"),
        P("side", None, None),
        P("side", "dev"),
        P(("side", "dev"), None),
        P(),
        P(("side", "dev"), None),
        P(("side", "dev"), None),
        P("dev", None, None, "side"),
        P("dev", "side", None),
    )
    out_specs = P(("side", "dev"), None)
    return jax.shard_map(
        on_device, mesh=mesh, in_specs=in_specs, out_specs=out_specs, check_vma=False
    )
```

time: 342 us -> 156 us (0.46)
  waiting for transfers between devices: 260 us -> 55.9 us
  Pallas kernels: 0 us -> 30.6 us
  starting transfers between devices: 14.1 us -> 40.7 us
  matrix products: 28.5 us -> 5.06 us
  between operations: 13.3 us -> 0.52 us
  blocking collectives: 5.14 us -> 0 us
    all_to_all x3 -> x1, waiting for transfers between devices: 171 us -> 0.01 us  [on_device(): lax.all_to_all(residual_blocks, 'dev', split_axis=0, concat_axis=0, tiled...]
    all_gather x1 -> x0, waiting for transfers between devices: 61.9 us -> none  [on_device(): lax.all_gather(head_values, 'dev', axis=0, tiled=True)]
    ppermute x0 -> x32, waiting for transfers between devices: none -> 55.9 us  [hop(): return lax.ppermute(value, axis, [(i, i ^ mask) for i in range(size)])]
    ppermute x0 -> x32, starting transfers between devices: none -> 34.3 us  [hop(): return lax.ppermute(value, axis, [(i, i ^ mask) for i in range(size)])]
    pallas_call x0 -> x5, Pallas kernels: none -> 30.6 us  [the longest x3 15.5 us: expert_rows(): pl.pallas_call(functools.partial(expert_kernel, blocks=blocks, heights=he...]
    dot_general x8 -> x7, matrix products: 28.5 us -> 5.06 us  [the longest x1 3.39 us: on_device(): jnp.einsum('rhc,hcv->rhv', latent_out, value_lift, preferred_element_type...]
    psum x1 -> x0, waiting for transfers between devices: 20.8 us -> none  [on_device(): row_total, latent_sum = lax.psum((local_total, local_latent), 'side')]
    all_to_all x3 -> x1, starting transfers between devices: 14 us -> 6.34 us  [on_device(): lax.all_to_all(residual_blocks, 'dev', split_axis=0, concat_axis=0, tiled...]
  transfers between devices with their start and end apart: 6 -> 33, of which waited for: 6 -> 20; matrix products, arithmetic and copies ran while one was open for 3% -> 10% of each run, Pallas kernels for 0% -> 9%
where the time goes in v3:
time: 156 us
  waiting for transfers between devices  55.9 us (36%)
  starting transfers between devices  40.7 us (26%)
  Pallas kernels  30.6 us (20%)
  local copies, waits for them, and re-layouts  14.6 us (9%)
  other arithmetic  8.72 us (6%)
  matrix products  5.06 us (3%)
    ppermute x32, waiting for transfers between devices, hop(): return lax.ppermute(value, axis, [(i, i ^ mask) for i in range(size)])  55.9 us
    ppermute x32, starting transfers between devices, hop(): return lax.ppermute(value, axis, [(i, i ^ mask) for i in range(size)])  34.3 us
    pallas_call x3, Pallas kernels, expert_rows(): pl.pallas_call(functools.partial(expert_kernel, blocks=blocks, heights=he...  15.5 us
    unnamed x19, local copies, waits for them, and re-layouts  8.72 us
    pallas_call x1, Pallas kernels, attend(): pl.pallas_call(functools.partial(attend_kernel, scale=QKD ** (-0.5)), gri...  8.33 us
    pallas_call x1, Pallas kernels, project(): pl.pallas_call(functools.partial(project_kernel, counts=counts, rows=rows...  6.78 us
    all_to_all x1, starting transfers between devices, on_device(): lax.all_to_all(residual_blocks, 'dev', split_axis=0, concat_axis=0, tiled...  6.34 us
    dot_general x1, matrix products, on_device(): jnp.einsum('rhc,hcv->rhv', latent_out, value_lift, preferred_element_type...  3.39 us
  transfers between devices with their start and end apart: 33, of which 20 were waited for; matrix products, arithmetic and copies ran while one was open for 10% of the time, Pallas kernels for 9%

profile of v3, /device:TPU:0, one launch (start us, length us, event | category | flops | bytes accessed | tf_op | source)
XLA Modules:
  0.0 156.1 jit_solution(14180858373237111730)
XLA Ops:
  2.1 8.3 %shard_map.109 = (bf16[16,32,512]{2,1,0:T(8,128)(2,1)S(1)}, bf16[16,32,512]{2,1,0:T(8,128)(2,1)S(1)}, f32[16,64,128]{2,1,0:T(8,128)S(1)}) custom-call(s32[17]{0:T(128)S(1)} %pad_add_fusion.length_ref, bf16[16,64,576]{2,1,0:T(8,128)(2,1)S(1)} %copy-done.3, bf16[16,576,384]{2,1,0:T(8,128)(2,1)} %bitcast.149), custom_call_target="tpu_custom_call" | custom-call | flops 905969664 | bytes 8257536 | tf_op jit(solution)/shard_map/pallas_call | solution.py:76
  13.2 3.4 %fusion = bf16[32,2,8,128]{3,2,1,0:T(8,128)(2,1)S(1)} fusion(bf16[32,512,128]{2,1,0:T(8,128)(2,1)} %param.14, bf16[16,32,512]{2,1,0:T(8,128)(2,1)S(1)} %add_convert_fusion), kind=kOutput, calls=%fused_computation.4 | convolution fusion | flops 67174400 | bytes 4849664 | tf_op jit(solution)/shard_map/rhc,hcv->rhv/dot_general | solution.py:461
  16.6 3.0 %collective-permute-start.2 = (bf16[16,4224]{1,0:T(8,128)(2,1)S(1)}, bf16[16,4224]{1,0:T(8,128)(2,1)S(1)}, u32[]{:S(2)}, u32[]{:S(2)}) collective-permute-start(bf16[16,4224]{1,0:T(8,128)(2,1)S(1)} %pad_maximum_fusion.7), channel_id=1, source_target_pairs={{0,4},{1,5},{2,6},{3,7},{4,0},{5,1},{6,2},{7,3},{8,12},{9,13},{10,... | collective-permute-start | bytes 405512 | tf_op jit(solution)/shard_map/ppermute | solution.py:17
  19.6 2.6 %collective-permute-start.3 = (bf16[16,4224]{1,0:T(8,128)(2,1)S(1)}, bf16[16,4224]{1,0:T(8,128)(2,1)S(1)}, u32[]{:S(2)}, u32[]{:S(2)}) collective-permute-start(bf16[16,4224]{1,0:T(8,128)(2,1)S(1)} %pad_maximum_fusion.7), channel_id=1, source_target_pairs={{0,8},{1,9},{2,10},{3,11},{4,12},{5,13},{6,14},{7,15},{8,0},{9,1},... | collective-permute-start | bytes 405512 | tf_op jit(solution)/shard_map/ppermute | solution.py:17
  22.2 4.1 %copy.58 = bf16[896,8,2,256]{3,1,2,0:T(8,128)(2,1)} copy(bf16[896,8,2,256]{3,2,1,0:T(2,128)(2,1)S(1)} %bitcast.148) | data formatting | bytes 14680064
  26.4 6.4 %collective-permute-done.3 = bf16[16,4224]{1,0:T(8,128)(2,1)S(1)} collective-permute-done((bf16[16,4224]{1,0:T(8,128)(2,1)S(1)}, bf16[16,4224]{1,0:T(8,128)(2,1)S(1)}, u32[]{:S(2)}, u32[]{:S(2)}) %collective-permute-start.3) | collective-permute-done | bytes 135200 | tf_op jit(solution)/shard_map/ppermute | solution.py:17
  36.1 3.5 %collective-permute-done.5.refs_1_ = bf16[4,16,2176]{2,1,0:T(8,128)(2,1)S(1)} collective-permute-done((bf16[4,16,2176]{2,1,0:T(8,128)(2,1)S(1)}, bf16[4,16,2176]{2,1,0:T(8,128)(2,1)S(1)}, u32[]{:S(2)}, u32[]{:S(2)}) %collective-permute-start.5) | collective-permute-done | bytes 278560 | tf_op jit(solution)/shard_map/ppermute | solution.py:17
  44.9 6.3 %all-to-all-start = ((bf16[16,8,448]{2,1,0:T(8,128)(2,1)}), bf16[16,8,448]{2,1,0:T(8,128)(2,1)}, u32[]{:S(2)}, u32[]{:S(2)}) async-start(bf16[16,8,448]{2,1,0:T(8,128)(2,1)} %bitcast.140), calls=%async_computation | async-start | bytes 262144 | tf_op jit(solution)/shard_map/all_to_all | solution.py:476
  51.3 2.3 %collective-permute-done.8.refs_5_ = bf16[8,16,2048]{2,1,0:T(8,128)(2,1)S(1)} collective-permute-done((bf16[8,16,2048]{2,1,0:T(8,128)(2,1)}, bf16[8,16,2048]{2,1,0:T(8,128)(2,1)S(1)}, u32[]{:S(2)}, u32[]{:S(2)}) %collective-permute-start.8) | collective-permute-done | bytes 524320 | tf_op jit(solution)/shard_map/ppermute | solution.py:17
  53.6 2.0 %copy-done = bf16[4096,448]{0,1:T(8,128)(2,1)S(1)} copy-done((bf16[4096,448]{0,1:T(8,128)(2,1)S(1)}, bf16[4096,448]{0,1:T(8,128)(2,1)}, u32[]{:S(2)}) %copy-start) | copy-done | bytes 3670040
  55.6 6.8 %shard_map.110 = (f32[448,128]{1,0:T(8,128)S(1)}, bf16[448,128]{1,0:T(8,128)(2,1)S(1)}) custom-call(s32[33]{0:T(128)S(1)} %stack.355.place_ref, bf16[4,16,2176]{2,1,0:T(8,128)(2,1)S(1)} %slice.118.refs_0_, bf16[4,16,2176]{2,1,0:T(8,128)(2,1)S(1)} %collective-permute-done.5.refs_1_, bf16[8,16,2176]{2,1,0:T(8,128)(2,1)S(1)} %collective-permute-done.6.refs_2_, ...), custom_call_target="tpu_custom_call" | custom-call | flops 939524096 | bytes 5767168 | tf_op jit(solution)/shard_map/pallas_call | solution.py:163
  63.8 4.9 %collective-permute-start.10 = (bf16[448,128]{1,0:T(8,128)(2,1)S(1)}, bf16[448,128]{1,0:T(8,128)(2,1)S(1)}, u32[]{:S(2)}, u32[]{:S(2)}) collective-permute-start(bf16[448,128]{1,0:T(8,128)(2,1)S(1)} %fusion.17), channel_id=1, source_target_pairs={{0,4},{1,5},{2,6},{3,7},{4,0},{5,1},{6,2},{7,3},{8,12},{9,13},{10,... | collective-permute-start | bytes 344072 | tf_op jit(solution)/shard_map/ppermute | solution.py:17
  74.0 6.7 %collective-permute-done.11 = bf16[448,128]{1,0:T(8,128)(2,1)S(1)} collective-permute-done((bf16[448,128]{1,0:T(8,128)(2,1)S(1)}, bf16[448,128]{1,0:T(8,128)(2,1)S(1)}, u32[]{:S(2)}, u32[]{:S(2)}) %collective-permute-start.11) | collective-permute-done | bytes 114720 | tf_op jit(solution)/shard_map/ppermute | solution.py:17
  82.8 4.1 %collective-permute-done.16.refs_1_ = bf16[4,224,128]{2,1,0:T(8,128)(2,1)S(1)} collective-permute-done((bf16[4,224,128]{2,1,0:T(8,128)(2,1)S(1)}, bf16[4,224,128]{2,1,0:T(8,128)(2,1)S(1)}, u32[]{:S(2)}, u32[]{:S(2)}) %collective-permute-start.16) | collective-permute-done | bytes 229408 | tf_op jit(solution)/shard_map/ppermute | solution.py:17
  92.3 3.4 %shard_map.111 = (f32[256,512]{1,0:T(8,128)S(1)}, f32[8,256]{1,0:T(8,128)S(1)}) custom-call(s32[16]{0:T(128)S(1)} %stack.400.place_ref, bf16[4,224,128]{2,1,0:T(8,128)(2,1)S(1)} %get-tuple-element.57.refs_0_, bf16[4,224,128]{2,1,0:T(8,128)(2,1)S(1)} %get-tuple-element.60.refs_1_, bf16[4,224,128]{2,1,0:T(8,128)(2,1)S(1)} %collective-permute-done.20.refs_2_, ...), custom_call_target="tpu_custom_call" | custom-call | flops 469762048 | bytes 2752512 | tf_op jit(solution)/shard_map/pallas_call | solution.py:370
  95.7 3.5 %shard_map.112 = (f32[256,512]{1,0:T(8,128)S(1)}, f32[8,256]{1,0:T(8,128)S(1)}) custom-call(s32[16]{0:T(128)S(1)} %stack.391.place_ref, bf16[4,224,128]{2,1,0:T(8,128)(2,1)S(1)} %collective-permute-done.14.refs_0_, bf16[4,224,128]{2,1,0:T(8,128)(2,1)S(1)} %collective-permute-done.16.refs_1_, bf16[4,224,128]{2,1,0:T(8,128)(2,1)S(1)} %collective-permute-done.18.refs_2_, ...), custom_call_target="tpu_custom_call" | custom-call | flops 469762048 | bytes 2752512 | tf_op jit(solution)/shard_map/pallas_call | solution.py:370
  101.7 8.6 %shard_map.113 = (bf16[2,128,3584]{2,1,0:T(8,128)(2,1)S(1)}, bf16[2,128,3584]{2,1,0:T(8,128)(2,1)}) custom-call(s32[48]{0:T(128)S(1)} %stack.382.place_ref, bf16[8,224,128]{2,1,0:T(8,128)(2,1)S(1)} %collective-permute-done.15.refs_0_, bf16[8,224,128]{2,1,0:T(8,128)(2,1)S(1)} %collective-permute-done.17.refs_1_, ...), custom_call_target="tpu_custom_call" | custom-call | flops 939524096 | bytes 5505024 | tf_op jit(solution)/shard_map/pallas_call | solution.py:370
  111.8 4.0 %collective-permute-done.24 = bf16[2,128,3584]{2,1,0:T(8,128)(2,1)} collective-permute-done((bf16[2,128,3584]{2,1,0:T(8,128)(2,1)}, bf16[2,128,3584]{2,1,0:T(8,128)(2,1)}, u32[]{:S(2)}, u32[]{:S(2)}) %collective-permute-start.24) | collective-permute-done | bytes 1835040 | tf_op jit(solution)/shard_map/ppermute | solution.py:17
  117.4 2.2 %collective-permute-start.25 = (bf16[64,3584]{1,0:T(8,128)(2,1)S(1)}, bf16[64,3584]{1,0:T(8,128)(2,1)S(1)}, u32[]{:S(2)}, u32[]{:S(2)}) collective-permute-start(bf16[64,3584]{1,0:T(8,128)(2,1)S(1)} %get-tuple-element.67), channel_id=1, source_target_pairs={{0,1},{1,0},{2,3},{3,2},{4,5},{5,4},{6,7},{7,6},{8,9},{9,8},{10,11... | collective-permute-start | bytes 1376264 | tf_op jit(solution)/shard_map/ppermute | solution.py:17
  121.5 8.9 %collective-permute-done.25 = bf16[64,3584]{1,0:T(8,128)(2,1)S(1)} collective-permute-done((bf16[64,3584]{1,0:T(8,128)(2,1)S(1)}, bf16[64,3584]{1,0:T(8,128)(2,1)S(1)}, u32[]{:S(2)}, u32[]{:S(2)}) %collective-permute-start.25) | collective-permute-done | bytes 458784 | tf_op jit(solution)/shard_map/ppermute | solution.py:17
  136.3 3.6 %collective-permute-done.28 = bf16[32,3584]{1,0:T(8,128)(2,1)S(1)} collective-permute-done((bf16[32,3584]{1,0:T(8,128)(2,1)S(1)}, bf16[32,3584]{1,0:T(8,128)(2,1)S(1)}, u32[]{:S(2)}, u32[]{:S(2)}) %collective-permute-start.28) | collective-permute-done | bytes 229408 | tf_op jit(solution)/shard_map/ppermute | solution.py:17
  140.0 2.6 %collective-permute-done.26 = bf16[32,3584]{1,0:T(8,128)(2,1)S(1)} collective-permute-done((bf16[32,3584]{1,0:T(8,128)(2,1)S(1)}, bf16[32,3584]{1,0:T(8,128)(2,1)S(1)}, u32[]{:S(2)}, u32[]{:S(2)}) %collective-permute-start.26) | collective-permute-done | bytes 229408 | tf_op jit(solution)/shard_map/ppermute | solution.py:17
  142.7 2.8 %collective-permute-start.29 = (bf16[8,7168]{1,0:T(8,128)(2,1)S(1)}, bf16[8,7168]{1,0:T(8,128)(2,1)S(1)}, u32[]{:S(2)}, u32[]{:S(2)}) collective-permute-start(bf16[8,7168]{1,0:T(8,128)(2,1)S(1)} %get-tuple-element.71), channel_id=1, source_target_pairs={{0,4},{1,5},{2,6},{3,7},{4,0},{5,1},{6,2},{7,3},{8,12},{9,13},{10,... | collective-permute-start | bytes 344072 | tf_op jit(solution)/shard_map/ppermute | solution.py:17
  148.9 6.4 %collective-permute-done.30 = bf16[8,7168]{1,0:T(8,128)(2,1)S(1)} collective-permute-done((bf16[8,7168]{1,0:T(8,128)(2,1)S(1)}, bf16[8,7168]{1,0:T(8,128)(2,1)S(1)}, u32[]{:S(2)}, u32[]{:S(2)}) %collective-permute-start.30) | collective-permute-done | bytes 114720 | tf_op jit(solution)/shard_map/ppermute | solution.py:17
  (140 shorter events, 45.0 us)
Async XLA Ops:
  16.6 9.7 %collective-permute-start.2 = (bf16[16,4224]{1,0:T(8,128)(2,1)S(1)}, bf16[16,4224]{1,0:T(8,128)(2,1)S(1)}, u32[]{:S(2)}, u32[]{:S(2)}) collective-permute-start(bf16[16,4224]{1,0:T(8,128)(2,1)S(1)} %pad_maximum_fusion.7), channel_id=1, source_target_pairs={{0,4},{1,5},{2,6},{3,7},{4,0},{5,1},{6,2},{7,3},{8,12},{9,13},{10,... | collective-permute-start | bytes 405512 | tf_op jit(solution)/shard_map/ppermute | solution.py:17
  19.6 13.2 %collective-permute-start.3 = (bf16[16,4224]{1,0:T(8,128)(2,1)S(1)}, bf16[16,4224]{1,0:T(8,128)(2,1)S(1)}, u32[]{:S(2)}, u32[]{:S(2)}) collective-permute-start(bf16[16,4224]{1,0:T(8,128)(2,1)S(1)} %pad_maximum_fusion.7), channel_id=1, source_target_pairs={{0,8},{1,9},{2,10},{3,11},{4,12},{5,13},{6,14},{7,15},{8,0},{9,1},... | collective-permute-start | bytes 405512 | tf_op jit(solution)/shard_map/ppermute | solution.py:17
  22.2 10.6 %collective-permute-start.4 = (bf16[16,4224]{1,0:T(8,128)(2,1)S(1)}, bf16[16,4224]{1,0:T(8,128)(2,1)S(1)}, u32[]{:S(2)}, u32[]{:S(2)}) collective-permute-start(bf16[16,4224]{1,0:T(8,128)(2,1)S(1)} %pad_maximum_fusion.7), channel_id=1, source_target_pairs={{0,12},{1,13},{2,14},{3,15},{4,8},{5,9},{6,10},{7,11},{8,4},{9,5},... | collective-permute-start | bytes 405512 | tf_op jit(solution)/shard_map/ppermute | solution.py:17
  32.9 6.7 %collective-permute-start.5 = (bf16[4,16,2176]{2,1,0:T(8,128)(2,1)S(1)}, bf16[4,16,2176]{2,1,0:T(8,128)(2,1)S(1)}, u32[]{:S(2)}, u32[]{:S(2)}) collective-permute-start(bf16[4,16,2176]{2,1,0:T(8,128)(2,1)S(1)} %slice.118.refs_0_), channel_id=1, source_target_pairs={{0,1},{1,0},{2,3},{3,2},{4,5},{5,4},{6,7},{7,6},{8,9},{9,8},{10,11... | collective-permute-start | bytes 835592 | tf_op jit(solution)/shard_map/ppermute | solution.py:17
  34.5 7.9 %collective-permute-start.7 = (bf16[4,16,2048]{2,1,0:T(8,128)(2,1)S(1)}, bf16[4,16,2048]{2,1,0:T(8,128)(2,1)S(1)}, u32[]{:S(2)}, u32[]{:S(2)}) collective-permute-start(bf16[4,16,2048]{2,1,0:T(8,128)(2,1)S(1)} %slice.119.refs_3_), channel_id=1, source_target_pairs={{0,2},{1,3},{2,0},{3,1},{4,6},{5,7},{6,4},{7,5},{8,10},{9,11},{10,... | collective-permute-start | bytes 786440 | tf_op jit(solution)/shard_map/ppermute | solution.py:17
  39.7 13.9 %collective-permute-start.6 = (bf16[8,16,2176]{2,1,0:T(8,128)(2,1)S(1)}, bf16[8,16,2176]{2,1,0:T(8,128)(2,1)S(1)}, u32[]{:S(2)}, u32[]{:S(2)}) collective-permute-start(bf16[8,16,2176]{2,1,0:T(8,128)(2,1)S(1)} %pad_maximum_fusion.1), channel_id=1, source_target_pairs={{0,2},{1,3},{2,0},{3,1},{4,6},{5,7},{6,4},{7,5},{8,10},{9,11},{10,... | collective-permute-start | bytes 1671176 | tf_op jit(solution)/shard_map/ppermute | solution.py:17
  43.2 10.3 %collective-permute-start.8 = (bf16[8,16,2048]{2,1,0:T(8,128)(2,1)}, bf16[8,16,2048]{2,1,0:T(8,128)(2,1)S(1)}, u32[]{:S(2)}, u32[]{:S(2)}) collective-permute-start(bf16[8,16,2048]{2,1,0:T(8,128)(2,1)} %pad_maximum_fusion.3), channel_id=1, source_target_pairs={{0,1},{1,0},{2,3},{3,2},{4,5},{5,4},{6,7},{7,6},{8,9},{9,8},{10,11... | collective-permute-start | bytes 1572872 | tf_op jit(solution)/shard_map/ppermute | solution.py:17
  44.9 17.6 %all-to-all-start = ((bf16[16,8,448]{2,1,0:T(8,128)(2,1)}), bf16[16,8,448]{2,1,0:T(8,128)(2,1)}, u32[]{:S(2)}, u32[]{:S(2)}) async-start(bf16[16,8,448]{2,1,0:T(8,128)(2,1)} %bitcast.140), calls=%async_computation | async-start | bytes 262144 | tf_op jit(solution)/shard_map/all_to_all | solution.py:476
  63.8 10.1 %collective-permute-start.10 = (bf16[448,128]{1,0:T(8,128)(2,1)S(1)}, bf16[448,128]{1,0:T(8,128)(2,1)S(1)}, u32[]{:S(2)}, u32[]{:S(2)}) collective-permute-start(bf16[448,128]{1,0:T(8,128)(2,1)S(1)} %fusion.17), channel_id=1, source_target_pairs={{0,4},{1,5},{2,6},{3,7},{4,0},{5,1},{6,2},{7,3},{8,12},{9,13},{10,... | collective-permute-start | bytes 344072 | tf_op jit(solution)/shard_map/ppermute | solution.py:17
  68.8 11.9 %collective-permute-start.11 = (bf16[448,128]{1,0:T(8,128)(2,1)S(1)}, bf16[448,128]{1,0:T(8,128)(2,1)S(1)}, u32[]{:S(2)}, u32[]{:S(2)}) collective-permute-start(bf16[448,128]{1,0:T(8,128)(2,1)S(1)} %fusion.17), channel_id=1, source_target_pairs={{0,8},{1,9},{2,10},{3,11},{4,12},{5,13},{6,14},{7,15},{8,0},{9,1},... | collective-permute-start | bytes 344072 | tf_op jit(solution)/shard_map/ppermute | solution.py:17
  70.1 10.6 %collective-permute-start.12 = (bf16[448,128]{1,0:T(8,128)(2,1)S(1)}, bf16[448,128]{1,0:T(8,128)(2,1)S(1)}, u32[]{:S(2)}, u32[]{:S(2)}) collective-permute-start(bf16[448,128]{1,0:T(8,128)(2,1)S(1)} %fusion.17), channel_id=1, source_target_pairs={{0,12},{1,13},{2,14},{3,15},{4,8},{5,9},{6,10},{7,11},{8,4},{9,5},... | collective-permute-start | bytes 344072 | tf_op jit(solution)/shard_map/ppermute | solution.py:17
  80.7 6.1 %collective-permute-start.16 = (bf16[4,224,128]{2,1,0:T(8,128)(2,1)S(1)}, bf16[4,224,128]{2,1,0:T(8,128)(2,1)S(1)}, u32[]{:S(2)}, u32[]{:S(2)}) collective-permute-start(bf16[4,224,128]{2,1,0:T(8,128)(2,1)S(1)} %get-tuple-element.60.refs_1_), channel_id=1, source_target_pairs={{0,2},{1,3},{2,0},{3,1},{4,6},{5,7},{6,4},{7,5},{8,10},{9,11},{10,... | collective-permute-start | bytes 688136 | tf_op jit(solution)/shard_map/ppermute | solution.py:17
  81.4 7.2 %collective-permute-start.14 = (bf16[4,224,128]{2,1,0:T(8,128)(2,1)S(1)}, bf16[4,224,128]{2,1,0:T(8,128)(2,1)S(1)}, u32[]{:S(2)}, u32[]{:S(2)}) collective-permute-start(bf16[4,224,128]{2,1,0:T(8,128)(2,1)S(1)} %get-tuple-element.57.refs_0_), channel_id=1, source_target_pairs={{0,1},{1,0},{2,3},{3,2},{4,5},{5,4},{6,7},{7,6},{8,9},{9,8},{10,11... | collective-permute-start | bytes 688136 | tf_op jit(solution)/shard_map/ppermute | solution.py:17
  82.8 8.8 %collective-permute-start.20 = (bf16[4,224,128]{2,1,0:T(8,128)(2,1)S(1)}, bf16[4,224,128]{2,1,0:T(8,128)(2,1)S(1)}, u32[]{:S(2)}, u32[]{:S(2)}) collective-permute-start(bf16[4,224,128]{2,1,0:T(8,128)(2,1)S(1)} %get-tuple-element.57.refs_0_), channel_id=1, source_target_pairs={{0,16},{16,0},{1,17},{17,1},{2,18},{18,2},{3,19},{19,3},{4,20},{20... | collective-permute-start | bytes 688136 | tf_op jit(solution)/shard_map/ppermute | solution.py:17
  86.9 12.3 %collective-permute-start.17 = (bf16[8,224,128]{2,1,0:T(8,128)(2,1)S(1)}, bf16[8,224,128]{2,1,0:T(8,128)(2,1)S(1)}, u32[]{:S(2)}, u32[]{:S(2)}) collective-permute-start(bf16[8,224,128]{2,1,0:T(8,128)(2,1)S(1)} %pad_maximum_fusion.6), channel_id=1, source_target_pairs={{0,1},{1,0},{2,3},{3,2},{4,5},{5,4},{6,7},{7,6},{8,9},{9,8},{10,11... | collective-permute-start | bytes 1376264 | tf_op jit(solution)/shard_map/ppermute | solution.py:17
  89.5 9.7 %collective-permute-start.15 = (bf16[8,224,128]{2,1,0:T(8,128)(2,1)}, bf16[8,224,128]{2,1,0:T(8,128)(2,1)S(1)}, u32[]{:S(2)}, u32[]{:S(2)}) collective-permute-start(bf16[8,224,128]{2,1,0:T(8,128)(2,1)} %pad_maximum_fusion.5), channel_id=1, source_target_pairs={{0,2},{1,3},{2,0},{3,1},{4,6},{5,7},{6,4},{7,5},{8,10},{9,11},{10,... | collective-permute-start | bytes 1376264 | tf_op jit(solution)/shard_map/ppermute | solution.py:17
  91.1 4.6 %collective-permute-start.18 = (bf16[4,224,128]{2,1,0:T(8,128)(2,1)S(1)}, bf16[4,224,128]{2,1,0:T(8,128)(2,1)S(1)}, u32[]{:S(2)}, u32[]{:S(2)}) collective-permute-start(bf16[4,224,128]{2,1,0:T(8,128)(2,1)S(1)} %collective-permute-done.14.refs_0_), channel_id=1, source_target_pairs={{0,16},{16,0},{1,17},{17,1},{2,18},{18,2},{3,19},{19,3},{4,20},{20... | collective-permute-start | bytes 688136 | tf_op jit(solution)/shard_map/ppermute | solution.py:17
  117.4 13.0 %collective-permute-start.25 = (bf16[64,3584]{1,0:T(8,128)(2,1)S(1)}, bf16[64,3584]{1,0:T(8,128)(2,1)S(1)}, u32[]{:S(2)}, u32[]{:S(2)}) collective-permute-start(bf16[64,3584]{1,0:T(8,128)(2,1)S(1)} %get-tuple-element.67), channel_id=1, source_target_pairs={{0,1},{1,0},{2,3},{3,2},{4,5},{5,4},{6,7},{7,6},{8,9},{9,8},{10,11... | collective-permute-start | bytes 1376264 | tf_op jit(solution)/shard_map/ppermute | solution.py:17
  119.6 12.3 %collective-permute-start.27 = (bf16[64,3584]{1,0:T(8,128)(2,1)S(1)}, bf16[64,3584]{1,0:T(8,128)(2,1)S(1)}, u32[]{:S(2)}, u32[]{:S(2)}) collective-permute-start(bf16[64,3584]{1,0:T(8,128)(2,1)S(1)} %get-tuple-element.68), channel_id=1, source_target_pairs={{0,2},{1,3},{2,0},{3,1},{4,6},{5,7},{6,4},{7,5},{8,10},{9,11},{10,... | collective-permute-start | bytes 1376264 | tf_op jit(solution)/shard_map/ppermute | solution.py:17
  133.4 6.6 %collective-permute-start.28 = (bf16[32,3584]{1,0:T(8,128)(2,1)S(1)}, bf16[32,3584]{1,0:T(8,128)(2,1)S(1)}, u32[]{:S(2)}, u32[]{:S(2)}) collective-permute-start(bf16[32,3584]{1,0:T(8,128)(2,1)S(1)} %slice.197), channel_id=1, source_target_pairs={{0,1},{1,0},{2,3},{3,2},{4,5},{5,4},{6,7},{7,6},{8,9},{9,8},{10,11... | collective-permute-start | bytes 688136 | tf_op jit(solution)/shard_map/ppermute | solution.py:17
  136.0 6.6 %collective-permute-start.26 = (bf16[32,3584]{1,0:T(8,128)(2,1)S(1)}, bf16[32,3584]{1,0:T(8,128)(2,1)S(1)}, u32[]{:S(2)}, u32[]{:S(2)}) collective-permute-start(bf16[32,3584]{1,0:T(8,128)(2,1)S(1)} %slice.198), channel_id=1, source_target_pairs={{0,2},{1,3},{2,0},{3,1},{4,6},{5,7},{6,4},{7,5},{8,10},{9,11},{10,... | collective-permute-start | bytes 688136 | tf_op jit(solution)/shard_map/ppermute | solution.py:17
  142.7 6.2 %collective-permute-start.29 = (bf16[8,7168]{1,0:T(8,128)(2,1)S(1)}, bf16[8,7168]{1,0:T(8,128)(2,1)S(1)}, u32[]{:S(2)}, u32[]{:S(2)}) collective-permute-start(bf16[8,7168]{1,0:T(8,128)(2,1)S(1)} %get-tuple-element.71), channel_id=1, source_target_pairs={{0,4},{1,5},{2,6},{3,7},{4,0},{5,1},{6,2},{7,3},{8,12},{9,13},{10,... | collective-permute-start | bytes 344072 | tf_op jit(solution)/shard_map/ppermute | solution.py:17
  145.5 9.9 %collective-permute-start.30 = (bf16[8,7168]{1,0:T(8,128)(2,1)S(1)}, bf16[8,7168]{1,0:T(8,128)(2,1)S(1)}, u32[]{:S(2)}, u32[]{:S(2)}) collective-permute-start(bf16[8,7168]{1,0:T(8,128)(2,1)S(1)} %get-tuple-element.73), channel_id=1, source_target_pairs={{0,8},{1,9},{2,10},{3,11},{4,12},{5,13},{6,14},{7,15},{8,0},{9,1},... | collective-permute-start | bytes 344072 | tf_op jit(solution)/shard_map/ppermute | solution.py:17
  147.0 8.3 %collective-permute-start.31 = (bf16[8,7168]{1,0:T(8,128)(2,1)S(1)}, bf16[8,7168]{1,0:T(8,128)(2,1)S(1)}, u32[]{:S(2)}, u32[]{:S(2)}) collective-permute-start(bf16[8,7168]{1,0:T(8,128)(2,1)S(1)} %get-tuple-element.72), channel_id=1, source_target_pairs={{0,12},{1,13},{2,14},{3,15},{4,8},{5,9},{6,10},{7,11},{8,4},{9,5},... | collective-permute-start | bytes 344072 | tf_op jit(solution)/shard_map/ppermute | solution.py:17
  (18 other events, 118.9 us)

commit v4 on v3

--- a/solution.py
+++ b/solution.py
@@ -11,13 +11,14 @@
 F32 = jnp.float32
 BF16 = jnp.bfloat16
 VMEM_LIMIT = 48 * 2**20
+LAST_VMEM_LIMIT = 52 * 2**20
 
 
 def hop(value, axis, size, mask):
     return lax.ppermute(value, axis, [(i, i ^ mask) for i in range(size)])
 
 
-def gather(block, split, groups, line_hop, plane_hop, beside):
+def gather(block, split, groups, line_hop, plane_hop, beside, after):
     arrived = {0: block}
     for group in groups:
         for k in group:
@@ -25,16 +26,22 @@
                 arrived[k] = line_hop(block, k)
     halves = ([], [])
     for at, group in enumerate(groups):
+        if at == 0 and len(group) > 1:
+            block, arrived[group[1]] = lax.optimization_barrier((block, arrived[group[1]]))
+            arrived[0] = block
         column = jnp.stack([arrived[k] for k in group])
         if at == len(groups) - 1:
             column, beside = lax.optimization_barrier((column, beside))
-        for parts, half, (one, two) in zip(halves, split(column), ((1, 2), (2, 1))):
-            near = plane_hop(half, one)
+        split_column = split(column)
+        nears = [plane_hop(half, one) for half, one in zip(split_column, (1, 2))]
+        if at == len(groups) - 1:
+            nears, after = lax.optimization_barrier((nears, after))
+        for parts, half, near, (one, two) in zip(halves, split_column, nears, ((1, 2), (2, 1))):
             rest = plane_hop(jnp.concatenate([half, near]), two)
             parts.append((half, [(0, k) for k in group]))
             parts.append((near, [(one, k) for k in group]))
             parts.append((rest, [(p, k) for p in (two, 3) for k in group]))
-    return halves, beside
+    return halves, beside, after
 
 
 def attend_kernel(length_ref, query_ref, cache_ref, own_ref, other_ref, stats_ref, latents, *, scale):
@@ -46,22 +53,28 @@
     side = length_ref[length_ref.shape[0] - 1]
     positions = side * slots + lax.broadcasted_iota(jnp.int32, (heads, slots), 1)
     lanes = lax.broadcasted_iota(jnp.int32, (heads, stats_ref.shape[2]), 1)
-    for at in range(group):
-        usable = positions < length_ref[first + at]
-        scores = jnp.dot(query_ref[at], cache_ref[at], preferred_element_type=F32) * scale
-        masked = jnp.where(usable, scores, -1e30)
-        top = jnp.max(masked, axis=1, keepdims=True)
-        raised = jnp.where(usable, jnp.exp(masked - top), 0.0)
-        total = jnp.sum(raised, axis=1, keepdims=True)
-        latent = lax.dot_general(
-            raised.astype(BF16),
+    everyone = range(group)
+    usable = [positions < length_ref[first + at] for at in everyone]
+    scores = [
+        jnp.dot(query_ref[at], cache_ref[at], preferred_element_type=F32) * scale for at in everyone
+    ]
+    masked = [jnp.where(usable[at], scores[at], -1e30) for at in everyone]
+    tops = [jnp.max(masked[at], axis=1, keepdims=True) for at in everyone]
+    raised = [jnp.where(usable[at], jnp.exp(masked[at] - tops[at]), 0.0) for at in everyone]
+    totals = [jnp.sum(raised[at], axis=1, keepdims=True) for at in everyone]
+    sums = [
+        lax.dot_general(
+            raised[at].astype(BF16),
             cache_ref[at, :latent_width, :],
             (((1,), (1,)), ((), ())),
             preferred_element_type=F32,
         )
-        latents[at] = latent / jnp.maximum(total, 1e-30)
-        stats_ref[at] = jnp.where(lanes == 0, top, total)
-    for at in range(group):
+        for at in everyone
+    ]
+    for at in everyone:
+        latents[at] = sums[at] / jnp.maximum(totals[at], 1e-30)
+        stats_ref[at] = jnp.where(lanes == 0, tops[at], totals[at])
+    for at in everyone:
         own_ref[at] = latents[at, pl.ds(pl.multiple_of(side * half, half), half), :].astype(BF16)
         other_ref[at] = latents[
             at, pl.ds(pl.multiple_of((1 - side) * half, half), half), :
@@ -126,11 +139,17 @@
                 map_ref.at[:, columns], mapping.at[:, columns], map_arrived.at[step]
             )
         )
-    for copy in copies + map_copies:
-        copy.start()
-    for copy in copies:
-        copy.wait()
+    in_half = steps // 2
+    for half in (0, 1):
+        for copy in copies[half * blocks : (half + 1) * blocks]:
+            copy.start()
+        for copy in map_copies[half * in_half : (half + 1) * in_half]:
+            copy.start()
     for step in range(steps):
+        if step % in_half == 0:
+            half = step // in_half
+            for copy in copies[half * blocks : (half + 1) * blocks]:
+                copy.wait()
         map_copies[step].wait()
         left = first if step * tile < depths else second
         column = step * tile if step * tile < depths else step * tile - depths
@@ -178,7 +197,7 @@
             pltpu.SemaphoreType.DMA((2 * sum(counts),)),
             pltpu.SemaphoreType.DMA((steps,)),
         ],
-        compiler_params=pltpu.CompilerParams(vmem_limit_bytes=VMEM_LIMIT),
+        compiler_params=pltpu.CompilerParams(vmem_limit_bytes=60 * 2**20),
         cost_estimate=pl.CostEstimate(
             flops=2 * total_rows * depth * width,
             bytes_accessed=2 * (total_rows * depth + depth * width),
@@ -194,7 +213,7 @@
     sums_in, refs = refs[: 2 * carried], refs[2 * carried :]
     if sizes:
         gate_ref, down_ref, *refs = refs
-        outs, refs = refs[: 2 * len(sizes[2])], refs[2 * len(sizes[2]) :]
+        outs, refs = refs[: 4 * len(sizes[2])], refs[4 * len(sizes[2]) :]
         total, squares, weights, rows, arrived, part_arrived = refs[:6]
         activated, results, down, down_arrived, sent = refs[6:]
         down_copy = pltpu.make_async_copy(down_ref, down, down_arrived)
@@ -317,7 +336,7 @@
                 copies.append(
                     pltpu.make_async_copy(
                         results.at[pl.ds(target, size)],
-                        outs[2 * which + side].at[half],
+                        outs[4 * which + 2 * half + side],
                         sent.at[len(copies)],
                     )
                 )
@@ -354,9 +373,9 @@
         in_specs += [whole, anywhere]
         owner_rows, _, groups = sizes
         out_shape = [
-            jax.ShapeDtypeStruct((2, 4 * len(group) * owner_rows, model_width // 2), BF16)
+            jax.ShapeDtypeStruct((4 * len(group) * owner_rows, model_width // 2), BF16)
             for group in groups
-            for _ in range(2)
+            for _ in range(4)
         ]
         out_specs = [anywhere] * len(out_shape)
         scratch = [pltpu.VMEM(a.shape, F32) for a in sums] + scratch
@@ -365,7 +384,7 @@
             pltpu.VMEM((2 * tokens, model_width // 2), BF16),
             pltpu.VMEM(down.shape, BF16),
             pltpu.SemaphoreType.DMA,
-            pltpu.SemaphoreType.DMA((2 * len(out_shape),)),
+            pltpu.SemaphoreType.DMA((len(out_shape),)),
         ]
     return pl.pallas_call(
         functools.partial(
@@ -380,7 +399,9 @@
         out_specs=out_specs,
         out_shape=out_shape,
         scratch_shapes=scratch,
-        compiler_params=pltpu.CompilerParams(vmem_limit_bytes=VMEM_LIMIT),
+        compiler_params=pltpu.CompilerParams(
+            vmem_limit_bytes=VMEM_LIMIT if finish is None else LAST_VMEM_LIMIT
+        ),
         cost_estimate=pl.CostEstimate(
             flops=2 * tokens * depth * double,
             bytes_accessed=2 * depth * (double + tokens),
@@ -461,7 +482,7 @@
     head_values = jnp.einsum("rhc,hcv->rhv", latent_out, value_lift, preferred_element_type=F32)
     head_values = head_values.astype(BF16).reshape(request_count, half_heads * value_width)
 
-    groups = [list(range(line))]
+    groups = [list(range(line // 2)), list(range(line // 2, line))]
 
     half_depth = half_heads * value_width // 2
     first_width = half_depth + weight_width
@@ -472,19 +493,21 @@
         (sent, residual, expert_in, norm_gain)
     )
 
-    residual_blocks = residual.reshape(token_count, chips, columns).swapaxes(0, 1)
-    residual_columns = lax.all_to_all(
-        residual_blocks, "dev", split_axis=0, concat_axis=0, tiled=True
-    )
-    residual_columns = residual_columns.reshape(half_tokens, columns).T
-    (first, second), in_rows = gather(
+    (first, second), in_rows, residual = gather(
         sent,
         lambda column: (column[:, :, :first_width], column[:, :, first_width:]),
         groups,
         line_hop,
         plane_hop,
         expert_in.reshape(model_width, 2 * units),
-    )
+        residual,
+    )
+
+    residual_blocks = residual.reshape(token_count, chips, columns).swapaxes(0, 1)
+    residual_columns = lax.all_to_all(
+        residual_blocks, "dev", split_axis=0, concat_axis=0, tiled=True
+    )
+
     place = jnp.stack(
         [
             at
@@ -496,6 +519,8 @@
     ).astype(jnp.int32)
     first_parts, second_parts = [[part for part, _ in half] for half in (first, second)]
     own_columns, sent_columns = project(first_parts, second_parts, output_map.T, place)
+    sent_columns, residual_columns = lax.optimization_barrier((sent_columns, residual_columns))
+    residual_columns = residual_columns.reshape(half_tokens, columns).T
     attention = own_columns + swap(sent_columns).astype(F32)
     hidden = (residual_columns.astype(F32) + attention).astype(BF16)
 
@@ -512,13 +537,14 @@
     gains = [gains[:, :first_rows], gains[:, first_rows:]]
     back_groups = [list(range(line))]
     hidden_groups = [list(range(line))]
-    (first, second), gates = gather(
+    (first, second), gates, _ = gather(
         hidden,
         lambda column: (column[:, :first_rows], column[:, first_rows:]),
         hidden_groups,
         line_hop,
         plane_hop,
         gates,
+        (),
     )
     down = expert_down[0]
     out_at = [(p, k) for p in range(plane) for k in range(line)]
@@ -549,27 +575,44 @@
             (gates, down, token_count, moved, back_groups) if last else None,
         )
 
+    orders = ((1, 2), (2, 1))
+    group_count = len(back_groups)
+    kept, sent = [], []
+    for at in range(group_count):
+        own, other = carried[4 * at : 4 * at + 4 : 2], carried[4 * at + 1 : 4 * at + 4 : 2]
+        if at:
+            other, _ = lax.optimization_barrier((other, sent[-1]))
+        other = [swap(half) for half in other]
+        rows = own[0].shape[0] // 2
+        sent.append(
+            [
+                (own[h][:rows].astype(F32) + other[h][:rows].astype(F32)).astype(BF16)
+                for h in (0, 1)
+            ]
+        )
+        kept.append([own[h][rows:].astype(F32) + other[h][rows:].astype(F32) for h in (0, 1)])
+    sent_sum = sent[0]
+    passed, whole = [], []
+    for at in range(group_count):
+        arrived = [plane_hop(sent[at][h], orders[h][0]) for h in (0, 1)]
+        summed = [kept[at][h] + arrived[h].astype(F32) for h in (0, 1)]
+        rows = summed[0].shape[0] // 2
+        passed.append([summed[h][rows:].astype(BF16) for h in (0, 1)])
+        whole.append([summed[h][:rows] for h in (0, 1)])
     routed_sum = 0.0
-    sent_sum = None
     for at, group in enumerate(back_groups):
-        own, other = carried[2 * at : 2 * at + 2]
-        if sent_sum is not None:
-            other, _ = lax.optimization_barrier((other, sent_sum))
-        other = swap(other)
-        half_sums = []
-        for half, (one, two) in enumerate(((1, 2), (2, 1))):
-            rows = own.shape[1] // 2
-            moved_sum = own[half, :rows].astype(F32) + other[half, :rows].astype(F32)
-            sent_sum = moved_sum.astype(BF16)
-            kept_sum = own[half, rows:].astype(F32) + other[half, rows:].astype(F32)
-            kept_sum = kept_sum + plane_hop(sent_sum, one).astype(F32)
-            rows = rows // 2
-            arrived = plane_hop(kept_sum[rows:].astype(BF16), two).astype(F32)
-            half_sums.append(kept_sum[:rows] + arrived)
-        plane_sum = jnp.concatenate(half_sums, axis=1).reshape(len(group), token_count, model_width)
+        moving = passed[at]
+        if at + 1 < group_count:
+            moving, _ = lax.optimization_barrier((moving, sent[at + 1]))
+        arrived = [plane_hop(moving[h], orders[h][1]) for h in (0, 1)]
+        plane_sum = [whole[at][h] + arrived[h].astype(F32) for h in (0, 1)]
+        plane_sum = jnp.concatenate(plane_sum, axis=1).reshape(len(group), token_count, model_width)
+        leaving = [plane_sum[place_at].astype(BF16) if k else None for place_at, k in enumerate(group)]
+        if at + 1 < group_count:
+            leaving, _ = lax.optimization_barrier((leaving, passed[at + 1]))
         for place_at, k in enumerate(group):
             if k:
-                routed_sum += line_hop(plane_sum[place_at].astype(BF16), k).astype(F32)
+                routed_sum += line_hop(leaving[place_at], k).astype(F32)
             else:
                 routed_sum += plane_sum[place_at]
 

time: 156 us -> 148 us (0.949)
  waiting for transfers between devices: 55.9 us -> 40.6 us
  other arithmetic: 8.72 us -> 12.1 us
  local copies, waits for them, and re-layouts: 14.6 us -> 17.8 us
  starting transfers between devices: 40.7 us -> 43.6 us
  Pallas kernels: 30.6 us -> 28.1 us
    ppermute x32 -> x37, waiting for transfers between devices: 55.9 us -> 40.6 us  [hop(): return lax.ppermute(value, axis, [(i, i ^ mask) for i in range(size)])]
    ppermute x32 -> x37, starting transfers between devices: 34.3 us -> 38.8 us  [hop(): return lax.ppermute(value, axis, [(i, i ^ mask) for i in range(size)])]
    convert_element_type x1 -> x2, other arithmetic: 1.64 us -> 4.1 us  [on_device(): (own[h][:rows].astype(F32) + other[h][:rows].astype(F32)).astype(BF16)]
    pallas_call x1, Pallas kernels: 8.33 us -> 6.52 us  [attend(): pl.pallas_call(functools.partial(attend_kernel, scale=QKD ** (-0.5)), gri...]
    unnamed x19 -> x51, local copies, waits for them, and re-layouts: 8.72 us -> 10.5 us
  transfers between devices with their start and end apart: 33 -> 38, of which waited for: 20 -> 19; matrix products, arithmetic and copies ran while one was open for 10% -> 17% of each run, Pallas kernels for 9% -> 8%
where the time goes in v4:
time: 148 us
  starting transfers between devices  43.6 us (29%)
  waiting for transfers between devices  40.6 us (27%)
  Pallas kernels  28.1 us (19%)
  local copies, waits for them, and re-layouts  17.8 us (12%)
  other arithmetic  12.1 us (8%)
  matrix products  4.96 us (3%)
    ppermute x37, waiting for transfers between devices, hop(): return lax.ppermute(value, axis, [(i, i ^ mask) for i in range(size)])  40.6 us
    ppermute x37, starting transfers between devices, hop(): return lax.ppermute(value, axis, [(i, i ^ mask) for i in range(size)])  38.8 us
    pallas_call x3, Pallas kernels, expert_rows(): pl.pallas_call(functools.partial(expert_kernel, blocks=blocks, heights=he...  16 us
    unnamed x51, local copies, waits for them, and re-layouts  10.5 us
    pallas_call x1, Pallas kernels, attend(): pl.pallas_call(functools.partial(attend_kernel, scale=QKD ** (-0.5)), gri...  6.52 us
    pallas_call x1, Pallas kernels, project(): pl.pallas_call(functools.partial(project_kernel, counts=counts, rows=rows...  5.6 us
    all_to_all x1, starting transfers between devices, on_device(): lax.all_to_all(residual_blocks, 'dev', split_axis=0, concat_axis=0, tiled...  4.8 us
    convert_element_type x2, other arithmetic, on_device(): (own[h][:rows].astype(F32) + other[h][:rows].astype(F32)).astype(BF16)  4.1 us
  transfers between devices with their start and end apart: 38, of which 19 were waited for; matrix products, arithmetic and copies ran while one was open for 17% of the time, Pallas kernels for 8%

profile of v4, /device:TPU:0, one launch (start us, length us, event | category | flops | bytes accessed | tf_op | source)
XLA Modules:
  0.0 147.9 jit_solution(6794664379067895644)
XLA Ops:
  2.1 6.5 %shard_map.109 = (bf16[16,32,512]{2,1,0:T(8,128)(2,1)S(1)}, bf16[16,32,512]{2,1,0:T(8,128)(2,1)S(1)}, f32[16,64,128]{2,1,0:T(8,128)S(1)}) custom-call(s32[17]{0:T(128)S(1)} %pad_add_fusion.length_ref, bf16[16,64,576]{2,1,0:T(8,128)(2,1)S(1)} %copy-done, bf16[16,576,384]{2,1,0:T(8,128)(2,1)} %bitcast.142), custom_call_target="tpu_custom_call" | custom-call | flops 905969664 | bytes 8257536 | tf_op jit(solution)/shard_map/pallas_call | solution.py:89
  11.4 3.3 %fusion = bf16[32,2,8,128]{3,2,1,0:T(8,128)(2,1)S(1)} fusion(bf16[32,512,128]{2,1,0:T(8,128)(2,1)} %param.14, bf16[16,32,512]{2,1,0:T(8,128)(2,1)S(1)} %add_convert_fusion), kind=kOutput, calls=%fused_computation.4 | convolution fusion | flops 67174400 | bytes 4849664 | tf_op jit(solution)/shard_map/rhc,hcv->rhv/dot_general | solution.py:482
  14.7 3.0 %collective-permute-start.2 = (bf16[16,4224]{1,0:T(8,128)(2,1)S(1)}, bf16[16,4224]{1,0:T(8,128)(2,1)S(1)}, u32[]{:S(2)}, u32[]{:S(2)}) collective-permute-start(bf16[16,4224]{1,0:T(8,128)(2,1)S(1)} %pad_maximum_fusion.9), channel_id=1, source_target_pairs={{0,4},{1,5},{2,6},{3,7},{4,0},{5,1},{6,2},{7,3},{8,12},{9,13},{10,... | collective-permute-start | bytes 405512 | tf_op jit(solution)/shard_map/ppermute | solution.py:18
  17.7 2.6 %collective-permute-start.5 = (bf16[16,4224]{1,0:T(8,128)(2,1)S(1)}, bf16[16,4224]{1,0:T(8,128)(2,1)S(1)}, u32[]{:S(2)}, u32[]{:S(2)}) collective-permute-start(bf16[16,4224]{1,0:T(8,128)(2,1)S(1)} %pad_maximum_fusion.9), channel_id=1, source_target_pairs={{0,8},{1,9},{2,10},{3,11},{4,12},{5,13},{6,14},{7,15},{8,0},{9,1},... | collective-permute-start | bytes 405512 | tf_op jit(solution)/shard_map/ppermute | solution.py:18
  20.3 4.6 %copy.58 = bf16[896,8,2,256]{3,1,2,0:T(8,128)(2,1)} copy(bf16[896,8,2,256]{3,2,1,0:T(2,128)(2,1)S(1)} %bitcast.141) | data formatting | bytes 14680064
  26.8 4.1 %collective-permute-done.5 = bf16[16,4224]{1,0:T(8,128)(2,1)S(1)} collective-permute-done((bf16[16,4224]{1,0:T(8,128)(2,1)S(1)}, bf16[16,4224]{1,0:T(8,128)(2,1)S(1)}, u32[]{:S(2)}, u32[]{:S(2)}) %collective-permute-start.5) | collective-permute-done | bytes 135200 | tf_op jit(solution)/shard_map/ppermute | solution.py:18
  37.5 1.9 %collective-permute-start.4 = (bf16[4,16,2176]{2,1,0:T(8,128)(2,1)S(1)}, bf16[4,16,2176]{2,1,0:T(8,128)(2,1)S(1)}, u32[]{:S(2)}, u32[]{:S(2)}) collective-permute-start(bf16[4,16,2176]{2,1,0:T(8,128)(2,1)S(1)} %pad_maximum_fusion.4), channel_id=1, source_target_pairs={{0,2},{1,3},{2,0},{3,1},{4,6},{5,7},{6,4},{7,5},{8,10},{9,11},{10,... | collective-permute-start | bytes 835592 | tf_op jit(solution)/shard_map/ppermute | solution.py:18
  45.5 4.8 %all-to-all-start = ((bf16[16,8,448]{2,1,0:T(8,128)(2,1)}), bf16[16,8,448]{2,1,0:T(8,128)(2,1)S(1)}, u32[]{:S(2)}, u32[]{:S(2)}) async-start(bf16[16,8,448]{2,1,0:T(8,128)(2,1)} %bitcast.134), calls=%async_computation | async-start | bytes 262144 | tf_op jit(solution)/shard_map/all_to_all | solution.py:507
  52.6 5.6 %shard_map.110 = (f32[448,128]{1,0:T(8,128)}, bf16[448,128]{1,0:T(8,128)(2,1)}) custom-call(s32[33]{0:T(128)} %stack.363.place_ref, bf16[2,16,2176]{2,1,0:T(8,128)(2,1)} %copy-done.3, bf16[2,16,2176]{2,1,0:T(8,128)(2,1)} %copy-done.11, bf16[4,16,2176]{2,1,0:T(8,128)(2,1)} %copy-done.15, bf16[2,16,2176]{2,1,0:T(8,128)(2,1)} %copy-done.4, ...), custom_call_target="tpu_custom_call" | custom-call | flops 939524096 | bytes 5767168 | tf_op jit(solution)/shard_map/pallas_call | solution.py:182
  60.9 2.0 %collective-permute-start.14 = (bf16[448,128]{1,0:T(8,128)(2,1)S(1)}, bf16[448,128]{1,0:T(8,128)(2,1)S(1)}, u32[]{:S(2)}, u32[]{:S(2)}) collective-permute-start(bf16[448,128]{1,0:T(8,128)(2,1)S(1)} %fusion.15), channel_id=1, source_target_pairs={{0,4},{1,5},{2,6},{3,7},{4,0},{5,1},{6,2},{7,3},{8,12},{9,13},{10,... | collective-permute-start | bytes 344072 | tf_op jit(solution)/shard_map/ppermute | solution.py:18
  62.9 2.4 %collective-permute-start.15 = (bf16[448,128]{1,0:T(8,128)(2,1)S(1)}, bf16[448,128]{1,0:T(8,128)(2,1)S(1)}, u32[]{:S(2)}, u32[]{:S(2)}) collective-permute-start(bf16[448,128]{1,0:T(8,128)(2,1)S(1)} %fusion.15), channel_id=1, source_target_pairs={{0,8},{1,9},{2,10},{3,11},{4,12},{5,13},{6,14},{7,15},{8,0},{9,1},... | collective-permute-start | bytes 344072 | tf_op jit(solution)/shard_map/ppermute | solution.py:18
  68.6 6.1 %collective-permute-done.15 = bf16[448,128]{1,0:T(8,128)(2,1)S(1)} collective-permute-done((bf16[448,128]{1,0:T(8,128)(2,1)S(1)}, bf16[448,128]{1,0:T(8,128)(2,1)S(1)}, u32[]{:S(2)}, u32[]{:S(2)}) %collective-permute-start.15) | collective-permute-done | bytes 114720 | tf_op jit(solution)/shard_map/ppermute | solution.py:18
  77.9 3.1 %collective-permute-done.18.refs_0_ = bf16[4,224,128]{2,1,0:T(8,128)(2,1)S(1)} collective-permute-done((bf16[4,224,128]{2,1,0:T(8,128)(2,1)S(1)}, bf16[4,224,128]{2,1,0:T(8,128)(2,1)S(1)}, u32[]{:S(2)}, u32[]{:S(2)}) %collective-permute-start.18) | collective-permute-done | bytes 229408 | tf_op jit(solution)/shard_map/ppermute | solution.py:18
  86.2 3.4 %shard_map.111 = (f32[256,512]{1,0:T(8,128)S(1)}, f32[8,256]{1,0:T(8,128)S(1)}) custom-call(s32[16]{0:T(128)S(1)} %stack.410.place_ref, bf16[4,224,128]{2,1,0:T(8,128)(2,1)S(1)} %get-tuple-element.83.refs_0_, bf16[4,224,128]{2,1,0:T(8,128)(2,1)S(1)} %get-tuple-element.86.refs_1_, bf16[4,224,128]{2,1,0:T(8,128)(2,1)S(1)} %collective-permute-done.24.refs_2_, ...), custom_call_target="tpu_custom_call" | custom-call | flops 469762048 | bytes 2752512 | tf_op jit(solution)/shard_map/pallas_call | solution.py:389
  89.6 3.5 %shard_map.112 = (f32[256,512]{1,0:T(8,128)S(1)}, f32[8,256]{1,0:T(8,128)S(1)}) custom-call(s32[16]{0:T(128)S(1)} %stack.401.place_ref, bf16[4,224,128]{2,1,0:T(8,128)(2,1)S(1)} %collective-permute-done.18.refs_0_, bf16[4,224,128]{2,1,0:T(8,128)(2,1)S(1)} %collective-permute-done.19.refs_1_, bf16[4,224,128]{2,1,0:T(8,128)(2,1)S(1)} %collective-permute-done.22.refs_2_, ...), custom_call_target="tpu_custom_call" | custom-call | flops 469762048 | bytes 2752512 | tf_op jit(solution)/shard_map/pallas_call | solution.py:389
  96.3 9.1 %shard_map.113 = (bf16[128,3584]{1,0:T(8,128)(2,1)}, bf16[128,3584]{1,0:T(8,128)(2,1)}, bf16[128,3584]{1,0:T(8,128)(2,1)}, bf16[128,3584]{1,0:T(8,128)(2,1)}) custom-call(s32[48]{0:T(128)S(1)} %stack.392.place_ref, bf16[8,224,128]{2,1,0:T(8,128)(2,1)S(1)} %collective-permute-done.20.refs_0_, bf16[8,224,128]{2,1,0:T(8,128)(2,1)S(1)} %collective-permute-done.21.refs_1_, ...), custom_call_target="tpu_custom_call" | custom-call | flops 939524096 | bytes 5505024 | tf_op jit(solution)/shard_map/pallas_call | solution.py:389
  106.3 2.0 %collective-permute-done.29 = bf16[128,3584]{1,0:T(8,128)(2,1)S(1)} collective-permute-done((bf16[128,3584]{1,0:T(8,128)(2,1)}, bf16[128,3584]{1,0:T(8,128)(2,1)S(1)}, u32[]{:S(2)}, u32[]{:S(2)}) %collective-permute-start.29) | collective-permute-done | bytes 917536 | tf_op jit(solution)/shard_map/ppermute | solution.py:18
  109.2 1.9 %add_convert_fusion.1 = bf16[64,3584]{1,0:T(8,128)(2,1)} fusion(bf16[128,3584]{1,0:T(8,128)(2,1)S(1)} %collective-permute-done.29, bf16[128,3584]{1,0:T(8,128)(2,1)} %get-tuple-element.81), kind=kLoop, calls=%fused_computation.18 | loop fusion | flops 917504 | bytes 1376256 | tf_op jit(solution)/shard_map/convert_element_type | solution.py:589
  111.6 2.2 %add_convert_fusion.2 = bf16[64,3584]{1,0:T(8,128)(2,1)} fusion(bf16[128,3584]{1,0:T(8,128)(2,1)S(1)} %collective-permute-done.28, bf16[128,3584]{1,0:T(8,128)(2,1)} %get-tuple-element.79), kind=kLoop, calls=%fused_computation.19 | loop fusion | flops 917504 | bytes 1376256 | tf_op jit(solution)/shard_map/convert_element_type | solution.py:589
  119.4 4.6 %collective-permute-done.32 = bf16[64,3584]{1,0:T(8,128)(2,1)} collective-permute-done((bf16[64,3584]{1,0:T(8,128)(2,1)}, bf16[64,3584]{1,0:T(8,128)(2,1)}, u32[]{:S(2)}, u32[]{:S(2)}) %collective-permute-start.32) | collective-permute-done | bytes 458784 | tf_op jit(solution)/shard_map/ppermute | solution.py:18
  129.1 3.2 %collective-permute-done.33 = bf16[32,3584]{1,0:T(8,128)(2,1)S(1)} collective-permute-done((bf16[32,3584]{1,0:T(8,128)(2,1)S(1)}, bf16[32,3584]{1,0:T(8,128)(2,1)S(1)}, u32[]{:S(2)}, u32[]{:S(2)}) %collective-permute-start.33) | collective-permute-done | bytes 229408 | tf_op jit(solution)/shard_map/ppermute | solution.py:18
  132.4 2.7 %collective-permute-done.31 = bf16[32,3584]{1,0:T(8,128)(2,1)S(1)} collective-permute-done((bf16[32,3584]{1,0:T(8,128)(2,1)S(1)}, bf16[32,3584]{1,0:T(8,128)(2,1)S(1)}, u32[]{:S(2)}, u32[]{:S(2)}) %collective-permute-start.31) | collective-permute-done | bytes 229408 | tf_op jit(solution)/shard_map/ppermute | solution.py:18
  135.2 2.0 %collective-permute-start.34 = (bf16[8,7168]{1,0:T(8,128)(2,1)S(1)}, bf16[8,7168]{1,0:T(8,128)(2,1)S(1)}, u32[]{:S(2)}, u32[]{:S(2)}) collective-permute-start(bf16[8,7168]{1,0:T(8,128)(2,1)S(1)} %get-tuple-element.93), channel_id=1, source_target_pairs={{0,4},{1,5},{2,6},{3,7},{4,0},{5,1},{6,2},{7,3},{8,12},{9,13},{10,... | collective-permute-start | bytes 344072 | tf_op jit(solution)/shard_map/ppermute | solution.py:18
  140.8 6.4 %collective-permute-done.35 = bf16[8,7168]{1,0:T(8,128)(2,1)S(1)} collective-permute-done((bf16[8,7168]{1,0:T(8,128)(2,1)S(1)}, bf16[8,7168]{1,0:T(8,128)(2,1)S(1)}, u32[]{:S(2)}, u32[]{:S(2)}) %collective-permute-start.35) | collective-permute-done | bytes 114720 | tf_op jit(solution)/shard_map/ppermute | solution.py:18
  (188 shorter events, 56.2 us)
Async XLA Ops:
  14.7 10.2 %collective-permute-start.2 = (bf16[16,4224]{1,0:T(8,128)(2,1)S(1)}, bf16[16,4224]{1,0:T(8,128)(2,1)S(1)}, u32[]{:S(2)}, u32[]{:S(2)}) collective-permute-start(bf16[16,4224]{1,0:T(8,128)(2,1)S(1)} %pad_maximum_fusion.9), channel_id=1, source_target_pairs={{0,4},{1,5},{2,6},{3,7},{4,0},{5,1},{6,2},{7,3},{8,12},{9,13},{10,... | collective-permute-start | bytes 405512 | tf_op jit(solution)/shard_map/ppermute | solution.py:18
  17.7 13.2 %collective-permute-start.5 = (bf16[16,4224]{1,0:T(8,128)(2,1)S(1)}, bf16[16,4224]{1,0:T(8,128)(2,1)S(1)}, u32[]{:S(2)}, u32[]{:S(2)}) collective-permute-start(bf16[16,4224]{1,0:T(8,128)(2,1)S(1)} %pad_maximum_fusion.9), channel_id=1, source_target_pairs={{0,8},{1,9},{2,10},{3,11},{4,12},{5,13},{6,14},{7,15},{8,0},{9,1},... | collective-permute-start | bytes 405512 | tf_op jit(solution)/shard_map/ppermute | solution.py:18
  20.3 10.6 %collective-permute-start.6 = (bf16[16,4224]{1,0:T(8,128)(2,1)S(1)}, bf16[16,4224]{1,0:T(8,128)(2,1)S(1)}, u32[]{:S(2)}, u32[]{:S(2)}) collective-permute-start(bf16[16,4224]{1,0:T(8,128)(2,1)S(1)} %pad_maximum_fusion.9), channel_id=1, source_target_pairs={{0,12},{1,13},{2,14},{3,15},{4,8},{5,9},{6,10},{7,11},{8,4},{9,5},... | collective-permute-start | bytes 405512 | tf_op jit(solution)/shard_map/ppermute | solution.py:18
  25.0 10.3 %collective-permute-start.10 = (bf16[2,16,2048]{2,1,0:T(8,128)(2,1)S(1)}, bf16[2,16,2048]{2,1,0:T(8,128)(2,1)S(1)}, u32[]{:S(2)}, u32[]{:S(2)}) collective-permute-start(bf16[2,16,2048]{2,1,0:T(8,128)(2,1)S(1)} %fusion.17.refs_6_), channel_id=1, source_target_pairs={{0,2},{1,3},{2,0},{3,1},{4,6},{5,7},{6,4},{7,5},{8,10},{9,11},{10,... | collective-permute-start | bytes 393224 | tf_op jit(solution)/shard_map/ppermute | solution.py:18
  31.0 6.4 %collective-permute-start.3 = (bf16[2,16,2176]{2,1,0:T(8,128)(2,1)S(1)}, bf16[2,16,2176]{2,1,0:T(8,128)(2,1)S(1)}, u32[]{:S(2)}, u32[]{:S(2)}) collective-permute-start(bf16[2,16,2176]{2,1,0:T(8,128)(2,1)S(1)} %fusion.16.refs_0_), channel_id=1, source_target_pairs={{0,1},{1,0},{2,3},{3,2},{4,5},{5,4},{6,7},{7,6},{8,9},{9,8},{10,11... | collective-permute-start | bytes 417800 | tf_op jit(solution)/shard_map/ppermute | solution.py:18
  32.6 7.8 %collective-permute-start.7 = (bf16[2,16,2176]{2,1,0:T(8,128)(2,1)S(1)}, bf16[2,16,2176]{2,1,0:T(8,128)(2,1)S(1)}, u32[]{:S(2)}, u32[]{:S(2)}) collective-permute-start(bf16[2,16,2176]{2,1,0:T(8,128)(2,1)S(1)} %slice.135.refs_3_), channel_id=1, source_target_pairs={{0,1},{1,0},{2,3},{3,2},{4,5},{5,4},{6,7},{7,6},{8,9},{9,8},{10,11... | collective-permute-start | bytes 417800 | tf_op jit(solution)/shard_map/ppermute | solution.py:18
  33.1 6.4 %collective-permute-start.8 = (bf16[2,16,2048]{2,1,0:T(8,128)(2,1)S(1)}, bf16[2,16,2048]{2,1,0:T(8,128)(2,1)S(1)}, u32[]{:S(2)}, u32[]{:S(2)}) collective-permute-start(bf16[2,16,2048]{2,1,0:T(8,128)(2,1)S(1)} %slice.136.refs_9_), channel_id=1, source_target_pairs={{0,2},{1,3},{2,0},{3,1},{4,6},{5,7},{6,4},{7,5},{8,10},{9,11},{10,... | collective-permute-start | bytes 393224 | tf_op jit(solution)/shard_map/ppermute | solution.py:18
  35.3 16.3 %collective-permute-start.11 = (bf16[4,16,2048]{2,1,0:T(8,128)(2,1)S(1)}, bf16[4,16,2048]{2,1,0:T(8,128)(2,1)S(1)}, u32[]{:S(2)}, u32[]{:S(2)}) collective-permute-start(bf16[4,16,2048]{2,1,0:T(8,128)(2,1)S(1)} %pad_maximum_fusion.7), channel_id=1, source_target_pairs={{0,1},{1,0},{2,3},{3,2},{4,5},{5,4},{6,7},{7,6},{8,9},{9,8},{10,11... | collective-permute-start | bytes 786440 | tf_op jit(solution)/shard_map/ppermute | solution.py:18
  37.5 13.4 %collective-permute-start.4 = (bf16[4,16,2176]{2,1,0:T(8,128)(2,1)S(1)}, bf16[4,16,2176]{2,1,0:T(8,128)(2,1)S(1)}, u32[]{:S(2)}, u32[]{:S(2)}) collective-permute-start(bf16[4,16,2176]{2,1,0:T(8,128)(2,1)S(1)} %pad_maximum_fusion.4), channel_id=1, source_target_pairs={{0,2},{1,3},{2,0},{3,1},{4,6},{5,7},{6,4},{7,5},{8,10},{9,11},{10,... | collective-permute-start | bytes 835592 | tf_op jit(solution)/shard_map/ppermute | solution.py:18
  40.4 11.1 %collective-permute-start.9 = (bf16[4,16,2176]{2,1,0:T(8,128)(2,1)S(1)}, bf16[4,16,2176]{2,1,0:T(8,128)(2,1)S(1)}, u32[]{:S(2)}, u32[]{:S(2)}) collective-permute-start(bf16[4,16,2176]{2,1,0:T(8,128)(2,1)S(1)} %pad_maximum_fusion.5), channel_id=1, source_target_pairs={{0,2},{1,3},{2,0},{3,1},{4,6},{5,7},{6,4},{7,5},{8,10},{9,11},{10,... | collective-permute-start | bytes 835592 | tf_op jit(solution)/shard_map/ppermute | solution.py:18
  43.1 8.5 %collective-permute-start.12 = (bf16[4,16,2048]{2,1,0:T(8,128)(2,1)}, bf16[4,16,2048]{2,1,0:T(8,128)(2,1)S(1)}, u32[]{:S(2)}, u32[]{:S(2)}) collective-permute-start(bf16[4,16,2048]{2,1,0:T(8,128)(2,1)} %pad_maximum_fusion.8), channel_id=1, source_target_pairs={{0,1},{1,0},{2,3},{3,2},{4,5},{5,4},{6,7},{7,6},{8,9},{9,8},{10,11... | collective-permute-start | bytes 786440 | tf_op jit(solution)/shard_map/ppermute | solution.py:18
  45.5 12.7 %all-to-all-start = ((bf16[16,8,448]{2,1,0:T(8,128)(2,1)}), bf16[16,8,448]{2,1,0:T(8,128)(2,1)S(1)}, u32[]{:S(2)}, u32[]{:S(2)}) async-start(bf16[16,8,448]{2,1,0:T(8,128)(2,1)} %bitcast.134), calls=%async_computation | async-start | bytes 262144 | tf_op jit(solution)/shard_map/all_to_all | solution.py:507
  60.9 7.7 %collective-permute-start.14 = (bf16[448,128]{1,0:T(8,128)(2,1)S(1)}, bf16[448,128]{1,0:T(8,128)(2,1)S(1)}, u32[]{:S(2)}, u32[]{:S(2)}) collective-permute-start(bf16[448,128]{1,0:T(8,128)(2,1)S(1)} %fusion.15), channel_id=1, source_target_pairs={{0,4},{1,5},{2,6},{3,7},{4,0},{5,1},{6,2},{7,3},{8,12},{9,13},{10,... | collective-permute-start | bytes 344072 | tf_op jit(solution)/shard_map/ppermute | solution.py:18
  62.9 11.8 %collective-permute-start.15 = (bf16[448,128]{1,0:T(8,128)(2,1)S(1)}, bf16[448,128]{1,0:T(8,128)(2,1)S(1)}, u32[]{:S(2)}, u32[]{:S(2)}) collective-permute-start(bf16[448,128]{1,0:T(8,128)(2,1)S(1)} %fusion.15), channel_id=1, source_target_pairs={{0,8},{1,9},{2,10},{3,11},{4,12},{5,13},{6,14},{7,15},{8,0},{9,1},... | collective-permute-start | bytes 344072 | tf_op jit(solution)/shard_map/ppermute | solution.py:18
  65.3 9.5 %collective-permute-start.16 = (bf16[448,128]{1,0:T(8,128)(2,1)S(1)}, bf16[448,128]{1,0:T(8,128)(2,1)S(1)}, u32[]{:S(2)}, u32[]{:S(2)}) collective-permute-start(bf16[448,128]{1,0:T(8,128)(2,1)S(1)} %fusion.15), channel_id=1, source_target_pairs={{0,12},{1,13},{2,14},{3,15},{4,8},{5,9},{6,10},{7,11},{8,4},{9,5},... | collective-permute-start | bytes 344072 | tf_op jit(solution)/shard_map/ppermute | solution.py:18
  77.9 7.6 %collective-permute-start.24 = (bf16[4,224,128]{2,1,0:T(8,128)(2,1)S(1)}, bf16[4,224,128]{2,1,0:T(8,128)(2,1)S(1)}, u32[]{:S(2)}, u32[]{:S(2)}) collective-permute-start(bf16[4,224,128]{2,1,0:T(8,128)(2,1)S(1)} %get-tuple-element.83.refs_0_), channel_id=1, source_target_pairs={{0,16},{16,0},{1,17},{17,1},{2,18},{18,2},{3,19},{19,3},{4,20},{20... | collective-permute-start | bytes 688136 | tf_op jit(solution)/shard_map/ppermute | solution.py:18
  82.7 11.1 %collective-permute-start.21 = (bf16[8,224,128]{2,1,0:T(8,128)(2,1)S(1)}, bf16[8,224,128]{2,1,0:T(8,128)(2,1)S(1)}, u32[]{:S(2)}, u32[]{:S(2)}) collective-permute-start(bf16[8,224,128]{2,1,0:T(8,128)(2,1)S(1)} %pad_maximum_fusion.3), channel_id=1, source_target_pairs={{0,1},{1,0},{2,3},{3,2},{4,5},{5,4},{6,7},{7,6},{8,9},{9,8},{10,11... | collective-permute-start | bytes 1376264 | tf_op jit(solution)/shard_map/ppermute | solution.py:18
  83.1 10.7 %collective-permute-start.20 = (bf16[8,224,128]{2,1,0:T(8,128)(2,1)S(1)}, bf16[8,224,128]{2,1,0:T(8,128)(2,1)S(1)}, u32[]{:S(2)}, u32[]{:S(2)}) collective-permute-start(bf16[8,224,128]{2,1,0:T(8,128)(2,1)S(1)} %pad_maximum_fusion.2), channel_id=1, source_target_pairs={{0,2},{1,3},{2,0},{3,1},{4,6},{5,7},{6,4},{7,5},{8,10},{9,11},{10,... | collective-permute-start | bytes 1376264 | tf_op jit(solution)/shard_map/ppermute | solution.py:18
  111.1 12.9 %collective-permute-start.32 = (bf16[64,3584]{1,0:T(8,128)(2,1)}, bf16[64,3584]{1,0:T(8,128)(2,1)}, u32[]{:S(2)}, u32[]{:S(2)}) collective-permute-start(bf16[64,3584]{1,0:T(8,128)(2,1)} %add_convert_fusion.1), channel_id=1, source_target_pairs={{0,2},{1,3},{2,0},{3,1},{4,6},{5,7},{6,4},{7,5},{8,10},{9,11},{10,... | collective-permute-start | bytes 1376264 | tf_op jit(solution)/shard_map/ppermute | solution.py:18
  113.8 13.4 %collective-permute-start.30 = (bf16[64,3584]{1,0:T(8,128)(2,1)}, bf16[64,3584]{1,0:T(8,128)(2,1)S(1)}, u32[]{:S(2)}, u32[]{:S(2)}) collective-permute-start(bf16[64,3584]{1,0:T(8,128)(2,1)} %add_convert_fusion.2), channel_id=1, source_target_pairs={{0,1},{1,0},{2,3},{3,2},{4,5},{5,4},{6,7},{7,6},{8,9},{9,8},{10,11... | collective-permute-start | bytes 1376264 | tf_op jit(solution)/shard_map/ppermute | solution.py:18
  125.4 6.9 %collective-permute-start.33 = (bf16[32,3584]{1,0:T(8,128)(2,1)S(1)}, bf16[32,3584]{1,0:T(8,128)(2,1)S(1)}, u32[]{:S(2)}, u32[]{:S(2)}) collective-permute-start(bf16[32,3584]{1,0:T(8,128)(2,1)S(1)} %slice.240), channel_id=1, source_target_pairs={{0,1},{1,0},{2,3},{3,2},{4,5},{5,4},{6,7},{7,6},{8,9},{9,8},{10,11... | collective-permute-start | bytes 688136 | tf_op jit(solution)/shard_map/ppermute | solution.py:18
  128.4 6.6 %collective-permute-start.31 = (bf16[32,3584]{1,0:T(8,128)(2,1)S(1)}, bf16[32,3584]{1,0:T(8,128)(2,1)S(1)}, u32[]{:S(2)}, u32[]{:S(2)}) collective-permute-start(bf16[32,3584]{1,0:T(8,128)(2,1)S(1)} %slice.241), channel_id=1, source_target_pairs={{0,2},{1,3},{2,0},{3,1},{4,6},{5,7},{6,4},{7,5},{8,10},{9,11},{10,... | collective-permute-start | bytes 688136 | tf_op jit(solution)/shard_map/ppermute | solution.py:18
  137.2 9.9 %collective-permute-start.35 = (bf16[8,7168]{1,0:T(8,128)(2,1)S(1)}, bf16[8,7168]{1,0:T(8,128)(2,1)S(1)}, u32[]{:S(2)}, u32[]{:S(2)}) collective-permute-start(bf16[8,7168]{1,0:T(8,128)(2,1)S(1)} %get-tuple-element.95), channel_id=1, source_target_pairs={{0,8},{1,9},{2,10},{3,11},{4,12},{5,13},{6,14},{7,15},{8,0},{9,1},... | collective-permute-start | bytes 344072 | tf_op jit(solution)/shard_map/ppermute | solution.py:18
  138.2 9.0 %collective-permute-start.36 = (bf16[8,7168]{1,0:T(8,128)(2,1)S(1)}, bf16[8,7168]{1,0:T(8,128)(2,1)S(1)}, u32[]{:S(2)}, u32[]{:S(2)}) collective-permute-start(bf16[8,7168]{1,0:T(8,128)(2,1)S(1)} %get-tuple-element.94), channel_id=1, source_target_pairs={{0,12},{1,13},{2,14},{3,15},{4,8},{5,9},{6,10},{7,11},{8,4},{9,5},... | collective-permute-start | bytes 344072 | tf_op jit(solution)/shard_map/ppermute | solution.py:18
  (37 other events, 294.7 us)

commit v5 on v4

--- a/solution.py
+++ b/solution.py
@@ -44,13 +44,15 @@
     return halves, beside, after
 
 
-def attend_kernel(length_ref, query_ref, cache_ref, own_ref, other_ref, stats_ref, latents, *, scale):
+def attend_kernel(
+    length_ref, side_ref, query_ref, cache_ref, own_ref, other_ref, stats_ref, latents, *, scale
+):
     group, heads, _ = query_ref.shape
     latent_width = own_ref.shape[2]
     slots = cache_ref.shape[2]
     half = heads // 2
     first = pl.program_id(0) * group
-    side = length_ref[length_ref.shape[0] - 1]
+    side = side_ref[0]
     positions = side * slots + lax.broadcasted_iota(jnp.int32, (heads, slots), 1)
     lanes = lax.broadcasted_iota(jnp.int32, (heads, stats_ref.shape[2]), 1)
     everyone = range(group)
@@ -85,20 +87,19 @@
     requests, heads, width = queries.shape
     slots = cache_columns.shape[2]
     group = 4
-    table = jnp.concatenate([lengths, side.reshape(1)]).astype(jnp.int32)
     return pl.pallas_call(
         functools.partial(attend_kernel, scale=QKD ** (-0.5)),
         grid_spec=pltpu.PrefetchScalarGridSpec(
-            num_scalar_prefetch=1,
+            num_scalar_prefetch=2,
             grid=(requests // group,),
             in_specs=[
-                pl.BlockSpec((group, heads, width), lambda r, table: (r, 0, 0)),
-                pl.BlockSpec((group, width, slots), lambda r, table: (r, 0, 0)),
+                pl.BlockSpec((group, heads, width), lambda r, lengths, side: (r, 0, 0)),
+                pl.BlockSpec((group, width, slots), lambda r, lengths, side: (r, 0, 0)),
             ],
             out_specs=[
-                pl.BlockSpec((group, heads // 2, latent_width), lambda r, table: (r, 0, 0)),
-                pl.BlockSpec((group, heads // 2, latent_width), lambda r, table: (r, 0, 0)),
-                pl.BlockSpec((group, heads, 128), lambda r, table: (r, 0, 0)),
+                pl.BlockSpec((group, heads // 2, latent_width), lambda r, lengths, side: (r, 0, 0)),
+                pl.BlockSpec((group, heads // 2, latent_width), lambda r, lengths, side: (r, 0, 0)),
+                pl.BlockSpec((group, heads, 128), lambda r, lengths, side: (r, 0, 0)),
             ],
             scratch_shapes=[pltpu.VMEM((group, heads, latent_width), F32)],
         ),
@@ -113,7 +114,7 @@
             bytes_accessed=2 * requests * width * (heads + slots),
             transcendentals=requests * heads * slots,
         ),
-    )(table, queries, cache_columns)
+    )(lengths, side.reshape(1), queries, cache_columns)
 
 
 def project_kernel(place_ref, *refs, counts, rows, depths, steps):
@@ -213,10 +214,18 @@
     sums_in, refs = refs[: 2 * carried], refs[2 * carried :]
     if sizes:
         gate_ref, down_ref, *refs = refs
-        outs, refs = refs[: 4 * len(sizes[2])], refs[4 * len(sizes[2]) :]
+        activated, outs, refs = refs[0], refs[1:5], refs[5:]
         total, squares, weights, rows, arrived, part_arrived = refs[:6]
-        activated, results, down, down_arrived, sent = refs[6:]
-        down_copy = pltpu.make_async_copy(down_ref, down, down_arrived)
+        results, down, down_arrived, sent = refs[6:]
+        width = down.shape[1] // 2
+        down_copies = []
+        for half in (0, 1):
+            columns = pl.ds(half * width, width)
+            down_copies.append(
+                pltpu.make_async_copy(
+                    down_ref.at[:, columns], down.at[:, columns], down_arrived.at[half]
+                )
+            )
     else:
         total, squares, weights, rows, arrived, part_arrived = refs
     lanes = rows.shape[1] // 2
@@ -245,7 +254,8 @@
     for copy in part_copies + weight_copies:
         copy.start()
     if sizes:
-        down_copy.start()
+        for copy in down_copies:
+            copy.start()
     if sums_in:
         squares[...] = sums_in[1][...]
     else:
@@ -291,8 +301,7 @@
     up_part = total[:, units:] * level
     raised = gate_part / (1.0 + jnp.exp(-gate_part))
     total[:, :units] = raised * up_part * gate_ref[...]
-    owner_rows, moved, groups = sizes
-    line = sum(len(group) for group in groups)
+    owner_rows, _ = sizes
     side_rows = total.shape[0] // 2
     order_at = 2 * len(spots)
     for first_row in (0, side_rows):
@@ -304,46 +313,78 @@
                 pieces.append(total[pl.ds(row, owner_rows), :units])
             row = first_row + 2 * pair * owner_rows
             activated[row : row + 2 * owner_rows, :] = jnp.concatenate(pieces).astype(BF16)
-    down_copy.wait()
+    lower(activated, down, results, outs, sent, down_copies, sizes, False)
+
+
+def lower_kernel(activated_ref, down_ref, *refs, sizes, kept):
+    outs, (results, down, arrived, sent) = refs[:4], refs[4:]
+    copies = []
+    width = down.shape[1] // 2
+    for half in (0, 1):
+        columns = pl.ds(half * width, width)
+        copies.append(
+            pltpu.make_async_copy(down_ref.at[:, columns], down.at[:, columns], arrived.at[half])
+        )
+        copies[-1].start()
+    lower(activated_ref, down, results, outs, sent, copies, sizes, kept)
+
+
+def lower(activated, down, results, outs, sent, arrivals, sizes, kept):
+    _, moved = sizes
     width = down.shape[1] // 2
     tile = 512
+    side_rows = activated.shape[0] // 2
     plane_rows = side_rows // 4
     copies = []
     for half in (0, 1):
-        order = [*moved[half], *(group for group in range(4) if group not in moved[half])]
+        order = [at for at in range(4) if (at in moved[half]) != kept]
+        rows = [
+            activated[side * side_rows + at * plane_rows : side * side_rows + (at + 1) * plane_rows, :]
+            for side in (1, 0)
+            for at in order
+        ]
+        rows = jnp.concatenate(rows)
+        arrivals[half].wait()
         for column in range(0, width, tile):
-            product = jnp.dot(
-                activated[...],
+            results[half, :, column : column + tile] = jnp.dot(
+                rows,
                 down[:, half * width + column : half * width + column + tile],
                 preferred_element_type=F32,
             ).astype(BF16)
-            for side in (0, 1):
-                source = 0
-                for group in groups:
-                    for place, at in enumerate(order):
-                        size = len(group) * owner_rows
-                        row = side * side_rows + at * plane_rows + source
-                        target = half * 2 * side_rows + side * side_rows + 4 * source + place * size
-                        results[target : target + size, column : column + tile] = product[
-                            row : row + size, :
-                        ]
-                    source += size
-        for side in (1, 0):
-            source = 0
-            for which, group in enumerate(groups):
-                size = 4 * len(group) * owner_rows
-                target = half * 2 * side_rows + side * side_rows + 4 * source
-                copies.append(
-                    pltpu.make_async_copy(
-                        results.at[pl.ds(target, size)],
-                        outs[4 * which + 2 * half + side],
-                        sent.at[len(copies)],
-                    )
+        for at, side in enumerate((1, 0)):
+            copies.append(
+                pltpu.make_async_copy(
+                    results.at[half, pl.ds(at * 2 * plane_rows, 2 * plane_rows)],
+                    outs[2 * half + side],
+                    sent.at[len(copies)],
                 )
-                copies[-1].start()
-                source += len(group) * owner_rows
+            )
+            copies[-1].start()
     for copy in copies:
         copy.wait()
+
+
+def lower_kept(activated, down, sizes):
+    tokens, units = activated.shape
+    anywhere = pl.BlockSpec(memory_space=pl.ANY)
+    return pl.pallas_call(
+        functools.partial(lower_kernel, sizes=sizes, kept=True),
+        in_specs=[pl.BlockSpec(memory_space=pltpu.VMEM), anywhere],
+        out_specs=[anywhere] * 4,
+        out_shape=[jax.ShapeDtypeStruct((tokens // 4, down.shape[1] // 2), BF16)] * 4,
+        scratch_shapes=[
+            pltpu.VMEM((2, tokens // 2, down.shape[1] // 2), BF16),
+            pltpu.VMEM(down.shape, BF16),
+            pltpu.SemaphoreType.DMA((2,)),
+            pltpu.SemaphoreType.DMA((4,)),
+        ],
+        compiler_params=pltpu.CompilerParams(vmem_limit_bytes=LAST_VMEM_LIMIT),
+        cost_estimate=pl.CostEstimate(
+            flops=tokens * units * down.shape[1],
+            bytes_accessed=2 * down.shape[1] * (units + tokens // 2),
+            transcendentals=0,
+        ),
+    )(activated, down)
 
 
 def expert_rows(parts, other_parts, halves, gains, weights, place, carried, finish):
@@ -371,20 +412,15 @@
         gates, down, *sizes = finish
         operands += [gates, down]
         in_specs += [whole, anywhere]
-        owner_rows, _, groups = sizes
-        out_shape = [
-            jax.ShapeDtypeStruct((4 * len(group) * owner_rows, model_width // 2), BF16)
-            for group in groups
-            for _ in range(4)
-        ]
-        out_specs = [anywhere] * len(out_shape)
+        out_shape = [jax.ShapeDtypeStruct((tokens, double // 2), BF16)]
+        out_shape += [jax.ShapeDtypeStruct((tokens // 4, model_width // 2), BF16)] * 4
+        out_specs = [whole] + [anywhere] * 4
         scratch = [pltpu.VMEM(a.shape, F32) for a in sums] + scratch
         scratch += [
-            pltpu.VMEM((tokens, double // 2), BF16),
-            pltpu.VMEM((2 * tokens, model_width // 2), BF16),
+            pltpu.VMEM((2, tokens // 2, model_width // 2), BF16),
             pltpu.VMEM(down.shape, BF16),
-            pltpu.SemaphoreType.DMA,
-            pltpu.SemaphoreType.DMA((len(out_shape),)),
+            pltpu.SemaphoreType.DMA((2,)),
+            pltpu.SemaphoreType.DMA((4,)),
         ]
     return pl.pallas_call(
         functools.partial(
@@ -535,7 +571,6 @@
     first_rows = -(-columns // 32) * 16
     gains = norm_gain.astype(F32).reshape(chips, columns)
     gains = [gains[:, :first_rows], gains[:, first_rows:]]
-    back_groups = [list(range(line))]
     hidden_groups = [list(range(line))]
     (first, second), gates, _ = gather(
         hidden,
@@ -563,7 +598,7 @@
         table += [spot for spot, _ in spots]
         if last:
             parts, carried = lax.optimization_barrier((parts, carried))
-            table += placed((p, k) for p in range(plane) for g in back_groups for k in g)
+            table += placed((p, k) for p in range(plane) for k in range(line))
         carried = expert_rows(
             parts,
             [swap(part) for part in parts],
@@ -572,49 +607,27 @@
             in_rows,
             jnp.stack(table).astype(jnp.int32),
             carried,
-            (gates, down, token_count, moved, back_groups) if last else None,
-        )
-
-    orders = ((1, 2), (2, 1))
-    group_count = len(back_groups)
-    kept, sent = [], []
-    for at in range(group_count):
-        own, other = carried[4 * at : 4 * at + 4 : 2], carried[4 * at + 1 : 4 * at + 4 : 2]
-        if at:
-            other, _ = lax.optimization_barrier((other, sent[-1]))
-        other = [swap(half) for half in other]
-        rows = own[0].shape[0] // 2
-        sent.append(
-            [
-                (own[h][:rows].astype(F32) + other[h][:rows].astype(F32)).astype(BF16)
-                for h in (0, 1)
-            ]
-        )
-        kept.append([own[h][rows:].astype(F32) + other[h][rows:].astype(F32) for h in (0, 1)])
-    sent_sum = sent[0]
-    passed, whole = [], []
-    for at in range(group_count):
-        arrived = [plane_hop(sent[at][h], orders[h][0]) for h in (0, 1)]
-        summed = [kept[at][h] + arrived[h].astype(F32) for h in (0, 1)]
-        rows = summed[0].shape[0] // 2
-        passed.append([summed[h][rows:].astype(BF16) for h in (0, 1)])
-        whole.append([summed[h][:rows] for h in (0, 1)])
-    routed_sum = 0.0
-    for at, group in enumerate(back_groups):
-        moving = passed[at]
-        if at + 1 < group_count:
-            moving, _ = lax.optimization_barrier((moving, sent[at + 1]))
-        arrived = [plane_hop(moving[h], orders[h][1]) for h in (0, 1)]
-        plane_sum = [whole[at][h] + arrived[h].astype(F32) for h in (0, 1)]
-        plane_sum = jnp.concatenate(plane_sum, axis=1).reshape(len(group), token_count, model_width)
-        leaving = [plane_sum[place_at].astype(BF16) if k else None for place_at, k in enumerate(group)]
-        if at + 1 < group_count:
-            leaving, _ = lax.optimization_barrier((leaving, passed[at + 1]))
-        for place_at, k in enumerate(group):
-            if k:
-                routed_sum += line_hop(leaving[place_at], k).astype(F32)
-            else:
-                routed_sum += plane_sum[place_at]
+            (gates, down, token_count, moved) if last else None,
+        )
+
+    def both_cores(partials):
+        other = [swap(partials[2 * h + 1]).astype(F32) for h in (0, 1)]
+        return [partials[2 * h].astype(F32) + other[h] for h in (0, 1)]
+
+    activated, *partials = carried
+    sent_sum = [part.astype(BF16) for part in both_cores(partials)]
+    activated, _ = lax.optimization_barrier((activated, sent_sum))
+    kept = both_cores(lower_kept(activated, down, (token_count, moved)))
+    half_sums = []
+    for h, (one, two) in enumerate(((1, 2), (2, 1))):
+        summed = kept[h] + plane_hop(sent_sum[h], one).astype(F32)
+        rows = summed.shape[0] // 2
+        arrived = plane_hop(summed[rows:].astype(BF16), two).astype(F32)
+        half_sums.append(summed[:rows] + arrived)
+    plane_sum = jnp.concatenate(half_sums, axis=1).reshape(line, token_count, model_width)
+    routed_sum = plane_sum[0]
+    for k in range(1, line):
+        routed_sum += line_hop(plane_sum[k].astype(BF16), k).astype(F32)
 
     tokens = chip * token_count + jnp.arange(token_count, dtype=jnp.int32)
     picked = (tokens[:, None] == jnp.arange(half_tokens, dtype=jnp.int32)[None, :]).astype(BF16)

time: 148 us -> 147 us (level)
  waiting for transfers between devices: 40.6 us -> 36.2 us
  Pallas kernels: 28.1 us -> 32 us
  other arithmetic: 12.1 us -> 9.01 us
    ppermute x37 -> x39, waiting for transfers between devices: 40.6 us -> 36.2 us  [hop(): return lax.ppermute(value, axis, [(i, i ^ mask) for i in range(size)])]
    pallas_call x0 -> x1, Pallas kernels: none -> 3.46 us  [lower_kept(): pl.pallas_call(functools.partial(lower_kernel, sizes=sizes, kept=True), i...]
    convert_element_type x2, other arithmetic: 4.1 us -> 1.77 us  [on_device(): sent_sum = [part.astype(BF16) for part in both_cores(partials)]]
    unnamed x51 -> x55, local copies, waits for them, and re-layouts: 10.5 us -> 11.4 us
    ppermute x37 -> x39, starting transfers between devices: 38.8 us -> 39.4 us  [hop(): return lax.ppermute(value, axis, [(i, i ^ mask) for i in range(size)])]
  transfers between devices with their start and end apart: 38 -> 40, of which waited for: 19 -> 19; matrix products, arithmetic and copies ran while one was open for 17% -> 16% of each run, Pallas kernels for 8% -> 11%
where the time goes in v5:
time: 147 us
  starting transfers between devices  44.2 us (30%)
  waiting for transfers between devices  36.2 us (25%)
  Pallas kernels  32 us (22%)
  local copies, waits for them, and re-layouts  18.6 us (13%)
  other arithmetic  9.01 us (6%)
  matrix products  6 us (4%)
    ppermute x39, starting transfers between devices, hop(): return lax.ppermute(value, axis, [(i, i ^ mask) for i in range(size)])  39.4 us
    ppermute x39, waiting for transfers between devices, hop(): return lax.ppermute(value, axis, [(i, i ^ mask) for i in range(size)])  36.2 us
    pallas_call x3, Pallas kernels, expert_rows(): pl.pallas_call(functools.partial(expert_kernel, blocks=blocks, heights=he...  16.4 us
    unnamed x55, local copies, waits for them, and re-layouts  11.4 us
    pallas_call x1, Pallas kernels, attend(): pl.pallas_call(functools.partial(attend_kernel, scale=QKD ** (-0.5)), gri...  6.5 us
    pallas_call x1, Pallas kernels, project(): pl.pallas_call(functools.partial(project_kernel, counts=counts, rows=rows...  5.6 us
    all_to_all x1, starting transfers between devices, on_device(): lax.all_to_all(residual_blocks, 'dev', split_axis=0, concat_axis=0, tiled...  4.8 us
    pallas_call x1, Pallas kernels, lower_kept(): pl.pallas_call(functools.partial(lower_kernel, sizes=sizes, kept=True), i...  3.46 us
  transfers between devices with their start and end apart: 40, of which 19 were waited for; matrix products, arithmetic and copies ran while one was open for 16% of the time, Pallas kernels for 11%

profile of v5, /device:TPU:0, one launch (start us, length us, event | category | flops | bytes accessed | tf_op | source)
XLA Modules:
  0.0 146.7 jit_solution(15152665973992705269)
XLA Ops:
  2.0 6.5 %shard_map.109 = (bf16[16,32,512]{2,1,0:T(8,128)(2,1)S(1)}, bf16[16,32,512]{2,1,0:T(8,128)(2,1)S(1)}, f32[16,64,128]{2,1,0:T(8,128)S(1)}) custom-call(s32[16]{0:T(128)S(1)} %copy-done.2, s32[1]{0:T(128)} %bitcast.33.side_ref, bf16[16,64,576]{2,1,0:T(8,128)(2,1)S(1)} %copy-done, bf16[16,576,384]{2,1,0:T(8,128)(2,1)} %bitcast.144), custom_call_target="tpu_custom_call" | custom-call | flops 905969664 | bytes 8257536 | tf_op jit(solution)/shard_map/pallas_call | solution.py:90
  11.3 3.3 %fusion = bf16[32,2,8,128]{3,2,1,0:T(8,128)(2,1)S(1)} fusion(bf16[32,512,128]{2,1,0:T(8,128)(2,1)} %param.14, bf16[16,32,512]{2,1,0:T(8,128)(2,1)S(1)} %add_convert_fusion), kind=kOutput, calls=%fused_computation.4 | convolution fusion | flops 67174400 | bytes 4849664 | tf_op jit(solution)/shard_map/rhc,hcv->rhv/dot_general | solution.py:518
  14.7 3.0 %collective-permute-start.2 = (bf16[16,4224]{1,0:T(8,128)(2,1)S(1)}, bf16[16,4224]{1,0:T(8,128)(2,1)S(1)}, u32[]{:S(2)}, u32[]{:S(2)}) collective-permute-start(bf16[16,4224]{1,0:T(8,128)(2,1)S(1)} %pad_maximum_fusion.9), channel_id=1, source_target_pairs={{0,4},{1,5},{2,6},{3,7},{4,0},{5,1},{6,2},{7,3},{8,12},{9,13},{10,... | collective-permute-start | bytes 405512 | tf_op jit(solution)/shard_map/ppermute | solution.py:18
  17.7 2.6 %collective-permute-start.5 = (bf16[16,4224]{1,0:T(8,128)(2,1)S(1)}, bf16[16,4224]{1,0:T(8,128)(2,1)S(1)}, u32[]{:S(2)}, u32[]{:S(2)}) collective-permute-start(bf16[16,4224]{1,0:T(8,128)(2,1)S(1)} %pad_maximum_fusion.9), channel_id=1, source_target_pairs={{0,8},{1,9},{2,10},{3,11},{4,12},{5,13},{6,14},{7,15},{8,0},{9,1},... | collective-permute-start | bytes 405512 | tf_op jit(solution)/shard_map/ppermute | solution.py:18
  20.2 4.6 %copy.58 = bf16[896,8,2,256]{3,1,2,0:T(8,128)(2,1)} copy(bf16[896,8,2,256]{3,2,1,0:T(2,128)(2,1)S(1)} %bitcast.143) | data formatting | bytes 14680064
  24.9 1.8 %collective-permute-start.10 = (bf16[2,16,2048]{2,1,0:T(8,128)(2,1)S(1)}, bf16[2,16,2048]{2,1,0:T(8,128)(2,1)S(1)}, u32[]{:S(2)}, u32[]{:S(2)}) collective-permute-start(bf16[2,16,2048]{2,1,0:T(8,128)(2,1)S(1)} %fusion.17.refs_6_), channel_id=1, source_target_pairs={{0,2},{1,3},{2,0},{3,1},{4,6},{5,7},{6,4},{7,5},{8,10},{9,11},{10,... | collective-permute-start | bytes 393224 | tf_op jit(solution)/shard_map/ppermute | solution.py:18
  26.7 4.1 %collective-permute-done.5 = bf16[16,4224]{1,0:T(8,128)(2,1)S(1)} collective-permute-done((bf16[16,4224]{1,0:T(8,128)(2,1)S(1)}, bf16[16,4224]{1,0:T(8,128)(2,1)S(1)}, u32[]{:S(2)}, u32[]{:S(2)}) %collective-permute-start.5) | collective-permute-done | bytes 135200 | tf_op jit(solution)/shard_map/ppermute | solution.py:18
  37.4 1.9 %collective-permute-start.4 = (bf16[4,16,2176]{2,1,0:T(8,128)(2,1)S(1)}, bf16[4,16,2176]{2,1,0:T(8,128)(2,1)S(1)}, u32[]{:S(2)}, u32[]{:S(2)}) collective-permute-start(bf16[4,16,2176]{2,1,0:T(8,128)(2,1)S(1)} %pad_maximum_fusion.4), channel_id=1, source_target_pairs={{0,2},{1,3},{2,0},{3,1},{4,6},{5,7},{6,4},{7,5},{8,10},{9,11},{10,... | collective-permute-start | bytes 835592 | tf_op jit(solution)/shard_map/ppermute | solution.py:18
  40.4 1.9 %collective-permute-start.9 = (bf16[4,16,2176]{2,1,0:T(8,128)(2,1)S(1)}, bf16[4,16,2176]{2,1,0:T(8,128)(2,1)S(1)}, u32[]{:S(2)}, u32[]{:S(2)}) collective-permute-start(bf16[4,16,2176]{2,1,0:T(8,128)(2,1)S(1)} %pad_maximum_fusion.5), channel_id=1, source_target_pairs={{0,2},{1,3},{2,0},{3,1},{4,6},{5,7},{6,4},{7,5},{8,10},{9,11},{10,... | collective-permute-start | bytes 835592 | tf_op jit(solution)/shard_map/ppermute | solution.py:18
  45.4 4.8 %all-to-all-start = ((bf16[16,8,448]{2,1,0:T(8,128)(2,1)}), bf16[16,8,448]{2,1,0:T(8,128)(2,1)S(1)}, u32[]{:S(2)}, u32[]{:S(2)}) async-start(bf16[16,8,448]{2,1,0:T(8,128)(2,1)} %bitcast.134), calls=%async_computation | async-start | bytes 262144 | tf_op jit(solution)/shard_map/all_to_all | solution.py:543
  52.4 5.6 %shard_map.110 = (f32[448,128]{1,0:T(8,128)}, bf16[448,128]{1,0:T(8,128)(2,1)}) custom-call(s32[33]{0:T(128)} %stack.363.place_ref, bf16[2,16,2176]{2,1,0:T(8,128)(2,1)} %copy-done.6, bf16[2,16,2176]{2,1,0:T(8,128)(2,1)} %copy-done.11, bf16[4,16,2176]{2,1,0:T(8,128)(2,1)} %copy-done.17, bf16[2,16,2176]{2,1,0:T(8,128)(2,1)} %copy-done.7, ...), custom_call_target="tpu_custom_call" | custom-call | flops 939524096 | bytes 5767168 | tf_op jit(solution)/shard_map/pallas_call | solution.py:183
  60.8 2.0 %collective-permute-start.14 = (bf16[448,128]{1,0:T(8,128)(2,1)S(1)}, bf16[448,128]{1,0:T(8,128)(2,1)S(1)}, u32[]{:S(2)}, u32[]{:S(2)}) collective-permute-start(bf16[448,128]{1,0:T(8,128)(2,1)S(1)} %fusion.15), channel_id=1, source_target_pairs={{0,4},{1,5},{2,6},{3,7},{4,0},{5,1},{6,2},{7,3},{8,12},{9,13},{10,... | collective-permute-start | bytes 344072 | tf_op jit(solution)/shard_map/ppermute | solution.py:18
  62.8 2.4 %collective-permute-start.15 = (bf16[448,128]{1,0:T(8,128)(2,1)S(1)}, bf16[448,128]{1,0:T(8,128)(2,1)S(1)}, u32[]{:S(2)}, u32[]{:S(2)}) collective-permute-start(bf16[448,128]{1,0:T(8,128)(2,1)S(1)} %fusion.15), channel_id=1, source_target_pairs={{0,8},{1,9},{2,10},{3,11},{4,12},{5,13},{6,14},{7,15},{8,0},{9,1},... | collective-permute-start | bytes 344072 | tf_op jit(solution)/shard_map/ppermute | solution.py:18
  68.5 6.1 %collective-permute-done.15 = bf16[448,128]{1,0:T(8,128)(2,1)S(1)} collective-permute-done((bf16[448,128]{1,0:T(8,128)(2,1)S(1)}, bf16[448,128]{1,0:T(8,128)(2,1)S(1)}, u32[]{:S(2)}, u32[]{:S(2)}) %collective-permute-start.15) | collective-permute-done | bytes 114720 | tf_op jit(solution)/shard_map/ppermute | solution.py:18
  77.7 3.1 %collective-permute-done.18.refs_0_ = bf16[4,224,128]{2,1,0:T(8,128)(2,1)S(1)} collective-permute-done((bf16[4,224,128]{2,1,0:T(8,128)(2,1)S(1)}, bf16[4,224,128]{2,1,0:T(8,128)(2,1)S(1)}, u32[]{:S(2)}, u32[]{:S(2)}) %collective-permute-start.18) | collective-permute-done | bytes 229408 | tf_op jit(solution)/shard_map/ppermute | solution.py:18
  86.0 3.4 %shard_map.111 = (f32[256,512]{1,0:T(8,128)S(1)}, f32[8,256]{1,0:T(8,128)S(1)}) custom-call(s32[16]{0:T(128)S(1)} %stack.410.place_ref, bf16[4,224,128]{2,1,0:T(8,128)(2,1)S(1)} %get-tuple-element.89.refs_0_, bf16[4,224,128]{2,1,0:T(8,128)(2,1)S(1)} %get-tuple-element.92.refs_1_, bf16[4,224,128]{2,1,0:T(8,128)(2,1)S(1)} %collective-permute-done.24.refs_2_, ...), custom_call_target="tpu_custom_call" | custom-call | flops 469762048 | bytes 2752512 | tf_op jit(solution)/shard_map/pallas_call | solution.py:425
  89.4 3.5 %shard_map.112 = (f32[256,512]{1,0:T(8,128)S(1)}, f32[8,256]{1,0:T(8,128)S(1)}) custom-call(s32[16]{0:T(128)S(1)} %stack.401.place_ref, bf16[4,224,128]{2,1,0:T(8,128)(2,1)S(1)} %collective-permute-done.18.refs_0_, bf16[4,224,128]{2,1,0:T(8,128)(2,1)S(1)} %collective-permute-done.19.refs_1_, bf16[4,224,128]{2,1,0:T(8,128)(2,1)S(1)} %collective-permute-done.22.refs_2_, ...), custom_call_target="tpu_custom_call" | custom-call | flops 469762048 | bytes 2752512 | tf_op jit(solution)/shard_map/pallas_call | solution.py:425
  97.4 9.6 %shard_map.113 = (bf16[256,256]{1,0:T(8,128)(2,1)S(1)}, bf16[64,3584]{1,0:T(8,128)(2,1)S(1)}, bf16[64,3584]{1,0:T(8,128)(2,1)S(1)}, bf16[64,3584]{1,0:T(8,128)(2,1)S(1)}, bf16[64,3584]{1,0:T(8,128)(2,1)}) custom-call(s32[48]{0:T(128)S(1)} %stack.392.place_ref, bf16[8,224,128]{2,1,0:T(8,128)(2,1)} %collective-permute-done.20.refs_0_, ...), custom_call_target="tpu_custom_call" | custom-call | flops 939524096 | bytes 5505024 | tf_op jit(solution)/shard_map/pallas_call | solution.py:425
  113.2 3.5 %shard_map.114 = (bf16[64,3584]{1,0:T(8,128)(2,1)S(1)}, bf16[64,3584]{1,0:T(8,128)(2,1)S(1)}, bf16[64,3584]{1,0:T(8,128)(2,1)S(1)}, bf16[64,3584]{1,0:T(8,128)(2,1)S(1)}) custom-call(bf16[256,256]{1,0:T(8,128)(2,1)S(1)} %get-tuple-element.96.activated_ref, bf16[256,7168]{1,0:T(8,128)(2,1)} %bitcast.142), custom_call_target="tpu_custom_call" | custom-call | flops 469762048 | bytes 5505024 | tf_op jit(solution)/shard_map/pallas_call | solution.py:370
  124.2 1.8 %collective-permute-start.35 = (bf16[32,3584]{1,0:T(8,128)(2,1)S(1)}, bf16[32,3584]{1,0:T(8,128)(2,1)S(1)}, u32[]{:S(2)}, u32[]{:S(2)}) collective-permute-start(bf16[32,3584]{1,0:T(8,128)(2,1)S(1)} %slice.196), channel_id=1, source_target_pairs={{0,1},{1,0},{2,3},{3,2},{4,5},{5,4},{6,7},{7,6},{8,9},{9,8},{10,11... | collective-permute-start | bytes 688136 | tf_op jit(solution)/shard_map/ppermute | solution.py:18
  128.0 3.1 %collective-permute-done.35 = bf16[32,3584]{1,0:T(8,128)(2,1)S(1)} collective-permute-done((bf16[32,3584]{1,0:T(8,128)(2,1)S(1)}, bf16[32,3584]{1,0:T(8,128)(2,1)S(1)}, u32[]{:S(2)}, u32[]{:S(2)}) %collective-permute-start.35) | collective-permute-done | bytes 229408 | tf_op jit(solution)/shard_map/ppermute | solution.py:18
  131.1 2.8 %collective-permute-done.32 = bf16[32,3584]{1,0:T(8,128)(2,1)S(1)} collective-permute-done((bf16[32,3584]{1,0:T(8,128)(2,1)S(1)}, bf16[32,3584]{1,0:T(8,128)(2,1)S(1)}, u32[]{:S(2)}, u32[]{:S(2)}) %collective-permute-start.32) | collective-permute-done | bytes 229408 | tf_op jit(solution)/shard_map/ppermute | solution.py:18
  134.1 2.0 %collective-permute-start.36 = (bf16[8,7168]{1,0:T(8,128)(2,1)S(1)}, bf16[8,7168]{1,0:T(8,128)(2,1)S(1)}, u32[]{:S(2)}, u32[]{:S(2)}) collective-permute-start(bf16[8,7168]{1,0:T(8,128)(2,1)S(1)} %get-tuple-element.105), channel_id=1, source_target_pairs={{0,4},{1,5},{2,6},{3,7},{4,0},{5,1},{6,2},{7,3},{8,12},{9,13},{10,... | collective-permute-start | bytes 344072 | tf_op jit(solution)/shard_map/ppermute | solution.py:18
  139.7 6.4 %collective-permute-done.37 = bf16[8,7168]{1,0:T(8,128)(2,1)S(1)} collective-permute-done((bf16[8,7168]{1,0:T(8,128)(2,1)S(1)}, bf16[8,7168]{1,0:T(8,128)(2,1)S(1)}, u32[]{:S(2)}, u32[]{:S(2)}) %collective-permute-start.37) | collective-permute-done | bytes 114720 | tf_op jit(solution)/shard_map/ppermute | solution.py:18
  (196 shorter events, 56.3 us)
Async XLA Ops:
  14.7 10.2 %collective-permute-start.2 = (bf16[16,4224]{1,0:T(8,128)(2,1)S(1)}, bf16[16,4224]{1,0:T(8,128)(2,1)S(1)}, u32[]{:S(2)}, u32[]{:S(2)}) collective-permute-start(bf16[16,4224]{1,0:T(8,128)(2,1)S(1)} %pad_maximum_fusion.9), channel_id=1, source_target_pairs={{0,4},{1,5},{2,6},{3,7},{4,0},{5,1},{6,2},{7,3},{8,12},{9,13},{10,... | collective-permute-start | bytes 405512 | tf_op jit(solution)/shard_map/ppermute | solution.py:18
  17.7 13.2 %collective-permute-start.5 = (bf16[16,4224]{1,0:T(8,128)(2,1)S(1)}, bf16[16,4224]{1,0:T(8,128)(2,1)S(1)}, u32[]{:S(2)}, u32[]{:S(2)}) collective-permute-start(bf16[16,4224]{1,0:T(8,128)(2,1)S(1)} %pad_maximum_fusion.9), channel_id=1, source_target_pairs={{0,8},{1,9},{2,10},{3,11},{4,12},{5,13},{6,14},{7,15},{8,0},{9,1},... | collective-permute-start | bytes 405512 | tf_op jit(solution)/shard_map/ppermute | solution.py:18
  20.2 10.6 %collective-permute-start.6 = (bf16[16,4224]{1,0:T(8,128)(2,1)S(1)}, bf16[16,4224]{1,0:T(8,128)(2,1)S(1)}, u32[]{:S(2)}, u32[]{:S(2)}) collective-permute-start(bf16[16,4224]{1,0:T(8,128)(2,1)S(1)} %pad_maximum_fusion.9), channel_id=1, source_target_pairs={{0,12},{1,13},{2,14},{3,15},{4,8},{5,9},{6,10},{7,11},{8,4},{9,5},... | collective-permute-start | bytes 405512 | tf_op jit(solution)/shard_map/ppermute | solution.py:18
  24.9 10.3 %collective-permute-start.10 = (bf16[2,16,2048]{2,1,0:T(8,128)(2,1)S(1)}, bf16[2,16,2048]{2,1,0:T(8,128)(2,1)S(1)}, u32[]{:S(2)}, u32[]{:S(2)}) collective-permute-start(bf16[2,16,2048]{2,1,0:T(8,128)(2,1)S(1)} %fusion.17.refs_6_), channel_id=1, source_target_pairs={{0,2},{1,3},{2,0},{3,1},{4,6},{5,7},{6,4},{7,5},{8,10},{9,11},{10,... | collective-permute-start | bytes 393224 | tf_op jit(solution)/shard_map/ppermute | solution.py:18
  31.0 6.4 %collective-permute-start.3 = (bf16[2,16,2176]{2,1,0:T(8,128)(2,1)S(1)}, bf16[2,16,2176]{2,1,0:T(8,128)(2,1)S(1)}, u32[]{:S(2)}, u32[]{:S(2)}) collective-permute-start(bf16[2,16,2176]{2,1,0:T(8,128)(2,1)S(1)} %fusion.16.refs_0_), channel_id=1, source_target_pairs={{0,1},{1,0},{2,3},{3,2},{4,5},{5,4},{6,7},{7,6},{8,9},{9,8},{10,11... | collective-permute-start | bytes 417800 | tf_op jit(solution)/shard_map/ppermute | solution.py:18
  32.5 7.8 %collective-permute-start.7 = (bf16[2,16,2176]{2,1,0:T(8,128)(2,1)S(1)}, bf16[2,16,2176]{2,1,0:T(8,128)(2,1)S(1)}, u32[]{:S(2)}, u32[]{:S(2)}) collective-permute-start(bf16[2,16,2176]{2,1,0:T(8,128)(2,1)S(1)} %slice.111.refs_3_), channel_id=1, source_target_pairs={{0,1},{1,0},{2,3},{3,2},{4,5},{5,4},{6,7},{7,6},{8,9},{9,8},{10,11... | collective-permute-start | bytes 417800 | tf_op jit(solution)/shard_map/ppermute | solution.py:18
  35.2 16.2 %collective-permute-start.11 = (bf16[4,16,2048]{2,1,0:T(8,128)(2,1)S(1)}, bf16[4,16,2048]{2,1,0:T(8,128)(2,1)S(1)}, u32[]{:S(2)}, u32[]{:S(2)}) collective-permute-start(bf16[4,16,2048]{2,1,0:T(8,128)(2,1)S(1)} %pad_maximum_fusion.7), channel_id=1, source_target_pairs={{0,1},{1,0},{2,3},{3,2},{4,5},{5,4},{6,7},{7,6},{8,9},{9,8},{10,11... | collective-permute-start | bytes 786440 | tf_op jit(solution)/shard_map/ppermute | solution.py:18
  37.4 13.4 %collective-permute-start.4 = (bf16[4,16,2176]{2,1,0:T(8,128)(2,1)S(1)}, bf16[4,16,2176]{2,1,0:T(8,128)(2,1)S(1)}, u32[]{:S(2)}, u32[]{:S(2)}) collective-permute-start(bf16[4,16,2176]{2,1,0:T(8,128)(2,1)S(1)} %pad_maximum_fusion.4), channel_id=1, source_target_pairs={{0,2},{1,3},{2,0},{3,1},{4,6},{5,7},{6,4},{7,5},{8,10},{9,11},{10,... | collective-permute-start | bytes 835592 | tf_op jit(solution)/shard_map/ppermute | solution.py:18
  40.4 11.1 %collective-permute-start.9 = (bf16[4,16,2176]{2,1,0:T(8,128)(2,1)S(1)}, bf16[4,16,2176]{2,1,0:T(8,128)(2,1)S(1)}, u32[]{:S(2)}, u32[]{:S(2)}) collective-permute-start(bf16[4,16,2176]{2,1,0:T(8,128)(2,1)S(1)} %pad_maximum_fusion.5), channel_id=1, source_target_pairs={{0,2},{1,3},{2,0},{3,1},{4,6},{5,7},{6,4},{7,5},{8,10},{9,11},{10,... | collective-permute-start | bytes 835592 | tf_op jit(solution)/shard_map/ppermute | solution.py:18
  43.0 8.5 %collective-permute-start.12 = (bf16[4,16,2048]{2,1,0:T(8,128)(2,1)}, bf16[4,16,2048]{2,1,0:T(8,128)(2,1)S(1)}, u32[]{:S(2)}, u32[]{:S(2)}) collective-permute-start(bf16[4,16,2048]{2,1,0:T(8,128)(2,1)} %pad_maximum_fusion.8), channel_id=1, source_target_pairs={{0,1},{1,0},{2,3},{3,2},{4,5},{5,4},{6,7},{7,6},{8,9},{9,8},{10,11... | collective-permute-start | bytes 786440 | tf_op jit(solution)/shard_map/ppermute | solution.py:18
  45.4 12.7 %all-to-all-start = ((bf16[16,8,448]{2,1,0:T(8,128)(2,1)}), bf16[16,8,448]{2,1,0:T(8,128)(2,1)S(1)}, u32[]{:S(2)}, u32[]{:S(2)}) async-start(bf16[16,8,448]{2,1,0:T(8,128)(2,1)} %bitcast.134), calls=%async_computation | async-start | bytes 262144 | tf_op jit(solution)/shard_map/all_to_all | solution.py:543
  60.8 7.7 %collective-permute-start.14 = (bf16[448,128]{1,0:T(8,128)(2,1)S(1)}, bf16[448,128]{1,0:T(8,128)(2,1)S(1)}, u32[]{:S(2)}, u32[]{:S(2)}) collective-permute-start(bf16[448,128]{1,0:T(8,128)(2,1)S(1)} %fusion.15), channel_id=1, source_target_pairs={{0,4},{1,5},{2,6},{3,7},{4,0},{5,1},{6,2},{7,3},{8,12},{9,13},{10,... | collective-permute-start | bytes 344072 | tf_op jit(solution)/shard_map/ppermute | solution.py:18
  62.8 11.8 %collective-permute-start.15 = (bf16[448,128]{1,0:T(8,128)(2,1)S(1)}, bf16[448,128]{1,0:T(8,128)(2,1)S(1)}, u32[]{:S(2)}, u32[]{:S(2)}) collective-permute-start(bf16[448,128]{1,0:T(8,128)(2,1)S(1)} %fusion.15), channel_id=1, source_target_pairs={{0,8},{1,9},{2,10},{3,11},{4,12},{5,13},{6,14},{7,15},{8,0},{9,1},... | collective-permute-start | bytes 344072 | tf_op jit(solution)/shard_map/ppermute | solution.py:18
  65.2 9.5 %collective-permute-start.16 = (bf16[448,128]{1,0:T(8,128)(2,1)S(1)}, bf16[448,128]{1,0:T(8,128)(2,1)S(1)}, u32[]{:S(2)}, u32[]{:S(2)}) collective-permute-start(bf16[448,128]{1,0:T(8,128)(2,1)S(1)} %fusion.15), channel_id=1, source_target_pairs={{0,12},{1,13},{2,14},{3,15},{4,8},{5,9},{6,10},{7,11},{8,4},{9,5},... | collective-permute-start | bytes 344072 | tf_op jit(solution)/shard_map/ppermute | solution.py:18
  77.7 7.6 %collective-permute-start.24 = (bf16[4,224,128]{2,1,0:T(8,128)(2,1)S(1)}, bf16[4,224,128]{2,1,0:T(8,128)(2,1)S(1)}, u32[]{:S(2)}, u32[]{:S(2)}) collective-permute-start(bf16[4,224,128]{2,1,0:T(8,128)(2,1)S(1)} %get-tuple-element.89.refs_0_), channel_id=1, source_target_pairs={{0,16},{16,0},{1,17},{17,1},{2,18},{18,2},{3,19},{19,3},{4,20},{20... | collective-permute-start | bytes 688136 | tf_op jit(solution)/shard_map/ppermute | solution.py:18
  82.6 11.2 %collective-permute-start.21 = (bf16[8,224,128]{2,1,0:T(8,128)(2,1)S(1)}, bf16[8,224,128]{2,1,0:T(8,128)(2,1)S(1)}, u32[]{:S(2)}, u32[]{:S(2)}) collective-permute-start(bf16[8,224,128]{2,1,0:T(8,128)(2,1)S(1)} %pad_maximum_fusion.3), channel_id=1, source_target_pairs={{0,1},{1,0},{2,3},{3,2},{4,5},{5,4},{6,7},{7,6},{8,9},{9,8},{10,11... | collective-permute-start | bytes 1376264 | tf_op jit(solution)/shard_map/ppermute | solution.py:18
  83.0 10.8 %collective-permute-start.20 = (bf16[8,224,128]{2,1,0:T(8,128)(2,1)S(1)}, bf16[8,224,128]{2,1,0:T(8,128)(2,1)}, u32[]{:S(2)}, u32[]{:S(2)}) collective-permute-start(bf16[8,224,128]{2,1,0:T(8,128)(2,1)S(1)} %pad_maximum_fusion.2), channel_id=1, source_target_pairs={{0,2},{1,3},{2,0},{3,1},{4,6},{5,7},{6,4},{7,5},{8,10},{9,11},{10,... | collective-permute-start | bytes 1376264 | tf_op jit(solution)/shard_map/ppermute | solution.py:18
  110.0 12.9 %collective-permute-start.34 = (bf16[64,3584]{1,0:T(8,128)(2,1)}, bf16[64,3584]{1,0:T(8,128)(2,1)}, u32[]{:S(2)}, u32[]{:S(2)}) collective-permute-start(bf16[64,3584]{1,0:T(8,128)(2,1)} %add_convert_fusion.1), channel_id=1, source_target_pairs={{0,2},{1,3},{2,0},{3,1},{4,6},{5,7},{6,4},{7,5},{8,10},{9,11},{10,... | collective-permute-start | bytes 1376264 | tf_op jit(solution)/shard_map/ppermute | solution.py:18
  111.4 14.6 %collective-permute-start.31 = (bf16[64,3584]{1,0:T(8,128)(2,1)}, bf16[64,3584]{1,0:T(8,128)(2,1)}, u32[]{:S(2)}, u32[]{:S(2)}) collective-permute-start(bf16[64,3584]{1,0:T(8,128)(2,1)} %add_convert_fusion.2), channel_id=1, source_target_pairs={{0,1},{1,0},{2,3},{3,2},{4,5},{5,4},{6,7},{7,6},{8,9},{9,8},{10,11... | collective-permute-start | bytes 1376264 | tf_op jit(solution)/shard_map/ppermute | solution.py:18
  116.7 9.3 %collective-permute-start.30 = (bf16[64,3584]{1,0:T(8,128)(2,1)S(1)}, bf16[64,3584]{1,0:T(8,128)(2,1)}, u32[]{:S(2)}, u32[]{:S(2)}) collective-permute-start(bf16[64,3584]{1,0:T(8,128)(2,1)S(1)} %get-tuple-element.98), channel_id=1, source_target_pairs={{0,16},{16,0},{1,17},{17,1},{2,18},{18,2},{3,19},{19,3},{4,20},{20... | collective-permute-start | bytes 1376264 | tf_op jit(solution)/shard_map/ppermute | solution.py:18
  124.2 6.9 %collective-permute-start.35 = (bf16[32,3584]{1,0:T(8,128)(2,1)S(1)}, bf16[32,3584]{1,0:T(8,128)(2,1)S(1)}, u32[]{:S(2)}, u32[]{:S(2)}) collective-permute-start(bf16[32,3584]{1,0:T(8,128)(2,1)S(1)} %slice.196), channel_id=1, source_target_pairs={{0,1},{1,0},{2,3},{3,2},{4,5},{5,4},{6,7},{7,6},{8,9},{9,8},{10,11... | collective-permute-start | bytes 688136 | tf_op jit(solution)/shard_map/ppermute | solution.py:18
  127.4 6.6 %collective-permute-start.32 = (bf16[32,3584]{1,0:T(8,128)(2,1)S(1)}, bf16[32,3584]{1,0:T(8,128)(2,1)S(1)}, u32[]{:S(2)}, u32[]{:S(2)}) collective-permute-start(bf16[32,3584]{1,0:T(8,128)(2,1)S(1)} %slice.197), channel_id=1, source_target_pairs={{0,2},{1,3},{2,0},{3,1},{4,6},{5,7},{6,4},{7,5},{8,10},{9,11},{10,... | collective-permute-start | bytes 688136 | tf_op jit(solution)/shard_map/ppermute | solution.py:18
  136.1 9.9 %collective-permute-start.37 = (bf16[8,7168]{1,0:T(8,128)(2,1)S(1)}, bf16[8,7168]{1,0:T(8,128)(2,1)S(1)}, u32[]{:S(2)}, u32[]{:S(2)}) collective-permute-start(bf16[8,7168]{1,0:T(8,128)(2,1)S(1)} %get-tuple-element.107), channel_id=1, source_target_pairs={{0,8},{1,9},{2,10},{3,11},{4,12},{5,13},{6,14},{7,15},{8,0},{9,1},... | collective-permute-start | bytes 344072 | tf_op jit(solution)/shard_map/ppermute | solution.py:18
  137.1 9.0 %collective-permute-start.38 = (bf16[8,7168]{1,0:T(8,128)(2,1)S(1)}, bf16[8,7168]{1,0:T(8,128)(2,1)S(1)}, u32[]{:S(2)}, u32[]{:S(2)}) collective-permute-start(bf16[8,7168]{1,0:T(8,128)(2,1)S(1)} %get-tuple-element.106), channel_id=1, source_target_pairs={{0,12},{1,13},{2,14},{3,15},{4,8},{5,9},{6,10},{7,11},{8,4},{9,5},... | collective-permute-start | bytes 344072 | tf_op jit(solution)/shard_map/ppermute | solution.py:18
  (41 other events, 298.1 us)

commit v6 on v5

--- a/solution.py
+++ b/solution.py
@@ -86,7 +86,7 @@
 def attend(queries, cache_columns, lengths, side, latent_width):
     requests, heads, width = queries.shape
     slots = cache_columns.shape[2]
-    group = 4
+    group = 8
     return pl.pallas_call(
         functools.partial(attend_kernel, scale=QKD ** (-0.5)),
         grid_spec=pltpu.PrefetchScalarGridSpec(
@@ -260,21 +260,15 @@
         squares[...] = sums_in[1][...]
     else:
         squares[...] = jnp.zeros_like(squares)
-    diagonals = {
-        height: lax.broadcasted_iota(jnp.int32, (height, height), 0)
-        == lax.broadcasted_iota(jnp.int32, (height, height), 1)
-        for height in set(heights)
-    }
     for at, (entry, k, row, height) in enumerate(spots):
         part_copies[2 * at].wait()
         part_copies[2 * at + 1].wait()
         wide = rows[row : row + height].astype(F32)
         squares[...] += jnp.sum((wide * wide).reshape(height // 8, 8, 2 * lanes), axis=0)
-        gain = gain_refs[halves[entry]][pl.ds(place_ref[len(spots) + at], 1), :]
-        gain = jnp.where(diagonals[height], gain, 0.0).astype(BF16)
-        rows[row : row + height] = jnp.dot(
-            gain, rows[row : row + height], preferred_element_type=F32
-        ).astype(BF16)
+        lane = lax.broadcasted_iota(jnp.int32, gain_refs[halves[entry]].shape, 1)
+        gain = jnp.where(lane == place_ref[len(spots) + at], gain_refs[halves[entry]][...], 0.0)
+        gain = jnp.sum(gain, axis=1, keepdims=True)
+        rows[row : row + height] = (wide * gain).astype(BF16)
     for entry in range(count):
         for at, spot in enumerate(spots):
             if spot[0] == entry:
@@ -569,8 +563,8 @@
     gates = jnp.concatenate([own_gates, swap(own_gates)])
 
     first_rows = -(-columns // 32) * 16
-    gains = norm_gain.astype(F32).reshape(chips, columns)
-    gains = [gains[:, :first_rows], gains[:, first_rows:]]
+    gains = norm_gain.astype(F32).reshape(chips, columns).T
+    gains = [gains[:first_rows], gains[first_rows:]]
     hidden_groups = [list(range(line))]
     (first, second), gates, _ = gather(
         hidden,

time: 147 us -> 145 us (0.986)
  Pallas kernels: 32 us -> 29.6 us
    pallas_call x3, Pallas kernels: 16.4 us -> 14.4 us  [expert_rows(): pl.pallas_call(functools.partial(expert_kernel, blocks=blocks, heights=he...]
  transfers between devices with their start and end apart: 40 -> 40, of which waited for: 19 -> 19; matrix products, arithmetic and copies ran while one was open for 16% -> 16% of each run, Pallas kernels for 11% -> 10%
where the time goes in v6:
time: 145 us
  starting transfers between devices  44.2 us (30%)
  waiting for transfers between devices  36.7 us (25%)
  Pallas kernels  29.6 us (20%)
  local copies, waits for them, and re-layouts  18.7 us (13%)
  other arithmetic  9.01 us (6%)
  matrix products  6 us (4%)
    ppermute x39, starting transfers between devices, hop(): return lax.ppermute(value, axis, [(i, i ^ mask) for i in range(size)])  39.4 us
    ppermute x39, waiting for transfers between devices, hop(): return lax.ppermute(value, axis, [(i, i ^ mask) for i in range(size)])  36.7 us
    pallas_call x3, Pallas kernels, expert_rows(): pl.pallas_call(functools.partial(expert_kernel, blocks=blocks, heights=he...  14.4 us
    unnamed x55, local copies, waits for them, and re-layouts  11.4 us
    pallas_call x1, Pallas kernels, attend(): pl.pallas_call(functools.partial(attend_kernel, scale=QKD ** (-0.5)), gri...  6.12 us
    pallas_call x1, Pallas kernels, project(): pl.pallas_call(functools.partial(project_kernel, counts=counts, rows=rows...  5.6 us
    all_to_all x1, starting transfers between devices, on_device(): lax.all_to_all(residual_blocks, 'dev', split_axis=0, concat_axis=0, tiled...  4.8 us
    pallas_call x1, Pallas kernels, lower_kept(): pl.pallas_call(functools.partial(lower_kernel, sizes=sizes, kept=True), i...  3.47 us
  transfers between devices with their start and end apart: 40, of which 19 were waited for; matrix products, arithmetic and copies ran while one was open for 16% of the time, Pallas kernels for 10%

profile of v6, /device:TPU:0, one launch (start us, length us, event | category | flops | bytes accessed | tf_op | source)
XLA Modules:
  0.0 144.9 jit_solution(7795638913710980247)
XLA Ops:
  2.0 6.1 %shard_map.109 = (bf16[16,32,512]{2,1,0:T(8,128)(2,1)S(1)}, bf16[16,32,512]{2,1,0:T(8,128)(2,1)S(1)}, f32[16,64,128]{2,1,0:T(8,128)S(1)}) custom-call(s32[16]{0:T(128)S(1)} %copy-done.2, s32[1]{0:T(128)} %bitcast.33.side_ref, bf16[16,64,576]{2,1,0:T(8,128)(2,1)S(1)} %copy-done, bf16[16,576,384]{2,1,0:T(8,128)(2,1)} %bitcast.145), custom_call_target="tpu_custom_call" | custom-call | flops 905969664 | bytes 8257536 | tf_op jit(solution)/shard_map/pallas_call | solution.py:90
  10.9 3.3 %fusion = bf16[32,2,8,128]{3,2,1,0:T(8,128)(2,1)S(1)} fusion(bf16[32,512,128]{2,1,0:T(8,128)(2,1)} %param.14, bf16[16,32,512]{2,1,0:T(8,128)(2,1)S(1)} %add_convert_fusion), kind=kOutput, calls=%fused_computation.4 | convolution fusion | flops 67174400 | bytes 4849664 | tf_op jit(solution)/shard_map/rhc,hcv->rhv/dot_general | solution.py:512
  14.3 3.0 %collective-permute-start.2 = (bf16[16,4224]{1,0:T(8,128)(2,1)S(1)}, bf16[16,4224]{1,0:T(8,128)(2,1)S(1)}, u32[]{:S(2)}, u32[]{:S(2)}) collective-permute-start(bf16[16,4224]{1,0:T(8,128)(2,1)S(1)} %pad_maximum_fusion.9), channel_id=1, source_target_pairs={{0,4},{1,5},{2,6},{3,7},{4,0},{5,1},{6,2},{7,3},{8,12},{9,13},{10,... | collective-permute-start | bytes 405512 | tf_op jit(solution)/shard_map/ppermute | solution.py:18
  17.3 2.6 %collective-permute-start.5 = (bf16[16,4224]{1,0:T(8,128)(2,1)S(1)}, bf16[16,4224]{1,0:T(8,128)(2,1)S(1)}, u32[]{:S(2)}, u32[]{:S(2)}) collective-permute-start(bf16[16,4224]{1,0:T(8,128)(2,1)S(1)} %pad_maximum_fusion.9), channel_id=1, source_target_pairs={{0,8},{1,9},{2,10},{3,11},{4,12},{5,13},{6,14},{7,15},{8,0},{9,1},... | collective-permute-start | bytes 405512 | tf_op jit(solution)/shard_map/ppermute | solution.py:18
  19.9 4.6 %copy.63 = bf16[896,8,2,256]{3,1,2,0:T(8,128)(2,1)} copy(bf16[896,8,2,256]{3,2,1,0:T(2,128)(2,1)S(1)} %bitcast.144) | data formatting | bytes 14680064
  24.5 1.8 %collective-permute-start.10 = (bf16[2,16,2048]{2,1,0:T(8,128)(2,1)S(1)}, bf16[2,16,2048]{2,1,0:T(8,128)(2,1)S(1)}, u32[]{:S(2)}, u32[]{:S(2)}) collective-permute-start(bf16[2,16,2048]{2,1,0:T(8,128)(2,1)S(1)} %fusion.17.refs_6_), channel_id=1, source_target_pairs={{0,2},{1,3},{2,0},{3,1},{4,6},{5,7},{6,4},{7,5},{8,10},{9,11},{10,... | collective-permute-start | bytes 393224 | tf_op jit(solution)/shard_map/ppermute | solution.py:18
  26.3 4.1 %collective-permute-done.5 = bf16[16,4224]{1,0:T(8,128)(2,1)S(1)} collective-permute-done((bf16[16,4224]{1,0:T(8,128)(2,1)S(1)}, bf16[16,4224]{1,0:T(8,128)(2,1)S(1)}, u32[]{:S(2)}, u32[]{:S(2)}) %collective-permute-start.5) | collective-permute-done | bytes 135200 | tf_op jit(solution)/shard_map/ppermute | solution.py:18
  37.0 1.9 %collective-permute-start.4 = (bf16[4,16,2176]{2,1,0:T(8,128)(2,1)S(1)}, bf16[4,16,2176]{2,1,0:T(8,128)(2,1)S(1)}, u32[]{:S(2)}, u32[]{:S(2)}) collective-permute-start(bf16[4,16,2176]{2,1,0:T(8,128)(2,1)S(1)} %pad_maximum_fusion.4), channel_id=1, source_target_pairs={{0,2},{1,3},{2,0},{3,1},{4,6},{5,7},{6,4},{7,5},{8,10},{9,11},{10,... | collective-permute-start | bytes 835592 | tf_op jit(solution)/shard_map/ppermute | solution.py:18
  40.0 1.9 %collective-permute-start.9 = (bf16[4,16,2176]{2,1,0:T(8,128)(2,1)S(1)}, bf16[4,16,2176]{2,1,0:T(8,128)(2,1)S(1)}, u32[]{:S(2)}, u32[]{:S(2)}) collective-permute-start(bf16[4,16,2176]{2,1,0:T(8,128)(2,1)S(1)} %pad_maximum_fusion.5), channel_id=1, source_target_pairs={{0,2},{1,3},{2,0},{3,1},{4,6},{5,7},{6,4},{7,5},{8,10},{9,11},{10,... | collective-permute-start | bytes 835592 | tf_op jit(solution)/shard_map/ppermute | solution.py:18
  45.0 4.8 %all-to-all-start = ((bf16[16,8,448]{2,1,0:T(8,128)(2,1)}), bf16[16,8,448]{2,1,0:T(8,128)(2,1)S(1)}, u32[]{:S(2)}, u32[]{:S(2)}) async-start(bf16[16,8,448]{2,1,0:T(8,128)(2,1)} %bitcast.135), calls=%async_computation | async-start | bytes 262144 | tf_op jit(solution)/shard_map/all_to_all | solution.py:537
  52.0 5.6 %shard_map.110 = (f32[448,128]{1,0:T(8,128)}, bf16[448,128]{1,0:T(8,128)(2,1)}) custom-call(s32[33]{0:T(128)} %stack.363.place_ref, bf16[2,16,2176]{2,1,0:T(8,128)(2,1)} %copy-done.6, bf16[2,16,2176]{2,1,0:T(8,128)(2,1)} %copy-done.11, bf16[4,16,2176]{2,1,0:T(8,128)(2,1)} %copy-done.17, bf16[2,16,2176]{2,1,0:T(8,128)(2,1)} %copy-done.7, ...), custom_call_target="tpu_custom_call" | custom-call | flops 939524096 | bytes 5767168 | tf_op jit(solution)/shard_map/pallas_call | solution.py:183
  60.4 2.0 %collective-permute-start.14 = (bf16[448,128]{1,0:T(8,128)(2,1)S(1)}, bf16[448,128]{1,0:T(8,128)(2,1)S(1)}, u32[]{:S(2)}, u32[]{:S(2)}) collective-permute-start(bf16[448,128]{1,0:T(8,128)(2,1)S(1)} %fusion.15), channel_id=1, source_target_pairs={{0,4},{1,5},{2,6},{3,7},{4,0},{5,1},{6,2},{7,3},{8,12},{9,13},{10,... | collective-permute-start | bytes 344072 | tf_op jit(solution)/shard_map/ppermute | solution.py:18
  62.4 2.4 %collective-permute-start.15 = (bf16[448,128]{1,0:T(8,128)(2,1)S(1)}, bf16[448,128]{1,0:T(8,128)(2,1)S(1)}, u32[]{:S(2)}, u32[]{:S(2)}) collective-permute-start(bf16[448,128]{1,0:T(8,128)(2,1)S(1)} %fusion.15), channel_id=1, source_target_pairs={{0,8},{1,9},{2,10},{3,11},{4,12},{5,13},{6,14},{7,15},{8,0},{9,1},... | collective-permute-start | bytes 344072 | tf_op jit(solution)/shard_map/ppermute | solution.py:18
  68.1 6.1 %collective-permute-done.15 = bf16[448,128]{1,0:T(8,128)(2,1)S(1)} collective-permute-done((bf16[448,128]{1,0:T(8,128)(2,1)S(1)}, bf16[448,128]{1,0:T(8,128)(2,1)S(1)}, u32[]{:S(2)}, u32[]{:S(2)}) %collective-permute-start.15) | collective-permute-done | bytes 114720 | tf_op jit(solution)/shard_map/ppermute | solution.py:18
  77.4 3.1 %collective-permute-done.18.refs_0_ = bf16[4,224,128]{2,1,0:T(8,128)(2,1)S(1)} collective-permute-done((bf16[4,224,128]{2,1,0:T(8,128)(2,1)S(1)}, bf16[4,224,128]{2,1,0:T(8,128)(2,1)S(1)}, u32[]{:S(2)}, u32[]{:S(2)}) %collective-permute-start.18) | collective-permute-done | bytes 229408 | tf_op jit(solution)/shard_map/ppermute | solution.py:18
  86.1 3.0 %shard_map.111 = (f32[256,512]{1,0:T(8,128)S(1)}, f32[8,256]{1,0:T(8,128)S(1)}) custom-call(s32[16]{0:T(128)S(1)} %stack.410.place_ref, bf16[4,224,128]{2,1,0:T(8,128)(2,1)S(1)} %get-tuple-element.89.refs_0_, bf16[4,224,128]{2,1,0:T(8,128)(2,1)S(1)} %get-tuple-element.92.refs_1_, bf16[4,224,128]{2,1,0:T(8,128)(2,1)S(1)} %collective-permute-done.24.refs_2_, ...), custom_call_target="tpu_custom_call" | custom-call | flops 469762048 | bytes 2752512 | tf_op jit(solution)/shard_map/pallas_call | solution.py:419
  89.2 3.1 %shard_map.112 = (f32[256,512]{1,0:T(8,128)S(1)}, f32[8,256]{1,0:T(8,128)S(1)}) custom-call(s32[16]{0:T(128)S(1)} %stack.401.place_ref, bf16[4,224,128]{2,1,0:T(8,128)(2,1)S(1)} %collective-permute-done.18.refs_0_, bf16[4,224,128]{2,1,0:T(8,128)(2,1)S(1)} %collective-permute-done.19.refs_1_, bf16[4,224,128]{2,1,0:T(8,128)(2,1)S(1)} %collective-permute-done.22.refs_2_, ...), custom_call_target="tpu_custom_call" | custom-call | flops 469762048 | bytes 2752512 | tf_op jit(solution)/shard_map/pallas_call | solution.py:419
  96.8 8.4 %shard_map.113 = (bf16[256,256]{1,0:T(8,128)(2,1)S(1)}, bf16[64,3584]{1,0:T(8,128)(2,1)S(1)}, bf16[64,3584]{1,0:T(8,128)(2,1)S(1)}, bf16[64,3584]{1,0:T(8,128)(2,1)S(1)}, bf16[64,3584]{1,0:T(8,128)(2,1)}) custom-call(s32[48]{0:T(128)S(1)} %stack.392.place_ref, bf16[8,224,128]{2,1,0:T(8,128)(2,1)} %collective-permute-done.20.refs_0_, ...), custom_call_target="tpu_custom_call" | custom-call | flops 939524096 | bytes 5505024 | tf_op jit(solution)/shard_map/pallas_call | solution.py:419
  111.2 3.5 %shard_map.114 = (bf16[64,3584]{1,0:T(8,128)(2,1)S(1)}, bf16[64,3584]{1,0:T(8,128)(2,1)S(1)}, bf16[64,3584]{1,0:T(8,128)(2,1)S(1)}, bf16[64,3584]{1,0:T(8,128)(2,1)S(1)}) custom-call(bf16[256,256]{1,0:T(8,128)(2,1)S(1)} %get-tuple-element.96.activated_ref, bf16[256,7168]{1,0:T(8,128)(2,1)} %bitcast.143), custom_call_target="tpu_custom_call" | custom-call | flops 469762048 | bytes 5505024 | tf_op jit(solution)/shard_map/pallas_call | solution.py:364
  122.3 1.9 %collective-permute-start.35 = (bf16[32,3584]{1,0:T(8,128)(2,1)S(1)}, bf16[32,3584]{1,0:T(8,128)(2,1)S(1)}, u32[]{:S(2)}, u32[]{:S(2)}) collective-permute-start(bf16[32,3584]{1,0:T(8,128)(2,1)S(1)} %slice.196), channel_id=1, source_target_pairs={{0,1},{1,0},{2,3},{3,2},{4,5},{5,4},{6,7},{7,6},{8,9},{9,8},{10,11... | collective-permute-start | bytes 688136 | tf_op jit(solution)/shard_map/ppermute | solution.py:18
  126.1 3.2 %collective-permute-done.35 = bf16[32,3584]{1,0:T(8,128)(2,1)S(1)} collective-permute-done((bf16[32,3584]{1,0:T(8,128)(2,1)S(1)}, bf16[32,3584]{1,0:T(8,128)(2,1)S(1)}, u32[]{:S(2)}, u32[]{:S(2)}) %collective-permute-start.35) | collective-permute-done | bytes 229408 | tf_op jit(solution)/shard_map/ppermute | solution.py:18
  129.4 2.8 %collective-permute-done.32 = bf16[32,3584]{1,0:T(8,128)(2,1)S(1)} collective-permute-done((bf16[32,3584]{1,0:T(8,128)(2,1)S(1)}, bf16[32,3584]{1,0:T(8,128)(2,1)S(1)}, u32[]{:S(2)}, u32[]{:S(2)}) %collective-permute-start.32) | collective-permute-done | bytes 229408 | tf_op jit(solution)/shard_map/ppermute | solution.py:18
  132.3 2.0 %collective-permute-start.36 = (bf16[8,7168]{1,0:T(8,128)(2,1)S(1)}, bf16[8,7168]{1,0:T(8,128)(2,1)S(1)}, u32[]{:S(2)}, u32[]{:S(2)}) collective-permute-start(bf16[8,7168]{1,0:T(8,128)(2,1)S(1)} %get-tuple-element.105), channel_id=1, source_target_pairs={{0,4},{1,5},{2,6},{3,7},{4,0},{5,1},{6,2},{7,3},{8,12},{9,13},{10,... | collective-permute-start | bytes 344072 | tf_op jit(solution)/shard_map/ppermute | solution.py:18
  137.8 6.4 %collective-permute-done.37 = bf16[8,7168]{1,0:T(8,128)(2,1)S(1)} collective-permute-done((bf16[8,7168]{1,0:T(8,128)(2,1)S(1)}, bf16[8,7168]{1,0:T(8,128)(2,1)S(1)}, u32[]{:S(2)}, u32[]{:S(2)}) %collective-permute-start.37) | collective-permute-done | bytes 114720 | tf_op jit(solution)/shard_map/ppermute | solution.py:18
  (197 shorter events, 56.6 us)
Async XLA Ops:
  14.3 10.2 %collective-permute-start.2 = (bf16[16,4224]{1,0:T(8,128)(2,1)S(1)}, bf16[16,4224]{1,0:T(8,128)(2,1)S(1)}, u32[]{:S(2)}, u32[]{:S(2)}) collective-permute-start(bf16[16,4224]{1,0:T(8,128)(2,1)S(1)} %pad_maximum_fusion.9), channel_id=1, source_target_pairs={{0,4},{1,5},{2,6},{3,7},{4,0},{5,1},{6,2},{7,3},{8,12},{9,13},{10,... | collective-permute-start | bytes 405512 | tf_op jit(solution)/shard_map/ppermute | solution.py:18
  17.3 13.2 %collective-permute-start.5 = (bf16[16,4224]{1,0:T(8,128)(2,1)S(1)}, bf16[16,4224]{1,0:T(8,128)(2,1)S(1)}, u32[]{:S(2)}, u32[]{:S(2)}) collective-permute-start(bf16[16,4224]{1,0:T(8,128)(2,1)S(1)} %pad_maximum_fusion.9), channel_id=1, source_target_pairs={{0,8},{1,9},{2,10},{3,11},{4,12},{5,13},{6,14},{7,15},{8,0},{9,1},... | collective-permute-start | bytes 405512 | tf_op jit(solution)/shard_map/ppermute | solution.py:18
  19.9 10.6 %collective-permute-start.6 = (bf16[16,4224]{1,0:T(8,128)(2,1)S(1)}, bf16[16,4224]{1,0:T(8,128)(2,1)S(1)}, u32[]{:S(2)}, u32[]{:S(2)}) collective-permute-start(bf16[16,4224]{1,0:T(8,128)(2,1)S(1)} %pad_maximum_fusion.9), channel_id=1, source_target_pairs={{0,12},{1,13},{2,14},{3,15},{4,8},{5,9},{6,10},{7,11},{8,4},{9,5},... | collective-permute-start | bytes 405512 | tf_op jit(solution)/shard_map/ppermute | solution.py:18
  24.5 10.3 %collective-permute-start.10 = (bf16[2,16,2048]{2,1,0:T(8,128)(2,1)S(1)}, bf16[2,16,2048]{2,1,0:T(8,128)(2,1)S(1)}, u32[]{:S(2)}, u32[]{:S(2)}) collective-permute-start(bf16[2,16,2048]{2,1,0:T(8,128)(2,1)S(1)} %fusion.17.refs_6_), channel_id=1, source_target_pairs={{0,2},{1,3},{2,0},{3,1},{4,6},{5,7},{6,4},{7,5},{8,10},{9,11},{10,... | collective-permute-start | bytes 393224 | tf_op jit(solution)/shard_map/ppermute | solution.py:18
  30.6 6.4 %collective-permute-start.3 = (bf16[2,16,2176]{2,1,0:T(8,128)(2,1)S(1)}, bf16[2,16,2176]{2,1,0:T(8,128)(2,1)S(1)}, u32[]{:S(2)}, u32[]{:S(2)}) collective-permute-start(bf16[2,16,2176]{2,1,0:T(8,128)(2,1)S(1)} %fusion.16.refs_0_), channel_id=1, source_target_pairs={{0,1},{1,0},{2,3},{3,2},{4,5},{5,4},{6,7},{7,6},{8,9},{9,8},{10,11... | collective-permute-start | bytes 417800 | tf_op jit(solution)/shard_map/ppermute | solution.py:18
  32.1 7.8 %collective-permute-start.7 = (bf16[2,16,2176]{2,1,0:T(8,128)(2,1)S(1)}, bf16[2,16,2176]{2,1,0:T(8,128)(2,1)S(1)}, u32[]{:S(2)}, u32[]{:S(2)}) collective-permute-start(bf16[2,16,2176]{2,1,0:T(8,128)(2,1)S(1)} %slice.111.refs_3_), channel_id=1, source_target_pairs={{0,1},{1,0},{2,3},{3,2},{4,5},{5,4},{6,7},{7,6},{8,9},{9,8},{10,11... | collective-permute-start | bytes 417800 | tf_op jit(solution)/shard_map/ppermute | solution.py:18
  34.8 16.2 %collective-permute-start.11 = (bf16[4,16,2048]{2,1,0:T(8,128)(2,1)S(1)}, bf16[4,16,2048]{2,1,0:T(8,128)(2,1)S(1)}, u32[]{:S(2)}, u32[]{:S(2)}) collective-permute-start(bf16[4,16,2048]{2,1,0:T(8,128)(2,1)S(1)} %pad_maximum_fusion.7), channel_id=1, source_target_pairs={{0,1},{1,0},{2,3},{3,2},{4,5},{5,4},{6,7},{7,6},{8,9},{9,8},{10,11... | collective-permute-start | bytes 786440 | tf_op jit(solution)/shard_map/ppermute | solution.py:18
  37.0 13.4 %collective-permute-start.4 = (bf16[4,16,2176]{2,1,0:T(8,128)(2,1)S(1)}, bf16[4,16,2176]{2,1,0:T(8,128)(2,1)S(1)}, u32[]{:S(2)}, u32[]{:S(2)}) collective-permute-start(bf16[4,16,2176]{2,1,0:T(8,128)(2,1)S(1)} %pad_maximum_fusion.4), channel_id=1, source_target_pairs={{0,2},{1,3},{2,0},{3,1},{4,6},{5,7},{6,4},{7,5},{8,10},{9,11},{10,... | collective-permute-start | bytes 835592 | tf_op jit(solution)/shard_map/ppermute | solution.py:18
  40.0 11.1 %collective-permute-start.9 = (bf16[4,16,2176]{2,1,0:T(8,128)(2,1)S(1)}, bf16[4,16,2176]{2,1,0:T(8,128)(2,1)S(1)}, u32[]{:S(2)}, u32[]{:S(2)}) collective-permute-start(bf16[4,16,2176]{2,1,0:T(8,128)(2,1)S(1)} %pad_maximum_fusion.5), channel_id=1, source_target_pairs={{0,2},{1,3},{2,0},{3,1},{4,6},{5,7},{6,4},{7,5},{8,10},{9,11},{10,... | collective-permute-start | bytes 835592 | tf_op jit(solution)/shard_map/ppermute | solution.py:18
  42.6 8.5 %collective-permute-start.12 = (bf16[4,16,2048]{2,1,0:T(8,128)(2,1)}, bf16[4,16,2048]{2,1,0:T(8,128)(2,1)S(1)}, u32[]{:S(2)}, u32[]{:S(2)}) collective-permute-start(bf16[4,16,2048]{2,1,0:T(8,128)(2,1)} %pad_maximum_fusion.8), channel_id=1, source_target_pairs={{0,1},{1,0},{2,3},{3,2},{4,5},{5,4},{6,7},{7,6},{8,9},{9,8},{10,11... | collective-permute-start | bytes 786440 | tf_op jit(solution)/shard_map/ppermute | solution.py:18
  45.0 12.7 %all-to-all-start = ((bf16[16,8,448]{2,1,0:T(8,128)(2,1)}), bf16[16,8,448]{2,1,0:T(8,128)(2,1)S(1)}, u32[]{:S(2)}, u32[]{:S(2)}) async-start(bf16[16,8,448]{2,1,0:T(8,128)(2,1)} %bitcast.135), calls=%async_computation | async-start | bytes 262144 | tf_op jit(solution)/shard_map/all_to_all | solution.py:537
  60.4 7.7 %collective-permute-start.14 = (bf16[448,128]{1,0:T(8,128)(2,1)S(1)}, bf16[448,128]{1,0:T(8,128)(2,1)S(1)}, u32[]{:S(2)}, u32[]{:S(2)}) collective-permute-start(bf16[448,128]{1,0:T(8,128)(2,1)S(1)} %fusion.15), channel_id=1, source_target_pairs={{0,4},{1,5},{2,6},{3,7},{4,0},{5,1},{6,2},{7,3},{8,12},{9,13},{10,... | collective-permute-start | bytes 344072 | tf_op jit(solution)/shard_map/ppermute | solution.py:18
  62.4 11.8 %collective-permute-start.15 = (bf16[448,128]{1,0:T(8,128)(2,1)S(1)}, bf16[448,128]{1,0:T(8,128)(2,1)S(1)}, u32[]{:S(2)}, u32[]{:S(2)}) collective-permute-start(bf16[448,128]{1,0:T(8,128)(2,1)S(1)} %fusion.15), channel_id=1, source_target_pairs={{0,8},{1,9},{2,10},{3,11},{4,12},{5,13},{6,14},{7,15},{8,0},{9,1},... | collective-permute-start | bytes 344072 | tf_op jit(solution)/shard_map/ppermute | solution.py:18
  64.8 9.5 %collective-permute-start.16 = (bf16[448,128]{1,0:T(8,128)(2,1)S(1)}, bf16[448,128]{1,0:T(8,128)(2,1)S(1)}, u32[]{:S(2)}, u32[]{:S(2)}) collective-permute-start(bf16[448,128]{1,0:T(8,128)(2,1)S(1)} %fusion.15), channel_id=1, source_target_pairs={{0,12},{1,13},{2,14},{3,15},{4,8},{5,9},{6,10},{7,11},{8,4},{9,5},... | collective-permute-start | bytes 344072 | tf_op jit(solution)/shard_map/ppermute | solution.py:18
  77.4 7.8 %collective-permute-start.24 = (bf16[4,224,128]{2,1,0:T(8,128)(2,1)S(1)}, bf16[4,224,128]{2,1,0:T(8,128)(2,1)S(1)}, u32[]{:S(2)}, u32[]{:S(2)}) collective-permute-start(bf16[4,224,128]{2,1,0:T(8,128)(2,1)S(1)} %get-tuple-element.89.refs_0_), channel_id=1, source_target_pairs={{0,16},{16,0},{1,17},{17,1},{2,18},{18,2},{3,19},{19,3},{4,20},{20... | collective-permute-start | bytes 688136 | tf_op jit(solution)/shard_map/ppermute | solution.py:18
  82.2 10.9 %collective-permute-start.21 = (bf16[8,224,128]{2,1,0:T(8,128)(2,1)S(1)}, bf16[8,224,128]{2,1,0:T(8,128)(2,1)S(1)}, u32[]{:S(2)}, u32[]{:S(2)}) collective-permute-start(bf16[8,224,128]{2,1,0:T(8,128)(2,1)S(1)} %pad_maximum_fusion.3), channel_id=1, source_target_pairs={{0,1},{1,0},{2,3},{3,2},{4,5},{5,4},{6,7},{7,6},{8,9},{9,8},{10,11... | collective-permute-start | bytes 1376264 | tf_op jit(solution)/shard_map/ppermute | solution.py:18
  82.6 10.5 %collective-permute-start.20 = (bf16[8,224,128]{2,1,0:T(8,128)(2,1)S(1)}, bf16[8,224,128]{2,1,0:T(8,128)(2,1)}, u32[]{:S(2)}, u32[]{:S(2)}) collective-permute-start(bf16[8,224,128]{2,1,0:T(8,128)(2,1)S(1)} %pad_maximum_fusion.2), channel_id=1, source_target_pairs={{0,2},{1,3},{2,0},{3,1},{4,6},{5,7},{6,4},{7,5},{8,10},{9,11},{10,... | collective-permute-start | bytes 1376264 | tf_op jit(solution)/shard_map/ppermute | solution.py:18
  108.1 12.9 %collective-permute-start.34 = (bf16[64,3584]{1,0:T(8,128)(2,1)}, bf16[64,3584]{1,0:T(8,128)(2,1)}, u32[]{:S(2)}, u32[]{:S(2)}) collective-permute-start(bf16[64,3584]{1,0:T(8,128)(2,1)} %add_convert_fusion.1), channel_id=1, source_target_pairs={{0,2},{1,3},{2,0},{3,1},{4,6},{5,7},{6,4},{7,5},{8,10},{9,11},{10,... | collective-permute-start | bytes 1376264 | tf_op jit(solution)/shard_map/ppermute | solution.py:18
  109.5 14.7 %collective-permute-start.31 = (bf16[64,3584]{1,0:T(8,128)(2,1)}, bf16[64,3584]{1,0:T(8,128)(2,1)}, u32[]{:S(2)}, u32[]{:S(2)}) collective-permute-start(bf16[64,3584]{1,0:T(8,128)(2,1)} %add_convert_fusion.2), channel_id=1, source_target_pairs={{0,1},{1,0},{2,3},{3,2},{4,5},{5,4},{6,7},{7,6},{8,9},{9,8},{10,11... | collective-permute-start | bytes 1376264 | tf_op jit(solution)/shard_map/ppermute | solution.py:18
  114.8 9.4 %collective-permute-start.30 = (bf16[64,3584]{1,0:T(8,128)(2,1)S(1)}, bf16[64,3584]{1,0:T(8,128)(2,1)}, u32[]{:S(2)}, u32[]{:S(2)}) collective-permute-start(bf16[64,3584]{1,0:T(8,128)(2,1)S(1)} %get-tuple-element.98), channel_id=1, source_target_pairs={{0,16},{16,0},{1,17},{17,1},{2,18},{18,2},{3,19},{19,3},{4,20},{20... | collective-permute-start | bytes 1376264 | tf_op jit(solution)/shard_map/ppermute | solution.py:18
  122.3 7.0 %collective-permute-start.35 = (bf16[32,3584]{1,0:T(8,128)(2,1)S(1)}, bf16[32,3584]{1,0:T(8,128)(2,1)S(1)}, u32[]{:S(2)}, u32[]{:S(2)}) collective-permute-start(bf16[32,3584]{1,0:T(8,128)(2,1)S(1)} %slice.196), channel_id=1, source_target_pairs={{0,1},{1,0},{2,3},{3,2},{4,5},{5,4},{6,7},{7,6},{8,9},{9,8},{10,11... | collective-permute-start | bytes 688136 | tf_op jit(solution)/shard_map/ppermute | solution.py:18
  125.6 6.6 %collective-permute-start.32 = (bf16[32,3584]{1,0:T(8,128)(2,1)S(1)}, bf16[32,3584]{1,0:T(8,128)(2,1)S(1)}, u32[]{:S(2)}, u32[]{:S(2)}) collective-permute-start(bf16[32,3584]{1,0:T(8,128)(2,1)S(1)} %slice.197), channel_id=1, source_target_pairs={{0,2},{1,3},{2,0},{3,1},{4,6},{5,7},{6,4},{7,5},{8,10},{9,11},{10,... | collective-permute-start | bytes 688136 | tf_op jit(solution)/shard_map/ppermute | solution.py:18
  134.3 9.9 %collective-permute-start.37 = (bf16[8,7168]{1,0:T(8,128)(2,1)S(1)}, bf16[8,7168]{1,0:T(8,128)(2,1)S(1)}, u32[]{:S(2)}, u32[]{:S(2)}) collective-permute-start(bf16[8,7168]{1,0:T(8,128)(2,1)S(1)} %get-tuple-element.107), channel_id=1, source_target_pairs={{0,8},{1,9},{2,10},{3,11},{4,12},{5,13},{6,14},{7,15},{8,0},{9,1},... | collective-permute-start | bytes 344072 | tf_op jit(solution)/shard_map/ppermute | solution.py:18
  135.2 9.0 %collective-permute-start.38 = (bf16[8,7168]{1,0:T(8,128)(2,1)S(1)}, bf16[8,7168]{1,0:T(8,128)(2,1)S(1)}, u32[]{:S(2)}, u32[]{:S(2)}) collective-permute-start(bf16[8,7168]{1,0:T(8,128)(2,1)S(1)} %get-tuple-element.106), channel_id=1, source_target_pairs={{0,12},{1,13},{2,14},{3,15},{4,8},{5,9},{6,10},{7,11},{8,4},{9,5},... | collective-permute-start | bytes 344072 | tf_op jit(solution)/shard_map/ppermute | solution.py:18
  (41 other events, 297.1 us)

commit v7 on v6

--- a/solution.py
+++ b/solution.py
@@ -11,7 +11,7 @@
 F32 = jnp.float32
 BF16 = jnp.bfloat16
 VMEM_LIMIT = 48 * 2**20
-LAST_VMEM_LIMIT = 52 * 2**20
+LAST_VMEM_LIMIT = 51 * 2**20
 
 
 def hop(value, axis, size, mask):

time: 145 us -> 145 us (level)
  transfers between devices with their start and end apart: 40 -> 40, of which waited for: 19 -> 19; matrix products, arithmetic and copies ran while one was open for 16% -> 15% of each run, Pallas kernels for 10% -> 11%
where the time goes in v7:
time: 145 us; the launch traced here: 144 us
  starting transfers between devices  44.3 us (31%)
  waiting for transfers between devices  37.2 us (26%)
  Pallas kernels  29.3 us (20%)
  local copies, waits for them, and re-layouts  18.5 us (13%)
  other arithmetic  9.04 us (6%)
  matrix products  4.95 us (3%)
    ppermute x39, starting transfers between devices, hop(): return lax.ppermute(value, axis, [(i, i ^ mask) for i in range(size)])  39.5 us
    ppermute x39, waiting for transfers between devices, hop(): return lax.ppermute(value, axis, [(i, i ^ mask) for i in range(size)])  37.2 us
    pallas_call x3, Pallas kernels, expert_rows(): pl.pallas_call(functools.partial(expert_kernel, blocks=blocks, heights=he...  13.9 us
    unnamed x55, local copies, waits for them, and re-layouts  11.2 us
    pallas_call x1, Pallas kernels, attend(): pl.pallas_call(functools.partial(attend_kernel, scale=QKD ** (-0.5)), gri...  6.12 us
    pallas_call x1, Pallas kernels, project(): pl.pallas_call(functools.partial(project_kernel, counts=counts, rows=rows...  5.59 us
    all_to_all x1, starting transfers between devices, on_device(): lax.all_to_all(residual_blocks, 'dev', split_axis=0, concat_axis=0, tiled...  4.79 us
    pallas_call x1, Pallas kernels, lower_kept(): pl.pallas_call(functools.partial(lower_kernel, sizes=sizes, kept=True), i...  3.7 us
  transfers between devices with their start and end apart: 40, of which 19 were waited for; matrix products, arithmetic and copies ran while one was open for 15% of the time, Pallas kernels for 11%

profile of v7, /device:TPU:0, one launch (start us, length us, event | category | flops | bytes accessed | tf_op | source)
XLA Modules:
  0.0 144.1 jit_solution(13361117854079430474)
XLA Ops:
  2.0 6.1 %shard_map.109 = (bf16[16,32,512]{2,1,0:T(8,128)(2,1)S(1)}, bf16[16,32,512]{2,1,0:T(8,128)(2,1)S(1)}, f32[16,64,128]{2,1,0:T(8,128)S(1)}) custom-call(s32[16]{0:T(128)S(1)} %copy-done.2, s32[1]{0:T(128)} %bitcast.33.side_ref, bf16[16,64,576]{2,1,0:T(8,128)(2,1)S(1)} %copy-done, bf16[16,576,384]{2,1,0:T(8,128)(2,1)} %bitcast.145), custom_call_target="tpu_custom_call" | custom-call | flops 905969664 | bytes 8257536 | tf_op jit(solution)/shard_map/pallas_call | solution.py:90
  10.9 3.3 %fusion = bf16[32,2,8,128]{3,2,1,0:T(8,128)(2,1)S(1)} fusion(bf16[32,512,128]{2,1,0:T(8,128)(2,1)} %param.14, bf16[16,32,512]{2,1,0:T(8,128)(2,1)S(1)} %add_convert_fusion), kind=kOutput, calls=%fused_computation.4 | convolution fusion | flops 67174400 | bytes 4849664 | tf_op jit(solution)/shard_map/rhc,hcv->rhv/dot_general | solution.py:512
  14.3 3.0 %collective-permute-start.2 = (bf16[16,4224]{1,0:T(8,128)(2,1)S(1)}, bf16[16,4224]{1,0:T(8,128)(2,1)S(1)}, u32[]{:S(2)}, u32[]{:S(2)}) collective-permute-start(bf16[16,4224]{1,0:T(8,128)(2,1)S(1)} %pad_maximum_fusion.9), channel_id=1, source_target_pairs={{0,4},{1,5},{2,6},{3,7},{4,0},{5,1},{6,2},{7,3},{8,12},{9,13},{10,... | collective-permute-start | bytes 405512 | tf_op jit(solution)/shard_map/ppermute | solution.py:18
  17.3 2.6 %collective-permute-start.5 = (bf16[16,4224]{1,0:T(8,128)(2,1)S(1)}, bf16[16,4224]{1,0:T(8,128)(2,1)S(1)}, u32[]{:S(2)}, u32[]{:S(2)}) collective-permute-start(bf16[16,4224]{1,0:T(8,128)(2,1)S(1)} %pad_maximum_fusion.9), channel_id=1, source_target_pairs={{0,8},{1,9},{2,10},{3,11},{4,12},{5,13},{6,14},{7,15},{8,0},{9,1},... | collective-permute-start | bytes 405512 | tf_op jit(solution)/shard_map/ppermute | solution.py:18
  19.8 4.6 %copy.63 = bf16[896,8,2,256]{3,1,2,0:T(8,128)(2,1)} copy(bf16[896,8,2,256]{3,2,1,0:T(2,128)(2,1)S(1)} %bitcast.144) | data formatting | bytes 14680064
  24.5 1.8 %collective-permute-start.10 = (bf16[2,16,2048]{2,1,0:T(8,128)(2,1)S(1)}, bf16[2,16,2048]{2,1,0:T(8,128)(2,1)S(1)}, u32[]{:S(2)}, u32[]{:S(2)}) collective-permute-start(bf16[2,16,2048]{2,1,0:T(8,128)(2,1)S(1)} %fusion.17.refs_6_), channel_id=1, source_target_pairs={{0,2},{1,3},{2,0},{3,1},{4,6},{5,7},{6,4},{7,5},{8,10},{9,11},{10,... | collective-permute-start | bytes 393224 | tf_op jit(solution)/shard_map/ppermute | solution.py:18
  26.3 4.1 %collective-permute-done.5 = bf16[16,4224]{1,0:T(8,128)(2,1)S(1)} collective-permute-done((bf16[16,4224]{1,0:T(8,128)(2,1)S(1)}, bf16[16,4224]{1,0:T(8,128)(2,1)S(1)}, u32[]{:S(2)}, u32[]{:S(2)}) %collective-permute-start.5) | collective-permute-done | bytes 135200 | tf_op jit(solution)/shard_map/ppermute | solution.py:18
  37.0 1.9 %collective-permute-start.4 = (bf16[4,16,2176]{2,1,0:T(8,128)(2,1)S(1)}, bf16[4,16,2176]{2,1,0:T(8,128)(2,1)S(1)}, u32[]{:S(2)}, u32[]{:S(2)}) collective-permute-start(bf16[4,16,2176]{2,1,0:T(8,128)(2,1)S(1)} %pad_maximum_fusion.4), channel_id=1, source_target_pairs={{0,2},{1,3},{2,0},{3,1},{4,6},{5,7},{6,4},{7,5},{8,10},{9,11},{10,... | collective-permute-start | bytes 835592 | tf_op jit(solution)/shard_map/ppermute | solution.py:18
  39.9 1.9 %collective-permute-start.9 = (bf16[4,16,2176]{2,1,0:T(8,128)(2,1)S(1)}, bf16[4,16,2176]{2,1,0:T(8,128)(2,1)S(1)}, u32[]{:S(2)}, u32[]{:S(2)}) collective-permute-start(bf16[4,16,2176]{2,1,0:T(8,128)(2,1)S(1)} %pad_maximum_fusion.5), channel_id=1, source_target_pairs={{0,2},{1,3},{2,0},{3,1},{4,6},{5,7},{6,4},{7,5},{8,10},{9,11},{10,... | collective-permute-start | bytes 835592 | tf_op jit(solution)/shard_map/ppermute | solution.py:18
  45.0 4.8 %all-to-all-start = ((bf16[16,8,448]{2,1,0:T(8,128)(2,1)}), bf16[16,8,448]{2,1,0:T(8,128)(2,1)S(1)}, u32[]{:S(2)}, u32[]{:S(2)}) async-start(bf16[16,8,448]{2,1,0:T(8,128)(2,1)} %bitcast.135), calls=%async_computation | async-start | bytes 262144 | tf_op jit(solution)/shard_map/all_to_all | solution.py:537
  52.0 5.6 %shard_map.110 = (f32[448,128]{1,0:T(8,128)}, bf16[448,128]{1,0:T(8,128)(2,1)}) custom-call(s32[33]{0:T(128)} %stack.363.place_ref, bf16[2,16,2176]{2,1,0:T(8,128)(2,1)} %copy-done.6, bf16[2,16,2176]{2,1,0:T(8,128)(2,1)} %copy-done.11, bf16[4,16,2176]{2,1,0:T(8,128)(2,1)} %copy-done.17, bf16[2,16,2176]{2,1,0:T(8,128)(2,1)} %copy-done.7, ...), custom_call_target="tpu_custom_call" | custom-call | flops 939524096 | bytes 5767168 | tf_op jit(solution)/shard_map/pallas_call | solution.py:183
  60.4 2.0 %collective-permute-start.14 = (bf16[448,128]{1,0:T(8,128)(2,1)S(1)}, bf16[448,128]{1,0:T(8,128)(2,1)S(1)}, u32[]{:S(2)}, u32[]{:S(2)}) collective-permute-start(bf16[448,128]{1,0:T(8,128)(2,1)S(1)} %fusion.15), channel_id=1, source_target_pairs={{0,4},{1,5},{2,6},{3,7},{4,0},{5,1},{6,2},{7,3},{8,12},{9,13},{10,... | collective-permute-start | bytes 344072 | tf_op jit(solution)/shard_map/ppermute | solution.py:18
  62.4 2.4 %collective-permute-start.15 = (bf16[448,128]{1,0:T(8,128)(2,1)S(1)}, bf16[448,128]{1,0:T(8,128)(2,1)S(1)}, u32[]{:S(2)}, u32[]{:S(2)}) collective-permute-start(bf16[448,128]{1,0:T(8,128)(2,1)S(1)} %fusion.15), channel_id=1, source_target_pairs={{0,8},{1,9},{2,10},{3,11},{4,12},{5,13},{6,14},{7,15},{8,0},{9,1},... | collective-permute-start | bytes 344072 | tf_op jit(solution)/shard_map/ppermute | solution.py:18
  68.1 6.2 %collective-permute-done.15 = bf16[448,128]{1,0:T(8,128)(2,1)S(1)} collective-permute-done((bf16[448,128]{1,0:T(8,128)(2,1)S(1)}, bf16[448,128]{1,0:T(8,128)(2,1)S(1)}, u32[]{:S(2)}, u32[]{:S(2)}) %collective-permute-start.15) | collective-permute-done | bytes 114720 | tf_op jit(solution)/shard_map/ppermute | solution.py:18
  77.3 3.1 %collective-permute-done.18.refs_0_ = bf16[4,224,128]{2,1,0:T(8,128)(2,1)S(1)} collective-permute-done((bf16[4,224,128]{2,1,0:T(8,128)(2,1)S(1)}, bf16[4,224,128]{2,1,0:T(8,128)(2,1)S(1)}, u32[]{:S(2)}, u32[]{:S(2)}) %collective-permute-start.18) | collective-permute-done | bytes 229408 | tf_op jit(solution)/shard_map/ppermute | solution.py:18
  86.1 3.0 %shard_map.111 = (f32[256,512]{1,0:T(8,128)S(1)}, f32[8,256]{1,0:T(8,128)S(1)}) custom-call(s32[16]{0:T(128)S(1)} %stack.410.place_ref, bf16[4,224,128]{2,1,0:T(8,128)(2,1)S(1)} %get-tuple-element.89.refs_0_, bf16[4,224,128]{2,1,0:T(8,128)(2,1)S(1)} %get-tuple-element.92.refs_1_, bf16[4,224,128]{2,1,0:T(8,128)(2,1)S(1)} %collective-permute-done.24.refs_2_, ...), custom_call_target="tpu_custom_call" | custom-call | flops 469762048 | bytes 2752512 | tf_op jit(solution)/shard_map/pallas_call | solution.py:419
  89.1 3.1 %shard_map.112 = (f32[256,512]{1,0:T(8,128)S(1)}, f32[8,256]{1,0:T(8,128)S(1)}) custom-call(s32[16]{0:T(128)S(1)} %stack.401.place_ref, bf16[4,224,128]{2,1,0:T(8,128)(2,1)S(1)} %collective-permute-done.18.refs_0_, bf16[4,224,128]{2,1,0:T(8,128)(2,1)S(1)} %collective-permute-done.19.refs_1_, bf16[4,224,128]{2,1,0:T(8,128)(2,1)S(1)} %collective-permute-done.22.refs_2_, ...), custom_call_target="tpu_custom_call" | custom-call | flops 469762048 | bytes 2752512 | tf_op jit(solution)/shard_map/pallas_call | solution.py:419
  96.5 7.8 %shard_map.113 = (bf16[256,256]{1,0:T(8,128)(2,1)S(1)}, bf16[64,3584]{1,0:T(8,128)(2,1)S(1)}, bf16[64,3584]{1,0:T(8,128)(2,1)S(1)}, bf16[64,3584]{1,0:T(8,128)(2,1)S(1)}, bf16[64,3584]{1,0:T(8,128)(2,1)}) custom-call(s32[48]{0:T(128)S(1)} %stack.392.place_ref, bf16[8,224,128]{2,1,0:T(8,128)(2,1)S(1)} %collective-permute-done.20.refs_0_, ...), custom_call_target="tpu_custom_call" | custom-call | flops 939524096 | bytes 5505024 | tf_op jit(solution)/shard_map/pallas_call | solution.py:419
  110.5 3.7 %shard_map.114 = (bf16[64,3584]{1,0:T(8,128)(2,1)S(1)}, bf16[64,3584]{1,0:T(8,128)(2,1)S(1)}, bf16[64,3584]{1,0:T(8,128)(2,1)S(1)}, bf16[64,3584]{1,0:T(8,128)(2,1)}) custom-call(bf16[256,256]{1,0:T(8,128)(2,1)S(1)} %get-tuple-element.96.activated_ref, bf16[256,7168]{1,0:T(8,128)(2,1)} %bitcast.143), custom_call_target="tpu_custom_call" | custom-call | flops 469762048 | bytes 5505024 | tf_op jit(solution)/shard_map/pallas_call | solution.py:364
  121.6 1.8 %collective-permute-start.35 = (bf16[32,3584]{1,0:T(8,128)(2,1)S(1)}, bf16[32,3584]{1,0:T(8,128)(2,1)S(1)}, u32[]{:S(2)}, u32[]{:S(2)}) collective-permute-start(bf16[32,3584]{1,0:T(8,128)(2,1)S(1)} %slice.196), channel_id=1, source_target_pairs={{0,1},{1,0},{2,3},{3,2},{4,5},{5,4},{6,7},{7,6},{8,9},{9,8},{10,11... | collective-permute-start | bytes 688136 | tf_op jit(solution)/shard_map/ppermute | solution.py:18
  125.4 3.1 %collective-permute-done.35 = bf16[32,3584]{1,0:T(8,128)(2,1)S(1)} collective-permute-done((bf16[32,3584]{1,0:T(8,128)(2,1)S(1)}, bf16[32,3584]{1,0:T(8,128)(2,1)S(1)}, u32[]{:S(2)}, u32[]{:S(2)}) %collective-permute-start.35) | collective-permute-done | bytes 229408 | tf_op jit(solution)/shard_map/ppermute | solution.py:18
  128.5 2.8 %collective-permute-done.32 = bf16[32,3584]{1,0:T(8,128)(2,1)S(1)} collective-permute-done((bf16[32,3584]{1,0:T(8,128)(2,1)S(1)}, bf16[32,3584]{1,0:T(8,128)(2,1)S(1)}, u32[]{:S(2)}, u32[]{:S(2)}) %collective-permute-start.32) | collective-permute-done | bytes 229408 | tf_op jit(solution)/shard_map/ppermute | solution.py:18
  131.5 2.0 %collective-permute-start.36 = (bf16[8,7168]{1,0:T(8,128)(2,1)S(1)}, bf16[8,7168]{1,0:T(8,128)(2,1)S(1)}, u32[]{:S(2)}, u32[]{:S(2)}) collective-permute-start(bf16[8,7168]{1,0:T(8,128)(2,1)S(1)} %get-tuple-element.105), channel_id=1, source_target_pairs={{0,4},{1,5},{2,6},{3,7},{4,0},{5,1},{6,2},{7,3},{8,12},{9,13},{10,... | collective-permute-start | bytes 344072 | tf_op jit(solution)/shard_map/ppermute | solution.py:18
  137.1 6.3 %collective-permute-done.37 = bf16[8,7168]{1,0:T(8,128)(2,1)S(1)} collective-permute-done((bf16[8,7168]{1,0:T(8,128)(2,1)S(1)}, bf16[8,7168]{1,0:T(8,128)(2,1)S(1)}, u32[]{:S(2)}, u32[]{:S(2)}) %collective-permute-start.37) | collective-permute-done | bytes 114720 | tf_op jit(solution)/shard_map/ppermute | solution.py:18
  (197 shorter events, 56.4 us)
Async XLA Ops:
  14.3 10.2 %collective-permute-start.2 = (bf16[16,4224]{1,0:T(8,128)(2,1)S(1)}, bf16[16,4224]{1,0:T(8,128)(2,1)S(1)}, u32[]{:S(2)}, u32[]{:S(2)}) collective-permute-start(bf16[16,4224]{1,0:T(8,128)(2,1)S(1)} %pad_maximum_fusion.9), channel_id=1, source_target_pairs={{0,4},{1,5},{2,6},{3,7},{4,0},{5,1},{6,2},{7,3},{8,12},{9,13},{10,... | collective-permute-start | bytes 405512 | tf_op jit(solution)/shard_map/ppermute | solution.py:18
  17.3 13.2 %collective-permute-start.5 = (bf16[16,4224]{1,0:T(8,128)(2,1)S(1)}, bf16[16,4224]{1,0:T(8,128)(2,1)S(1)}, u32[]{:S(2)}, u32[]{:S(2)}) collective-permute-start(bf16[16,4224]{1,0:T(8,128)(2,1)S(1)} %pad_maximum_fusion.9), channel_id=1, source_target_pairs={{0,8},{1,9},{2,10},{3,11},{4,12},{5,13},{6,14},{7,15},{8,0},{9,1},... | collective-permute-start | bytes 405512 | tf_op jit(solution)/shard_map/ppermute | solution.py:18
  19.8 10.6 %collective-permute-start.6 = (bf16[16,4224]{1,0:T(8,128)(2,1)S(1)}, bf16[16,4224]{1,0:T(8,128)(2,1)S(1)}, u32[]{:S(2)}, u32[]{:S(2)}) collective-permute-start(bf16[16,4224]{1,0:T(8,128)(2,1)S(1)} %pad_maximum_fusion.9), channel_id=1, source_target_pairs={{0,12},{1,13},{2,14},{3,15},{4,8},{5,9},{6,10},{7,11},{8,4},{9,5},... | collective-permute-start | bytes 405512 | tf_op jit(solution)/shard_map/ppermute | solution.py:18
  24.5 10.3 %collective-permute-start.10 = (bf16[2,16,2048]{2,1,0:T(8,128)(2,1)S(1)}, bf16[2,16,2048]{2,1,0:T(8,128)(2,1)S(1)}, u32[]{:S(2)}, u32[]{:S(2)}) collective-permute-start(bf16[2,16,2048]{2,1,0:T(8,128)(2,1)S(1)} %fusion.17.refs_6_), channel_id=1, source_target_pairs={{0,2},{1,3},{2,0},{3,1},{4,6},{5,7},{6,4},{7,5},{8,10},{9,11},{10,... | collective-permute-start | bytes 393224 | tf_op jit(solution)/shard_map/ppermute | solution.py:18
  30.5 6.4 %collective-permute-start.3 = (bf16[2,16,2176]{2,1,0:T(8,128)(2,1)S(1)}, bf16[2,16,2176]{2,1,0:T(8,128)(2,1)S(1)}, u32[]{:S(2)}, u32[]{:S(2)}) collective-permute-start(bf16[2,16,2176]{2,1,0:T(8,128)(2,1)S(1)} %fusion.16.refs_0_), channel_id=1, source_target_pairs={{0,1},{1,0},{2,3},{3,2},{4,5},{5,4},{6,7},{7,6},{8,9},{9,8},{10,11... | collective-permute-start | bytes 417800 | tf_op jit(solution)/shard_map/ppermute | solution.py:18
  32.1 7.8 %collective-permute-start.7 = (bf16[2,16,2176]{2,1,0:T(8,128)(2,1)S(1)}, bf16[2,16,2176]{2,1,0:T(8,128)(2,1)S(1)}, u32[]{:S(2)}, u32[]{:S(2)}) collective-permute-start(bf16[2,16,2176]{2,1,0:T(8,128)(2,1)S(1)} %slice.111.refs_3_), channel_id=1, source_target_pairs={{0,1},{1,0},{2,3},{3,2},{4,5},{5,4},{6,7},{7,6},{8,9},{9,8},{10,11... | collective-permute-start | bytes 417800 | tf_op jit(solution)/shard_map/ppermute | solution.py:18
  34.8 16.2 %collective-permute-start.11 = (bf16[4,16,2048]{2,1,0:T(8,128)(2,1)S(1)}, bf16[4,16,2048]{2,1,0:T(8,128)(2,1)S(1)}, u32[]{:S(2)}, u32[]{:S(2)}) collective-permute-start(bf16[4,16,2048]{2,1,0:T(8,128)(2,1)S(1)} %pad_maximum_fusion.7), channel_id=1, source_target_pairs={{0,1},{1,0},{2,3},{3,2},{4,5},{5,4},{6,7},{7,6},{8,9},{9,8},{10,11... | collective-permute-start | bytes 786440 | tf_op jit(solution)/shard_map/ppermute | solution.py:18
  37.0 13.4 %collective-permute-start.4 = (bf16[4,16,2176]{2,1,0:T(8,128)(2,1)S(1)}, bf16[4,16,2176]{2,1,0:T(8,128)(2,1)S(1)}, u32[]{:S(2)}, u32[]{:S(2)}) collective-permute-start(bf16[4,16,2176]{2,1,0:T(8,128)(2,1)S(1)} %pad_maximum_fusion.4), channel_id=1, source_target_pairs={{0,2},{1,3},{2,0},{3,1},{4,6},{5,7},{6,4},{7,5},{8,10},{9,11},{10,... | collective-permute-start | bytes 835592 | tf_op jit(solution)/shard_map/ppermute | solution.py:18
  39.9 11.1 %collective-permute-start.9 = (bf16[4,16,2176]{2,1,0:T(8,128)(2,1)S(1)}, bf16[4,16,2176]{2,1,0:T(8,128)(2,1)S(1)}, u32[]{:S(2)}, u32[]{:S(2)}) collective-permute-start(bf16[4,16,2176]{2,1,0:T(8,128)(2,1)S(1)} %pad_maximum_fusion.5), channel_id=1, source_target_pairs={{0,2},{1,3},{2,0},{3,1},{4,6},{5,7},{6,4},{7,5},{8,10},{9,11},{10,... | collective-permute-start | bytes 835592 | tf_op jit(solution)/shard_map/ppermute | solution.py:18
  42.6 8.4 %collective-permute-start.12 = (bf16[4,16,2048]{2,1,0:T(8,128)(2,1)}, bf16[4,16,2048]{2,1,0:T(8,128)(2,1)S(1)}, u32[]{:S(2)}, u32[]{:S(2)}) collective-permute-start(bf16[4,16,2048]{2,1,0:T(8,128)(2,1)} %pad_maximum_fusion.8), channel_id=1, source_target_pairs={{0,1},{1,0},{2,3},{3,2},{4,5},{5,4},{6,7},{7,6},{8,9},{9,8},{10,11... | collective-permute-start | bytes 786440 | tf_op jit(solution)/shard_map/ppermute | solution.py:18
  45.0 12.7 %all-to-all-start = ((bf16[16,8,448]{2,1,0:T(8,128)(2,1)}), bf16[16,8,448]{2,1,0:T(8,128)(2,1)S(1)}, u32[]{:S(2)}, u32[]{:S(2)}) async-start(bf16[16,8,448]{2,1,0:T(8,128)(2,1)} %bitcast.135), calls=%async_computation | async-start | bytes 262144 | tf_op jit(solution)/shard_map/all_to_all | solution.py:537
  60.4 7.7 %collective-permute-start.14 = (bf16[448,128]{1,0:T(8,128)(2,1)S(1)}, bf16[448,128]{1,0:T(8,128)(2,1)S(1)}, u32[]{:S(2)}, u32[]{:S(2)}) collective-permute-start(bf16[448,128]{1,0:T(8,128)(2,1)S(1)} %fusion.15), channel_id=1, source_target_pairs={{0,4},{1,5},{2,6},{3,7},{4,0},{5,1},{6,2},{7,3},{8,12},{9,13},{10,... | collective-permute-start | bytes 344072 | tf_op jit(solution)/shard_map/ppermute | solution.py:18
  62.4 11.8 %collective-permute-start.15 = (bf16[448,128]{1,0:T(8,128)(2,1)S(1)}, bf16[448,128]{1,0:T(8,128)(2,1)S(1)}, u32[]{:S(2)}, u32[]{:S(2)}) collective-permute-start(bf16[448,128]{1,0:T(8,128)(2,1)S(1)} %fusion.15), channel_id=1, source_target_pairs={{0,8},{1,9},{2,10},{3,11},{4,12},{5,13},{6,14},{7,15},{8,0},{9,1},... | collective-permute-start | bytes 344072 | tf_op jit(solution)/shard_map/ppermute | solution.py:18
  64.7 9.5 %collective-permute-start.16 = (bf16[448,128]{1,0:T(8,128)(2,1)S(1)}, bf16[448,128]{1,0:T(8,128)(2,1)S(1)}, u32[]{:S(2)}, u32[]{:S(2)}) collective-permute-start(bf16[448,128]{1,0:T(8,128)(2,1)S(1)} %fusion.15), channel_id=1, source_target_pairs={{0,12},{1,13},{2,14},{3,15},{4,8},{5,9},{6,10},{7,11},{8,4},{9,5},... | collective-permute-start | bytes 344072 | tf_op jit(solution)/shard_map/ppermute | solution.py:18
  77.3 7.8 %collective-permute-start.24 = (bf16[4,224,128]{2,1,0:T(8,128)(2,1)S(1)}, bf16[4,224,128]{2,1,0:T(8,128)(2,1)S(1)}, u32[]{:S(2)}, u32[]{:S(2)}) collective-permute-start(bf16[4,224,128]{2,1,0:T(8,128)(2,1)S(1)} %get-tuple-element.89.refs_0_), channel_id=1, source_target_pairs={{0,16},{16,0},{1,17},{17,1},{2,18},{18,2},{3,19},{19,3},{4,20},{20... | collective-permute-start | bytes 688136 | tf_op jit(solution)/shard_map/ppermute | solution.py:18
  82.2 10.9 %collective-permute-start.21 = (bf16[8,224,128]{2,1,0:T(8,128)(2,1)S(1)}, bf16[8,224,128]{2,1,0:T(8,128)(2,1)S(1)}, u32[]{:S(2)}, u32[]{:S(2)}) collective-permute-start(bf16[8,224,128]{2,1,0:T(8,128)(2,1)S(1)} %pad_maximum_fusion.3), channel_id=1, source_target_pairs={{0,1},{1,0},{2,3},{3,2},{4,5},{5,4},{6,7},{7,6},{8,9},{9,8},{10,11... | collective-permute-start | bytes 1376264 | tf_op jit(solution)/shard_map/ppermute | solution.py:18
  82.6 10.5 %collective-permute-start.20 = (bf16[8,224,128]{2,1,0:T(8,128)(2,1)S(1)}, bf16[8,224,128]{2,1,0:T(8,128)(2,1)S(1)}, u32[]{:S(2)}, u32[]{:S(2)}) collective-permute-start(bf16[8,224,128]{2,1,0:T(8,128)(2,1)S(1)} %pad_maximum_fusion.2), channel_id=1, source_target_pairs={{0,2},{1,3},{2,0},{3,1},{4,6},{5,7},{6,4},{7,5},{8,10},{9,11},{10,... | collective-permute-start | bytes 1376264 | tf_op jit(solution)/shard_map/ppermute | solution.py:18
  107.4 12.9 %collective-permute-start.34 = (bf16[64,3584]{1,0:T(8,128)(2,1)}, bf16[64,3584]{1,0:T(8,128)(2,1)}, u32[]{:S(2)}, u32[]{:S(2)}) collective-permute-start(bf16[64,3584]{1,0:T(8,128)(2,1)} %add_convert_fusion.1), channel_id=1, source_target_pairs={{0,2},{1,3},{2,0},{3,1},{4,6},{5,7},{6,4},{7,5},{8,10},{9,11},{10,... | collective-permute-start | bytes 1376264 | tf_op jit(solution)/shard_map/ppermute | solution.py:18
  108.8 14.6 %collective-permute-start.31 = (bf16[64,3584]{1,0:T(8,128)(2,1)}, bf16[64,3584]{1,0:T(8,128)(2,1)}, u32[]{:S(2)}, u32[]{:S(2)}) collective-permute-start(bf16[64,3584]{1,0:T(8,128)(2,1)} %add_convert_fusion.2), channel_id=1, source_target_pairs={{0,1},{1,0},{2,3},{3,2},{4,5},{5,4},{6,7},{7,6},{8,9},{9,8},{10,11... | collective-permute-start | bytes 1376264 | tf_op jit(solution)/shard_map/ppermute | solution.py:18
  114.3 9.1 %collective-permute-start.30 = (bf16[64,3584]{1,0:T(8,128)(2,1)S(1)}, bf16[64,3584]{1,0:T(8,128)(2,1)}, u32[]{:S(2)}, u32[]{:S(2)}) collective-permute-start(bf16[64,3584]{1,0:T(8,128)(2,1)S(1)} %get-tuple-element.98), channel_id=1, source_target_pairs={{0,16},{16,0},{1,17},{17,1},{2,18},{18,2},{3,19},{19,3},{4,20},{20... | collective-permute-start | bytes 1376264 | tf_op jit(solution)/shard_map/ppermute | solution.py:18
  121.6 6.9 %collective-permute-start.35 = (bf16[32,3584]{1,0:T(8,128)(2,1)S(1)}, bf16[32,3584]{1,0:T(8,128)(2,1)S(1)}, u32[]{:S(2)}, u32[]{:S(2)}) collective-permute-start(bf16[32,3584]{1,0:T(8,128)(2,1)S(1)} %slice.196), channel_id=1, source_target_pairs={{0,1},{1,0},{2,3},{3,2},{4,5},{5,4},{6,7},{7,6},{8,9},{9,8},{10,11... | collective-permute-start | bytes 688136 | tf_op jit(solution)/shard_map/ppermute | solution.py:18
  124.7 6.6 %collective-permute-start.32 = (bf16[32,3584]{1,0:T(8,128)(2,1)S(1)}, bf16[32,3584]{1,0:T(8,128)(2,1)S(1)}, u32[]{:S(2)}, u32[]{:S(2)}) collective-permute-start(bf16[32,3584]{1,0:T(8,128)(2,1)S(1)} %slice.197), channel_id=1, source_target_pairs={{0,2},{1,3},{2,0},{3,1},{4,6},{5,7},{6,4},{7,5},{8,10},{9,11},{10,... | collective-permute-start | bytes 688136 | tf_op jit(solution)/shard_map/ppermute | solution.py:18
  133.5 9.9 %collective-permute-start.37 = (bf16[8,7168]{1,0:T(8,128)(2,1)S(1)}, bf16[8,7168]{1,0:T(8,128)(2,1)S(1)}, u32[]{:S(2)}, u32[]{:S(2)}) collective-permute-start(bf16[8,7168]{1,0:T(8,128)(2,1)S(1)} %get-tuple-element.107), channel_id=1, source_target_pairs={{0,8},{1,9},{2,10},{3,11},{4,12},{5,13},{6,14},{7,15},{8,0},{9,1},... | collective-permute-start | bytes 344072 | tf_op jit(solution)/shard_map/ppermute | solution.py:18
  134.5 9.0 %collective-permute-start.38 = (bf16[8,7168]{1,0:T(8,128)(2,1)S(1)}, bf16[8,7168]{1,0:T(8,128)(2,1)S(1)}, u32[]{:S(2)}, u32[]{:S(2)}) collective-permute-start(bf16[8,7168]{1,0:T(8,128)(2,1)S(1)} %get-tuple-element.106), channel_id=1, source_target_pairs={{0,12},{1,13},{2,14},{3,15},{4,8},{5,9},{6,10},{7,11},{8,4},{9,5},... | collective-permute-start | bytes 344072 | tf_op jit(solution)/shard_map/ppermute | solution.py:18
  (41 other events, 293.3 us)

commit v8 on v7

--- a/solution.py
+++ b/solution.py
@@ -198,7 +198,7 @@
             pltpu.SemaphoreType.DMA((2 * sum(counts),)),
             pltpu.SemaphoreType.DMA((steps,)),
         ],
-        compiler_params=pltpu.CompilerParams(vmem_limit_bytes=60 * 2**20),
+        compiler_params=pltpu.CompilerParams(vmem_limit_bytes=50 * 2**20),
         cost_estimate=pl.CostEstimate(
             flops=2 * total_rows * depth * width,
             bytes_accessed=2 * (total_rows * depth + depth * width),

time: 145 us -> 143 us (0.986)
  local copies, waits for them, and re-layouts: 18.5 us -> 13.9 us
  waiting for transfers between devices: 37.2 us -> 40.7 us
    unnamed x55 -> x29, local copies, waits for them, and re-layouts: 11.2 us -> 7.87 us
    ppermute x39, waiting for transfers between devices: 37.2 us -> 39.8 us  [hop(): return lax.ppermute(value, axis, [(i, i ^ mask) for i in range(size)])]
  transfers between devices with their start and end apart: 40 -> 40, of which waited for: 19 -> 21; matrix products, arithmetic and copies ran while one was open for 15% -> 13% of each run, Pallas kernels for 11% -> 11%
where the time goes in v8:
time: 143 us
  starting transfers between devices  44.1 us (31%)
  waiting for transfers between devices  40.7 us (28%)
  Pallas kernels  30.3 us (21%)
  local copies, waits for them, and re-layouts  13.9 us (10%)
  other arithmetic  8.19 us (6%)
  matrix products  5.03 us (4%)
    ppermute x39, waiting for transfers between devices, hop(): return lax.ppermute(value, axis, [(i, i ^ mask) for i in range(size)])  39.8 us
    ppermute x39, starting transfers between devices, hop(): return lax.ppermute(value, axis, [(i, i ^ mask) for i in range(size)])  39.3 us
    pallas_call x3, Pallas kernels, expert_rows(): pl.pallas_call(functools.partial(expert_kernel, blocks=blocks, heights=he...  13.9 us
    unnamed x29, local copies, waits for them, and re-layouts  7.87 us
    pallas_call x1, Pallas kernels, project(): pl.pallas_call(functools.partial(project_kernel, counts=counts, rows=rows...  6.59 us
    pallas_call x1, Pallas kernels, attend(): pl.pallas_call(functools.partial(attend_kernel, scale=QKD ** (-0.5)), gri...  6.12 us
    all_to_all x1, starting transfers between devices, on_device(): lax.all_to_all(residual_blocks, 'dev', split_axis=0, concat_axis=0, tiled...  4.77 us
    pallas_call x1, Pallas kernels, lower_kept(): pl.pallas_call(functools.partial(lower_kernel, sizes=sizes, kept=True), i...  3.67 us
  transfers between devices with their start and end apart: 40, of which 21 were waited for; matrix products, arithmetic and copies ran while one was open for 13% of the time, Pallas kernels for 11%

profile of v8, /device:TPU:0, one launch (start us, length us, event | category | flops | bytes accessed | tf_op | source)
XLA Modules:
  0.0 142.9 jit_solution(11706314257431917010)
XLA Ops:
  2.0 6.1 %shard_map.109 = (bf16[16,32,512]{2,1,0:T(8,128)(2,1)S(1)}, bf16[16,32,512]{2,1,0:T(8,128)(2,1)S(1)}, f32[16,64,128]{2,1,0:T(8,128)S(1)}) custom-call(s32[16]{0:T(128)S(1)} %copy-done.2, s32[1]{0:T(128)} %bitcast.33.side_ref, bf16[16,64,576]{2,1,0:T(8,128)(2,1)S(1)} %copy-done, bf16[16,576,384]{2,1,0:T(8,128)(2,1)} %bitcast.145), custom_call_target="tpu_custom_call" | custom-call | flops 905969664 | bytes 8257536 | tf_op jit(solution)/shard_map/pallas_call | solution.py:90
  10.9 3.4 %fusion = bf16[32,2,8,128]{3,2,1,0:T(8,128)(2,1)S(1)} fusion(bf16[32,512,128]{2,1,0:T(8,128)(2,1)} %param.14, bf16[16,32,512]{2,1,0:T(8,128)(2,1)S(1)} %add_convert_fusion), kind=kOutput, calls=%fused_computation.4 | convolution fusion | flops 67174400 | bytes 4849664 | tf_op jit(solution)/shard_map/rhc,hcv->rhv/dot_general | solution.py:512
  14.3 3.0 %collective-permute-start.2 = (bf16[16,4224]{1,0:T(8,128)(2,1)S(1)}, bf16[16,4224]{1,0:T(8,128)(2,1)S(1)}, u32[]{:S(2)}, u32[]{:S(2)}) collective-permute-start(bf16[16,4224]{1,0:T(8,128)(2,1)S(1)} %pad_maximum_fusion.9), channel_id=1, source_target_pairs={{0,4},{1,5},{2,6},{3,7},{4,0},{5,1},{6,2},{7,3},{8,12},{9,13},{10,... | collective-permute-start | bytes 405512 | tf_op jit(solution)/shard_map/ppermute | solution.py:18
  17.4 2.6 %collective-permute-start.5 = (bf16[16,4224]{1,0:T(8,128)(2,1)S(1)}, bf16[16,4224]{1,0:T(8,128)(2,1)S(1)}, u32[]{:S(2)}, u32[]{:S(2)}) collective-permute-start(bf16[16,4224]{1,0:T(8,128)(2,1)S(1)} %pad_maximum_fusion.9), channel_id=1, source_target_pairs={{0,8},{1,9},{2,10},{3,11},{4,12},{5,13},{6,14},{7,15},{8,0},{9,1},... | collective-permute-start | bytes 405512 | tf_op jit(solution)/shard_map/ppermute | solution.py:18
  20.0 4.1 %copy.63 = bf16[896,8,2,256]{3,1,2,0:T(8,128)(2,1)} copy(bf16[896,8,2,256]{3,2,1,0:T(2,128)(2,1)S(1)} %bitcast.144) | data formatting | bytes 14680064
  24.1 1.8 %collective-permute-start.10 = (bf16[2,16,2048]{2,1,0:T(8,128)(2,1)S(1)}, bf16[2,16,2048]{2,1,0:T(8,128)(2,1)S(1)}, u32[]{:S(2)}, u32[]{:S(2)}) collective-permute-start(bf16[2,16,2048]{2,1,0:T(8,128)(2,1)S(1)} %fusion.17.refs_6_), channel_id=1, source_target_pairs={{0,2},{1,3},{2,0},{3,1},{4,6},{5,7},{6,4},{7,5},{8,10},{9,11},{10,... | collective-permute-start | bytes 393224 | tf_op jit(solution)/shard_map/ppermute | solution.py:18
  25.9 4.6 %collective-permute-done.5 = bf16[16,4224]{1,0:T(8,128)(2,1)S(1)} collective-permute-done((bf16[16,4224]{1,0:T(8,128)(2,1)S(1)}, bf16[16,4224]{1,0:T(8,128)(2,1)S(1)}, u32[]{:S(2)}, u32[]{:S(2)}) %collective-permute-start.5) | collective-permute-done | bytes 135200 | tf_op jit(solution)/shard_map/ppermute | solution.py:18
  45.0 4.8 %all-to-all-start = ((bf16[16,8,448]{2,1,0:T(8,128)(2,1)}), bf16[16,8,448]{2,1,0:T(8,128)(2,1)S(1)}, u32[]{:S(2)}, u32[]{:S(2)}) async-start(bf16[16,8,448]{2,1,0:T(8,128)(2,1)} %bitcast.135), calls=%async_computation | async-start | bytes 262144 | tf_op jit(solution)/shard_map/all_to_all | solution.py:537
  50.1 6.6 %shard_map.110 = (f32[448,128]{1,0:T(8,128)S(1)}, bf16[448,128]{1,0:T(8,128)(2,1)S(1)}) custom-call(s32[33]{0:T(128)S(1)} %stack.363.place_ref, bf16[2,16,2176]{2,1,0:T(8,128)(2,1)S(1)} %fusion.16.refs_0_, bf16[2,16,2176]{2,1,0:T(8,128)(2,1)S(1)} %collective-permute-done.3.refs_1_, bf16[4,16,2176]{2,1,0:T(8,128)(2,1)S(1)} %collective-permute-done.4.refs_2_, ...), custom_call_target="tpu_custom_call" | custom-call | flops 939524096 | bytes 5767168 | tf_op jit(solution)/shard_map/pallas_call | solution.py:183
  59.2 1.7 %collective-permute-start.14 = (bf16[448,128]{1,0:T(8,128)(2,1)S(1)}, bf16[448,128]{1,0:T(8,128)(2,1)S(1)}, u32[]{:S(2)}, u32[]{:S(2)}) collective-permute-start(bf16[448,128]{1,0:T(8,128)(2,1)S(1)} %fusion.15), channel_id=1, source_target_pairs={{0,4},{1,5},{2,6},{3,7},{4,0},{5,1},{6,2},{7,3},{8,12},{9,13},{10,... | collective-permute-start | bytes 344072 | tf_op jit(solution)/shard_map/ppermute | solution.py:18
  66.2 6.6 %collective-permute-done.15 = bf16[448,128]{1,0:T(8,128)(2,1)S(1)} collective-permute-done((bf16[448,128]{1,0:T(8,128)(2,1)S(1)}, bf16[448,128]{1,0:T(8,128)(2,1)S(1)}, u32[]{:S(2)}, u32[]{:S(2)}) %collective-permute-start.15) | collective-permute-done | bytes 114720 | tf_op jit(solution)/shard_map/ppermute | solution.py:18
  76.0 2.9 %collective-permute-done.18.refs_0_ = bf16[4,224,128]{2,1,0:T(8,128)(2,1)S(1)} collective-permute-done((bf16[4,224,128]{2,1,0:T(8,128)(2,1)S(1)}, bf16[4,224,128]{2,1,0:T(8,128)(2,1)S(1)}, u32[]{:S(2)}, u32[]{:S(2)}) %collective-permute-start.18) | collective-permute-done | bytes 229408 | tf_op jit(solution)/shard_map/ppermute | solution.py:18
  78.9 1.7 %collective-permute-done.19.refs_1_ = bf16[4,224,128]{2,1,0:T(8,128)(2,1)S(1)} collective-permute-done((bf16[4,224,128]{2,1,0:T(8,128)(2,1)S(1)}, bf16[4,224,128]{2,1,0:T(8,128)(2,1)S(1)}, u32[]{:S(2)}, u32[]{:S(2)}) %collective-permute-start.19) | collective-permute-done | bytes 229408 | tf_op jit(solution)/shard_map/ppermute | solution.py:18
  84.8 3.0 %shard_map.111 = (f32[256,512]{1,0:T(8,128)S(1)}, f32[8,256]{1,0:T(8,128)S(1)}) custom-call(s32[16]{0:T(128)S(1)} %stack.410.place_ref, bf16[4,224,128]{2,1,0:T(8,128)(2,1)S(1)} %get-tuple-element.89.refs_0_, bf16[4,224,128]{2,1,0:T(8,128)(2,1)S(1)} %get-tuple-element.92.refs_1_, bf16[4,224,128]{2,1,0:T(8,128)(2,1)S(1)} %collective-permute-done.24.refs_2_, ...), custom_call_target="tpu_custom_call" | custom-call | flops 469762048 | bytes 2752512 | tf_op jit(solution)/shard_map/pallas_call | solution.py:419
  87.8 3.1 %shard_map.112 = (f32[256,512]{1,0:T(8,128)S(1)}, f32[8,256]{1,0:T(8,128)S(1)}) custom-call(s32[16]{0:T(128)S(1)} %stack.401.place_ref, bf16[4,224,128]{2,1,0:T(8,128)(2,1)S(1)} %collective-permute-done.18.refs_0_, bf16[4,224,128]{2,1,0:T(8,128)(2,1)S(1)} %collective-permute-done.19.refs_1_, bf16[4,224,128]{2,1,0:T(8,128)(2,1)S(1)} %collective-permute-done.22.refs_2_, ...), custom_call_target="tpu_custom_call" | custom-call | flops 469762048 | bytes 2752512 | tf_op jit(solution)/shard_map/pallas_call | solution.py:419
  95.1 7.8 %shard_map.113 = (bf16[256,256]{1,0:T(8,128)(2,1)S(1)}, bf16[64,3584]{1,0:T(8,128)(2,1)S(1)}, bf16[64,3584]{1,0:T(8,128)(2,1)S(1)}, bf16[64,3584]{1,0:T(8,128)(2,1)S(1)}, bf16[64,3584]{1,0:T(8,128)(2,1)}) custom-call(s32[48]{0:T(128)S(1)} %stack.392.place_ref, bf16[8,224,128]{2,1,0:T(8,128)(2,1)S(1)} %collective-permute-done.20.refs_0_, ...), custom_call_target="tpu_custom_call" | custom-call | flops 939524096 | bytes 5505024 | tf_op jit(solution)/shard_map/pallas_call | solution.py:419
  107.3 1.7 %collective-permute-start.31 = (bf16[64,3584]{1,0:T(8,128)(2,1)}, bf16[64,3584]{1,0:T(8,128)(2,1)}, u32[]{:S(2)}, u32[]{:S(2)}) collective-permute-start(bf16[64,3584]{1,0:T(8,128)(2,1)} %add_convert_fusion.2), channel_id=1, source_target_pairs={{0,1},{1,0},{2,3},{3,2},{4,5},{5,4},{6,7},{7,6},{8,9},{9,8},{10,11... | collective-permute-start | bytes 1376264 | tf_op jit(solution)/shard_map/ppermute | solution.py:18
  109.0 3.7 %shard_map.114 = (bf16[64,3584]{1,0:T(8,128)(2,1)S(1)}, bf16[64,3584]{1,0:T(8,128)(2,1)S(1)}, bf16[64,3584]{1,0:T(8,128)(2,1)S(1)}, bf16[64,3584]{1,0:T(8,128)(2,1)}) custom-call(bf16[256,256]{1,0:T(8,128)(2,1)S(1)} %get-tuple-element.96.activated_ref, bf16[256,7168]{1,0:T(8,128)(2,1)} %bitcast.143), custom_call_target="tpu_custom_call" | custom-call | flops 469762048 | bytes 5505024 | tf_op jit(solution)/shard_map/pallas_call | solution.py:364
  117.1 1.8 %collective-permute-done.34 = bf16[64,3584]{1,0:T(8,128)(2,1)} collective-permute-done((bf16[64,3584]{1,0:T(8,128)(2,1)}, bf16[64,3584]{1,0:T(8,128)(2,1)}, u32[]{:S(2)}, u32[]{:S(2)}) %collective-permute-start.34) | collective-permute-done | bytes 458784 | tf_op jit(solution)/shard_map/ppermute | solution.py:18
  120.2 1.7 %collective-permute-start.35 = (bf16[32,3584]{1,0:T(8,128)(2,1)S(1)}, bf16[32,3584]{1,0:T(8,128)(2,1)S(1)}, u32[]{:S(2)}, u32[]{:S(2)}) collective-permute-start(bf16[32,3584]{1,0:T(8,128)(2,1)S(1)} %slice.196), channel_id=1, source_target_pairs={{0,1},{1,0},{2,3},{3,2},{4,5},{5,4},{6,7},{7,6},{8,9},{9,8},{10,11... | collective-permute-start | bytes 688136 | tf_op jit(solution)/shard_map/ppermute | solution.py:18
  123.8 3.3 %collective-permute-done.35 = bf16[32,3584]{1,0:T(8,128)(2,1)S(1)} collective-permute-done((bf16[32,3584]{1,0:T(8,128)(2,1)S(1)}, bf16[32,3584]{1,0:T(8,128)(2,1)S(1)}, u32[]{:S(2)}, u32[]{:S(2)}) %collective-permute-start.35) | collective-permute-done | bytes 229408 | tf_op jit(solution)/shard_map/ppermute | solution.py:18
  127.1 2.7 %collective-permute-done.32 = bf16[32,3584]{1,0:T(8,128)(2,1)S(1)} collective-permute-done((bf16[32,3584]{1,0:T(8,128)(2,1)S(1)}, bf16[32,3584]{1,0:T(8,128)(2,1)S(1)}, u32[]{:S(2)}, u32[]{:S(2)}) %collective-permute-start.32) | collective-permute-done | bytes 229408 | tf_op jit(solution)/shard_map/ppermute | solution.py:18
  130.0 2.1 %collective-permute-start.36 = (bf16[8,7168]{1,0:T(8,128)(2,1)S(1)}, bf16[8,7168]{1,0:T(8,128)(2,1)S(1)}, u32[]{:S(2)}, u32[]{:S(2)}) collective-permute-start(bf16[8,7168]{1,0:T(8,128)(2,1)S(1)} %get-tuple-element.105), channel_id=1, source_target_pairs={{0,4},{1,5},{2,6},{3,7},{4,0},{5,1},{6,2},{7,3},{8,12},{9,13},{10,... | collective-permute-start | bytes 344072 | tf_op jit(solution)/shard_map/ppermute | solution.py:18
  135.9 6.3 %collective-permute-done.37 = bf16[8,7168]{1,0:T(8,128)(2,1)S(1)} collective-permute-done((bf16[8,7168]{1,0:T(8,128)(2,1)S(1)}, bf16[8,7168]{1,0:T(8,128)(2,1)S(1)}, u32[]{:S(2)}, u32[]{:S(2)}) %collective-permute-start.37) | collective-permute-done | bytes 114720 | tf_op jit(solution)/shard_map/ppermute | solution.py:18
  (171 shorter events, 55.2 us)
Async XLA Ops:
  14.3 9.7 %collective-permute-start.2 = (bf16[16,4224]{1,0:T(8,128)(2,1)S(1)}, bf16[16,4224]{1,0:T(8,128)(2,1)S(1)}, u32[]{:S(2)}, u32[]{:S(2)}) collective-permute-start(bf16[16,4224]{1,0:T(8,128)(2,1)S(1)} %pad_maximum_fusion.9), channel_id=1, source_target_pairs={{0,4},{1,5},{2,6},{3,7},{4,0},{5,1},{6,2},{7,3},{8,12},{9,13},{10,... | collective-permute-start | bytes 405512 | tf_op jit(solution)/shard_map/ppermute | solution.py:18
  17.4 13.2 %collective-permute-start.5 = (bf16[16,4224]{1,0:T(8,128)(2,1)S(1)}, bf16[16,4224]{1,0:T(8,128)(2,1)S(1)}, u32[]{:S(2)}, u32[]{:S(2)}) collective-permute-start(bf16[16,4224]{1,0:T(8,128)(2,1)S(1)} %pad_maximum_fusion.9), channel_id=1, source_target_pairs={{0,8},{1,9},{2,10},{3,11},{4,12},{5,13},{6,14},{7,15},{8,0},{9,1},... | collective-permute-start | bytes 405512 | tf_op jit(solution)/shard_map/ppermute | solution.py:18
  19.9 10.6 %collective-permute-start.6 = (bf16[16,4224]{1,0:T(8,128)(2,1)S(1)}, bf16[16,4224]{1,0:T(8,128)(2,1)S(1)}, u32[]{:S(2)}, u32[]{:S(2)}) collective-permute-start(bf16[16,4224]{1,0:T(8,128)(2,1)S(1)} %pad_maximum_fusion.9), channel_id=1, source_target_pairs={{0,12},{1,13},{2,14},{3,15},{4,8},{5,9},{6,10},{7,11},{8,4},{9,5},... | collective-permute-start | bytes 405512 | tf_op jit(solution)/shard_map/ppermute | solution.py:18
  24.1 10.1 %collective-permute-start.10 = (bf16[2,16,2048]{2,1,0:T(8,128)(2,1)S(1)}, bf16[2,16,2048]{2,1,0:T(8,128)(2,1)S(1)}, u32[]{:S(2)}, u32[]{:S(2)}) collective-permute-start(bf16[2,16,2048]{2,1,0:T(8,128)(2,1)S(1)} %fusion.17.refs_6_), channel_id=1, source_target_pairs={{0,2},{1,3},{2,0},{3,1},{4,6},{5,7},{6,4},{7,5},{8,10},{9,11},{10,... | collective-permute-start | bytes 393224 | tf_op jit(solution)/shard_map/ppermute | solution.py:18
  30.6 6.7 %collective-permute-start.3 = (bf16[2,16,2176]{2,1,0:T(8,128)(2,1)S(1)}, bf16[2,16,2176]{2,1,0:T(8,128)(2,1)S(1)}, u32[]{:S(2)}, u32[]{:S(2)}) collective-permute-start(bf16[2,16,2176]{2,1,0:T(8,128)(2,1)S(1)} %fusion.16.refs_0_), channel_id=1, source_target_pairs={{0,1},{1,0},{2,3},{3,2},{4,5},{5,4},{6,7},{7,6},{8,9},{9,8},{10,11... | collective-permute-start | bytes 417800 | tf_op jit(solution)/shard_map/ppermute | solution.py:18
  32.2 8.1 %collective-permute-start.7 = (bf16[2,16,2176]{2,1,0:T(8,128)(2,1)S(1)}, bf16[2,16,2176]{2,1,0:T(8,128)(2,1)S(1)}, u32[]{:S(2)}, u32[]{:S(2)}) collective-permute-start(bf16[2,16,2176]{2,1,0:T(8,128)(2,1)S(1)} %slice.111.refs_3_), channel_id=1, source_target_pairs={{0,1},{1,0},{2,3},{3,2},{4,5},{5,4},{6,7},{7,6},{8,9},{9,8},{10,11... | collective-permute-start | bytes 417800 | tf_op jit(solution)/shard_map/ppermute | solution.py:18
  32.7 6.9 %collective-permute-start.8 = (bf16[2,16,2048]{2,1,0:T(8,128)(2,1)S(1)}, bf16[2,16,2048]{2,1,0:T(8,128)(2,1)S(1)}, u32[]{:S(2)}, u32[]{:S(2)}) collective-permute-start(bf16[2,16,2048]{2,1,0:T(8,128)(2,1)S(1)} %slice.112.refs_9_), channel_id=1, source_target_pairs={{0,2},{1,3},{2,0},{3,1},{4,6},{5,7},{6,4},{7,5},{8,10},{9,11},{10,... | collective-permute-start | bytes 393224 | tf_op jit(solution)/shard_map/ppermute | solution.py:18
  34.3 15.6 %collective-permute-start.11 = (bf16[4,16,2048]{2,1,0:T(8,128)(2,1)S(1)}, bf16[4,16,2048]{2,1,0:T(8,128)(2,1)S(1)}, u32[]{:S(2)}, u32[]{:S(2)}) collective-permute-start(bf16[4,16,2048]{2,1,0:T(8,128)(2,1)S(1)} %pad_maximum_fusion.7), channel_id=1, source_target_pairs={{0,1},{1,0},{2,3},{3,2},{4,5},{5,4},{6,7},{7,6},{8,9},{9,8},{10,11... | collective-permute-start | bytes 786440 | tf_op jit(solution)/shard_map/ppermute | solution.py:18
  38.1 11.8 %collective-permute-start.4 = (bf16[4,16,2176]{2,1,0:T(8,128)(2,1)}, bf16[4,16,2176]{2,1,0:T(8,128)(2,1)S(1)}, u32[]{:S(2)}, u32[]{:S(2)}) collective-permute-start(bf16[4,16,2176]{2,1,0:T(8,128)(2,1)} %pad_maximum_fusion.4), channel_id=1, source_target_pairs={{0,2},{1,3},{2,0},{3,1},{4,6},{5,7},{6,4},{7,5},{8,10},{9,11},{10,... | collective-permute-start | bytes 835592 | tf_op jit(solution)/shard_map/ppermute | solution.py:18
  40.3 9.7 %collective-permute-start.9 = (bf16[4,16,2176]{2,1,0:T(8,128)(2,1)S(1)}, bf16[4,16,2176]{2,1,0:T(8,128)(2,1)S(1)}, u32[]{:S(2)}, u32[]{:S(2)}) collective-permute-start(bf16[4,16,2176]{2,1,0:T(8,128)(2,1)S(1)} %pad_maximum_fusion.5), channel_id=1, source_target_pairs={{0,2},{1,3},{2,0},{3,1},{4,6},{5,7},{6,4},{7,5},{8,10},{9,11},{10,... | collective-permute-start | bytes 835592 | tf_op jit(solution)/shard_map/ppermute | solution.py:18
  42.6 7.2 %collective-permute-start.12 = (bf16[4,16,2048]{2,1,0:T(8,128)(2,1)}, bf16[4,16,2048]{2,1,0:T(8,128)(2,1)S(1)}, u32[]{:S(2)}, u32[]{:S(2)}) collective-permute-start(bf16[4,16,2048]{2,1,0:T(8,128)(2,1)} %pad_maximum_fusion.8), channel_id=1, source_target_pairs={{0,1},{1,0},{2,3},{3,2},{4,5},{5,4},{6,7},{7,6},{8,9},{9,8},{10,11... | collective-permute-start | bytes 786440 | tf_op jit(solution)/shard_map/ppermute | solution.py:18
  45.0 12.6 %all-to-all-start = ((bf16[16,8,448]{2,1,0:T(8,128)(2,1)}), bf16[16,8,448]{2,1,0:T(8,128)(2,1)S(1)}, u32[]{:S(2)}, u32[]{:S(2)}) async-start(bf16[16,8,448]{2,1,0:T(8,128)(2,1)} %bitcast.135), calls=%async_computation | async-start | bytes 262144 | tf_op jit(solution)/shard_map/all_to_all | solution.py:537
  59.2 7.0 %collective-permute-start.14 = (bf16[448,128]{1,0:T(8,128)(2,1)S(1)}, bf16[448,128]{1,0:T(8,128)(2,1)S(1)}, u32[]{:S(2)}, u32[]{:S(2)}) collective-permute-start(bf16[448,128]{1,0:T(8,128)(2,1)S(1)} %fusion.15), channel_id=1, source_target_pairs={{0,4},{1,5},{2,6},{3,7},{4,0},{5,1},{6,2},{7,3},{8,12},{9,13},{10,... | collective-permute-start | bytes 344072 | tf_op jit(solution)/shard_map/ppermute | solution.py:18
  60.9 11.8 %collective-permute-start.15 = (bf16[448,128]{1,0:T(8,128)(2,1)S(1)}, bf16[448,128]{1,0:T(8,128)(2,1)S(1)}, u32[]{:S(2)}, u32[]{:S(2)}) collective-permute-start(bf16[448,128]{1,0:T(8,128)(2,1)S(1)} %fusion.15), channel_id=1, source_target_pairs={{0,8},{1,9},{2,10},{3,11},{4,12},{5,13},{6,14},{7,15},{8,0},{9,1},... | collective-permute-start | bytes 344072 | tf_op jit(solution)/shard_map/ppermute | solution.py:18
  62.5 10.3 %collective-permute-start.16 = (bf16[448,128]{1,0:T(8,128)(2,1)S(1)}, bf16[448,128]{1,0:T(8,128)(2,1)S(1)}, u32[]{:S(2)}, u32[]{:S(2)}) collective-permute-start(bf16[448,128]{1,0:T(8,128)(2,1)S(1)} %fusion.15), channel_id=1, source_target_pairs={{0,12},{1,13},{2,14},{3,15},{4,8},{5,9},{6,10},{7,11},{8,4},{9,5},... | collective-permute-start | bytes 344072 | tf_op jit(solution)/shard_map/ppermute | solution.py:18
  76.0 7.8 %collective-permute-start.24 = (bf16[4,224,128]{2,1,0:T(8,128)(2,1)S(1)}, bf16[4,224,128]{2,1,0:T(8,128)(2,1)S(1)}, u32[]{:S(2)}, u32[]{:S(2)}) collective-permute-start(bf16[4,224,128]{2,1,0:T(8,128)(2,1)S(1)} %get-tuple-element.89.refs_0_), channel_id=1, source_target_pairs={{0,16},{16,0},{1,17},{17,1},{2,18},{18,2},{3,19},{19,3},{4,20},{20... | collective-permute-start | bytes 688136 | tf_op jit(solution)/shard_map/ppermute | solution.py:18
  80.7 11.0 %collective-permute-start.21 = (bf16[8,224,128]{2,1,0:T(8,128)(2,1)S(1)}, bf16[8,224,128]{2,1,0:T(8,128)(2,1)S(1)}, u32[]{:S(2)}, u32[]{:S(2)}) collective-permute-start(bf16[8,224,128]{2,1,0:T(8,128)(2,1)S(1)} %pad_maximum_fusion.3), channel_id=1, source_target_pairs={{0,1},{1,0},{2,3},{3,2},{4,5},{5,4},{6,7},{7,6},{8,9},{9,8},{10,11... | collective-permute-start | bytes 1376264 | tf_op jit(solution)/shard_map/ppermute | solution.py:18
  81.1 10.6 %collective-permute-start.20 = (bf16[8,224,128]{2,1,0:T(8,128)(2,1)S(1)}, bf16[8,224,128]{2,1,0:T(8,128)(2,1)S(1)}, u32[]{:S(2)}, u32[]{:S(2)}) collective-permute-start(bf16[8,224,128]{2,1,0:T(8,128)(2,1)S(1)} %pad_maximum_fusion.2), channel_id=1, source_target_pairs={{0,2},{1,3},{2,0},{3,1},{4,6},{5,7},{6,4},{7,5},{8,10},{9,11},{10,... | collective-permute-start | bytes 1376264 | tf_op jit(solution)/shard_map/ppermute | solution.py:18
  106.0 12.9 %collective-permute-start.34 = (bf16[64,3584]{1,0:T(8,128)(2,1)}, bf16[64,3584]{1,0:T(8,128)(2,1)}, u32[]{:S(2)}, u32[]{:S(2)}) collective-permute-start(bf16[64,3584]{1,0:T(8,128)(2,1)} %add_convert_fusion.1), channel_id=1, source_target_pairs={{0,2},{1,3},{2,0},{3,1},{4,6},{5,7},{6,4},{7,5},{8,10},{9,11},{10,... | collective-permute-start | bytes 1376264 | tf_op jit(solution)/shard_map/ppermute | solution.py:18
  107.3 14.6 %collective-permute-start.31 = (bf16[64,3584]{1,0:T(8,128)(2,1)}, bf16[64,3584]{1,0:T(8,128)(2,1)}, u32[]{:S(2)}, u32[]{:S(2)}) collective-permute-start(bf16[64,3584]{1,0:T(8,128)(2,1)} %add_convert_fusion.2), channel_id=1, source_target_pairs={{0,1},{1,0},{2,3},{3,2},{4,5},{5,4},{6,7},{7,6},{8,9},{9,8},{10,11... | collective-permute-start | bytes 1376264 | tf_op jit(solution)/shard_map/ppermute | solution.py:18
  112.7 9.2 %collective-permute-start.30 = (bf16[64,3584]{1,0:T(8,128)(2,1)S(1)}, bf16[64,3584]{1,0:T(8,128)(2,1)}, u32[]{:S(2)}, u32[]{:S(2)}) collective-permute-start(bf16[64,3584]{1,0:T(8,128)(2,1)S(1)} %get-tuple-element.98), channel_id=1, source_target_pairs={{0,16},{16,0},{1,17},{17,1},{2,18},{18,2},{3,19},{19,3},{4,20},{20... | collective-permute-start | bytes 1376264 | tf_op jit(solution)/shard_map/ppermute | solution.py:18
  120.2 6.9 %collective-permute-start.35 = (bf16[32,3584]{1,0:T(8,128)(2,1)S(1)}, bf16[32,3584]{1,0:T(8,128)(2,1)S(1)}, u32[]{:S(2)}, u32[]{:S(2)}) collective-permute-start(bf16[32,3584]{1,0:T(8,128)(2,1)S(1)} %slice.196), channel_id=1, source_target_pairs={{0,1},{1,0},{2,3},{3,2},{4,5},{5,4},{6,7},{7,6},{8,9},{9,8},{10,11... | collective-permute-start | bytes 688136 | tf_op jit(solution)/shard_map/ppermute | solution.py:18
  132.1 10.0 %collective-permute-start.37 = (bf16[8,7168]{1,0:T(8,128)(2,1)S(1)}, bf16[8,7168]{1,0:T(8,128)(2,1)S(1)}, u32[]{:S(2)}, u32[]{:S(2)}) collective-permute-start(bf16[8,7168]{1,0:T(8,128)(2,1)S(1)} %get-tuple-element.107), channel_id=1, source_target_pairs={{0,8},{1,9},{2,10},{3,11},{4,12},{5,13},{6,14},{7,15},{8,0},{9,1},... | collective-permute-start | bytes 344072 | tf_op jit(solution)/shard_map/ppermute | solution.py:18
  133.5 8.7 %collective-permute-start.38 = (bf16[8,7168]{1,0:T(8,128)(2,1)S(1)}, bf16[8,7168]{1,0:T(8,128)(2,1)S(1)}, u32[]{:S(2)}, u32[]{:S(2)}) collective-permute-start(bf16[8,7168]{1,0:T(8,128)(2,1)S(1)} %get-tuple-element.106), channel_id=1, source_target_pairs={{0,12},{1,13},{2,14},{3,15},{4,8},{5,9},{6,10},{7,11},{8,4},{9,5},... | collective-permute-start | bytes 344072 | tf_op jit(solution)/shard_map/ppermute | solution.py:18
  (28 other events, 141.2 us)
